TPU v7x, 32 devices: a whole 2x2x4 slice. The times are simulated.
32 devices in a mesh: parts: 2 (over y), sensor: 4 (over z), tm: 2 (over x), lag: 2 (over core).
Axes of the slice: x: 2, y: 2, z: 4, core: 2. Of those that a mesh axis runs over, the one named last changes fastest.
Arguments:
- readings: bfloat16 [128, 128, 1024], P(('parts', 'sensor'), None, 'tm'), parts along dimension 0, may hold values from -6 to 6
- present: int32 [128, 1024], P(('parts', 'sensor'), 'tm'), parts along dimension 0, may hold values from 0 to 1, as said below
- pair_first: int32 [64], P(('parts', 'sensor')), parts along dimension 0, may hold values from 0 to 63, as said below
- pair_second: int32 [64], P(('parts', 'sensor')), parts along dimension 0, may hold values from 0 to 63, as said below
Outputs:
- pair_cov: bfloat16 [64, 25, 128, 128], P(('parts', 'sensor'), None, ('tm', 'lag')), parts along dimension 0
- strength: float32 [25, 128, 128], P(None, ('parts', 'sensor')), parts along dimension 1
There are 2 independent parts, one for each index of `parts`. A program takes and returns all parts, laid end to end along the dimension named above; each array names one. Nothing has to cross between parts.
Inputs may be any that keep to these rules, and one draw needn't show every extreme that they name: Each block misses one run of consecutive steps (possibly empty) shorter than 512; all its other steps are present. `pair_first`: blocks are laid 16 to an index of sensor in order; the 8 pairs held by an index of sensor have their first block on that index. `pair_second`: A pair's second block lies on an index of sensor at most 3 away from the first's; of the pairs held by one index, at most 2 have their second block on any one index, and some index reaches 2 in every draw.
All inputs are finite; a program needn't handle non-finite values.
Results may differ from a plain program's by a relative error of at most 0.0085.
Values may be sent and summed in bfloat16 or wider, within the bound.
No kernel may reach another device: no remote copies, remote signals or barrier semaphores. Data moves between devices by JAX's collectives and lax.ppermute only.
A program may use at most 64 MiB of HBM per device.

v0:
```python
import jax
import jax.numpy as jnp
from jax import lax
from jax.sharding import PartitionSpec as P

LAGS = 25
REACH = 3
CAP = 2


def passed_along(block, axis, distance):
    devices = range(lax.axis_size(axis))
    route = [(i - distance, i) for i in devices if i - distance in devices]
    return lax.ppermute(block, axis, route)


def local(readings, present, pair_first, pair_second):
    blk_dev, block_size, steps_here = readings.shape
    pair_count = pair_first.shape[0]
    tm_count = lax.axis_size("tm")
    lag_count = lax.axis_size("lag")
    home_index = lax.axis_index("sensor")
    tm_place = lax.axis_index("tm")
    lag_place = lax.axis_index("lag")
    highest = lax.Precision.HIGHEST
    observed = present.astype(jnp.float32)
    values = readings.astype(jnp.float32)
    totals = jnp.sum(values * observed[:, None, :], axis=2)
    counts = jnp.sum(observed, axis=1)
    totals, counts = lax.psum((totals, counts), "tm")
    average = totals / counts[:, None]
    centered = ((values - average[:, :, None]) * observed[:, None, :]).astype(jnp.bfloat16)
    local_first = pair_first - home_index * blk_dev
    owner_index = pair_second // blk_dev
    partner_local = pair_second - owner_index * blk_dev
    positions = jnp.arange(pair_count)
    earlier = (owner_index[:, None] == owner_index[None, :]) & (
        positions[None, :] < positions[:, None]
    )
    slot_rank = jnp.sum(earlier.astype(jnp.int32), axis=1)
    slot_index = (owner_index - home_index + REACH) * CAP + slot_rank
    groups = 2 * REACH + 1
    slot_count = groups * CAP
    slot_hot = slot_index[:, None] == jnp.arange(slot_count)[None, :]
    requests = jnp.sum(jnp.where(slot_hot, partner_local[:, None], 0), axis=0).reshape(groups, CAP)
    slot_float = slot_hot.astype(jnp.float32)
    asked_list = []
    block_list = []
    for group_step in range(groups):
        shift_by = group_step - REACH
        if shift_by == 0:
            requested = requests[group_step]
            block_list.append(centered[requested])
        else:
            requested = passed_along(requests[group_step], "sensor", shift_by)
            block_list.append(passed_along(centered[requested], "sensor", -shift_by))
        asked_list.append(requested)
    fetched = jnp.concatenate(block_list, axis=0)
    served = jnp.concatenate(asked_list, axis=0)
    partner = fetched[slot_index]
    per_row = block_size // (tm_count * lag_count)
    row_offset = (tm_place * lag_count + lag_place) * per_row
    first_rows = jnp.take(centered, local_first, axis=0)
    time_edge = passed_along(partner[:, :, : LAGS - 1], "tm", -1)
    extended = jnp.concatenate([partner, time_edge], axis=2)
    own_rows = first_rows.reshape(pair_count, tm_count, lag_count, per_row, steps_here)
    own_rows = lax.dynamic_index_in_dim(own_rows, lag_place, 2, False).reshape(
        pair_count, tm_count * per_row, steps_here
    )
    lagged = [
        jnp.einsum(
            "pat,pbt->apb",
            own_rows,
            extended[:, :, lag_step : lag_step + steps_here],
            preferred_element_type=jnp.float32,
        )
        for lag_step in range(LAGS)
    ]
    summed = lax.psum_scatter(
        jnp.stack(lagged, axis=2).astype(jnp.bfloat16), "tm", scatter_dimension=0, tiled=True
    ).astype(jnp.float32)
    lag_values = jnp.arange(LAGS, dtype=jnp.float32)
    scales = 1.0 / jnp.sqrt(steps_here * tm_count - lag_values)
    standard = summed * scales[None, None, :, None]
    pair_cov = jnp.transpose(standard, (1, 2, 0, 3)).astype(jnp.bfloat16)
    squares = standard * standard
    row_part = jnp.sum(squares, axis=3) / block_size
    col_part = jnp.sum(squares, axis=0) / block_size
    first_hot = (local_first[:, None] == jnp.arange(blk_dev)[None, :]).astype(jnp.float32)
    row_blocks = jnp.einsum("rpl,pk->lkr", row_part, first_hot, precision=highest)
    partial_value = lax.dynamic_update_slice(
        jnp.zeros((LAGS, blk_dev, block_size), jnp.float32), row_blocks, (0, 0, row_offset)
    )
    outgoing_sums = jnp.einsum("ps,plb->slb", slot_float, col_part, precision=highest)
    back_list = []
    for group_step in range(groups):
        shift_by = group_step - REACH
        portion = outgoing_sums[group_step * CAP : (group_step + 1) * CAP]
        if shift_by == 0:
            back_list.append(portion)
        else:
            back_list.append(passed_along(portion, "sensor", shift_by))
    returned = jnp.concatenate(back_list, axis=0)
    served_hot = (served[:, None] == jnp.arange(blk_dev)[None, :]).astype(jnp.float32)
    partial_value = partial_value + jnp.einsum(
        "nk,nlb->lkb", served_hot, returned, precision=highest
    )
    strength = lax.psum(partial_value.astype(jnp.bfloat16), ("tm", "lag")).astype(jnp.float32)
    return (pair_cov, strength)


def solution(mesh):
    in_specs = (
        P(("parts", "sensor"), None, "tm"),
        P(("parts", "sensor"), "tm"),
        P(("parts", "sensor")),
        P(("parts", "sensor")),
    )
    out_specs = (
        P(("parts", "sensor"), None, ("tm", "lag"), None),
        P(None, ("parts", "sensor"), None),
    )
    return jax.shard_map(local, mesh=mesh, in_specs=in_specs, out_specs=out_specs, check_vma=False)
```

profile of v0, /device:TPU:0, one launch (start us, length us, event | category | flops | bytes accessed | tf_op | source)
XLA Modules:
  0.0 226.5 jit_solution(1018439716209790307)
XLA Ops:
  8.2 6.9 %collective-permute-start.10 = (s32[2]{0:T(128)S(1)}, s32[2]{0:T(128)S(1)}, u32[]{:S(2)}, u32[]{:S(2)}) collective-permute-start(s32[2]{0:T(128)S(1)} %get-tuple-element.26), channel_id=1, source_target_pairs={{0,12},{1,13},{2,14},{3,15},{16,28},{17,29},{18,30},{19,31}} | collective-permute-start | bytes 32 | tf_op jit(solution)/shard_map/ppermute | solution.py:14
  15.2 1.3 collective-permute-start.8
  16.5 2.5 %collective-permute-start.6 = (s32[2]{0:T(128)S(1)}, s32[2]{0:T(128)S(1)}, u32[]{:S(2)}, u32[]{:S(2)}) collective-permute-start(s32[2]{0:T(128)S(1)} %get-tuple-element.28), channel_id=1, source_target_pairs={{0,4},{4,8},{8,12},{1,5},{5,9},{9,13},{2,6},{6,10},{10,14},{3,7},{... | collective-permute-start | bytes 32 | tf_op jit(solution)/shard_map/ppermute | solution.py:14
  19.0 1.3 collective-permute-start.4
  20.3 1.3 collective-permute-start.2
  23.9 2.1 fusion
  26.0 5.1 %all-reduce = (f32[16,128]{1,0:T(8,128)S(1)}, f32[16]{0:T(128)S(1)}) all-reduce(f32[16,128]{1,0:T(8,128)S(1)} %fusion, f32[16]{0:T(128)S(1)} %convert_reduce_fusion.1), channel_id=1, replica_groups=mesh['parts'=2,'sensor'=4,'tm'=2,'lag'=2] {'tm'}, use_global_device_ids=true, to_apply=%region_1.0 | all-reduce | flops 2064 | bytes 16512 | tf_op jit(solution)/shard_map/psum | solution.py:30
  31.1 2.2 fusion.2
  35.5 1.3 collective-permute-start
  36.9 7.0 %collective-permute-done = s32[2]{0:T(128)S(1)} collective-permute-done((s32[2]{0:T(128)S(1)}, s32[2]{0:T(128)S(1)}, u32[]{:S(2)}, u32[]{:S(2)}) %collective-permute-start) | collective-permute-done | bytes 40 | tf_op jit(solution)/shard_map/ppermute | solution.py:14
  45.1 2.4 %collective-permute-start.1 = (bf16[2,128,512]{2,1,0:T(8,128)(2,1)S(1)}, bf16[2,128,512]{2,1,0:T(8,128)(2,1)}, u32[]{:S(2)}, u32[]{:S(2)}) collective-permute-start(bf16[2,128,512]{2,1,0:T(8,128)(2,1)S(1)} %gather_fusion), channel_id=1, source_target_pairs={{0,12},{1,13},{2,14},{3,15},{16,28},{17,29},{18,30},{19,31}} | collective-permute-start | bytes 786440 | tf_op jit(solution)/shard_map/ppermute | solution.py:14
  47.5 2.0 collective-permute-start.3
  49.5 1.3 gather_fusion.2
  50.8 2.5 %collective-permute-start.5 = (bf16[2,128,512]{2,1,0:T(8,128)(2,1)}, bf16[2,128,512]{2,1,0:T(8,128)(2,1)}, u32[]{:S(2)}, u32[]{:S(2)}) collective-permute-start(bf16[2,128,512]{2,1,0:T(8,128)(2,1)} %gather_fusion.2), channel_id=1, source_target_pairs={{0,4},{4,8},{8,12},{1,5},{5,9},{9,13},{2,6},{6,10},{10,14},{3,7},{... | collective-permute-start | bytes 786440 | tf_op jit(solution)/shard_map/ppermute | solution.py:14
  54.4 1.3 gather_fusion.4
  55.7 1.3 collective-permute-start.7
  57.0 1.3 collective-permute-start.9
  58.3 1.3 collective-permute-start.11
  59.6 1.7 constant_dynamic-update-slice_fusion.6
  61.2 1.7 constant_dynamic-update-slice_fusion.5
  62.9 1.7 constant_dynamic-update-slice_fusion.4
  66.0 12.5 %collective-permute-done.9 = bf16[2,128,512]{2,1,0:T(8,128)(2,1)S(1)} collective-permute-done((bf16[2,128,512]{2,1,0:T(8,128)(2,1)S(1)}, bf16[2,128,512]{2,1,0:T(8,128)(2,1)S(1)}, u32[]{:S(2)}, u32[]{:S(2)}) %collective-permute-start.9) | collective-permute-done | bytes 262176 | tf_op jit(solution)/shard_map/ppermute | solution.py:14
  79.9 2.1 gather_fusion.7
  82.1 1.5 collective-permute-start.12
  83.6 1.1 fusion.9
  84.8 5.6 %collective-permute-done.12 = bf16[8,128,24]{2,1,0:T(8,128)(2,1)S(1)} collective-permute-done((bf16[8,128,24]{2,1,0:T(8,128)(2,1)S(1)}, bf16[8,128,24]{2,1,0:T(8,128)(2,1)S(1)}, u32[]{:S(2)}, u32[]{:S(2)}) %collective-permute-start.12) | collective-permute-done | bytes 49184 | tf_op jit(solution)/shard_map/ppermute | solution.py:14
  90.4 1.3 fusion.11
  91.7 1.2 fusion.13
  92.9 1.2 fusion.15
  94.2 1.2 fusion.17
  95.4 1.2 fusion.19
  96.7 1.3 fusion.21
  97.9 1.2 fusion.23
  99.2 1.3 fusion.25
  100.4 1.3 fusion.27
  101.7 1.2 fusion.29
  102.9 1.2 fusion.31
  104.2 1.3 fusion.33
  105.4 1.2 fusion.35
  106.7 1.2 fusion.37
  107.9 1.3 fusion.39
  109.2 1.3 fusion.41
  110.4 1.3 fusion.43
  111.7 1.3 fusion.45
  112.9 1.2 fusion.47
  114.2 1.3 fusion.49
  115.4 1.3 fusion.51
  116.7 1.3 fusion.53
  117.9 1.2 fusion.55
  119.2 1.2 fusion.57
  120.7 41.9 %reduce-scatter.2.cloned.1.call-done = bf16[32,8,25,128]{3,0,1,2:T(8,128)(2,1)} async-done(((bf16[64,8,25,128]{3,0,1,2:T(8,128)(2,1)}), bf16[32,8,25,128]{3,0,1,2:T(8,128)(2,1)}) %reduce-scatter.2.cloned.1.call-update) | async-done | bytes 1638416 | tf_op jit(solution)/shard_map/reduce_scatter | solution.py:79
  162.7 2.5 %fusion.5 = (f32[32,8,25]{0,1,2:T(8,128)S(1)}, f32[8,25,128]{2,0,1:T(8,128)S(1)}, bf16[8,25,32,128]{3,2,0,1:T(8,128)(2,1)S(1)}) fusion(bf16[32,8,25,128]{3,0,1,2:T(8,128)(2,1)} %reduce-scatter.2.cloned.1.call-done, f32[25]{0:T(128)S(1)} %subtract_rsqrt_fusion), kind=kLoop, calls=%fused_computation.17 | loop fusion | flops 4883200 | bytes 3404900 | tf_op jit(solution)/shard_map/reduce_sum | solution.py:87
  165.6 5.2 %collective-permute-start.18 = (f32[2,25,128]{2,0,1:T(2,128)S(1)}, f32[2,25,128]{2,0,1:T(2,128)S(1)}, u32[]{:S(2)}, u32[]{:S(2)}) collective-permute-start(f32[2,25,128]{2,0,1:T(2,128)S(1)} %get-tuple-element.17), channel_id=1, source_target_pairs={{0,12},{1,13},{2,14},{3,15},{16,28},{17,29},{18,30},{19,31}} | collective-permute-start | bytes 76808 | tf_op jit(solution)/shard_map/ppermute | solution.py:14
  170.8 1.3 collective-permute-start.17
  172.1 2.5 %collective-permute-start.16 = (f32[2,25,128]{2,0,1:T(2,128)S(1)}, f32[2,25,128]{2,0,1:T(2,128)S(1)}, u32[]{:S(2)}, u32[]{:S(2)}) collective-permute-start(f32[2,25,128]{2,0,1:T(2,128)S(1)} %get-tuple-element.19), channel_id=1, source_target_pairs={{0,4},{4,8},{8,12},{1,5},{5,9},{9,13},{2,6},{6,10},{10,14},{3,7},{... | collective-permute-start | bytes 76808 | tf_op jit(solution)/shard_map/ppermute | solution.py:14
  174.6 1.3 collective-permute-start.15
  175.9 1.3 collective-permute-start.14
  177.2 1.3 collective-permute-start.13
  178.6 1.7 collective-permute-done.15
  180.3 2.5 %collective-permute-done.14 = f32[2,25,128]{2,0,1:T(2,128)S(1)} collective-permute-done((f32[2,25,128]{2,0,1:T(2,128)S(1)}, f32[2,25,128]{2,0,1:T(2,128)S(1)}, u32[]{:S(2)}, u32[]{:S(2)}) %collective-permute-start.14) | collective-permute-done | bytes 25632 | tf_op jit(solution)/shard_map/ppermute | solution.py:14
  182.8 3.1 %collective-permute-done.13 = f32[2,25,128]{2,0,1:T(2,128)S(1)} collective-permute-done((f32[2,25,128]{2,0,1:T(2,128)S(1)}, f32[2,25,128]{2,0,1:T(2,128)S(1)}, u32[]{:S(2)}, u32[]{:S(2)}) %collective-permute-start.13) | collective-permute-done | bytes 25632 | tf_op jit(solution)/shard_map/ppermute | solution.py:14
  187.9 1.4 copy.9
  189.3 28.7 %all-reduce.3.cloned.1.call-done = bf16[25,16,128]{2,1,0:T(8,128)(2,1)} async-done(((bf16[25,16,128]{2,1,0:T(8,128)(2,1)}), bf16[25,16,128]{2,1,0:T(8,128)(2,1)}) %all-reduce.3.cloned.1.call-update) | async-done | bytes 102416 | tf_op jit(solution)/shard_map/psum | solution.py:108
  218.0 1.6 convert_element_type.39
  (64 shorter events, 13.7 us)
Async XLA Ops:
  7.2 155.5 %reduce-scatter.2.cloned.1.call-start = ((), (), s32[]{:S(2)}) async-start(), calls=%async_computation.1 | async-start | bytes 4915200 | tf_op jit(solution)/shard_map/reduce_scatter | solution.py:79
  8.2 27.3 %collective-permute-start.10 = (s32[2]{0:T(128)S(1)}, s32[2]{0:T(128)S(1)}, u32[]{:S(2)}, u32[]{:S(2)}) collective-permute-start(s32[2]{0:T(128)S(1)} %get-tuple-element.26), channel_id=1, source_target_pairs={{0,12},{1,13},{2,14},{3,15},{16,28},{17,29},{18,30},{19,31}} | collective-permute-start | bytes 32 | tf_op jit(solution)/shard_map/ppermute | solution.py:14
  15.2 21.6 %collective-permute-start.8 = (s32[2]{0:T(128)S(1)}, s32[2]{0:T(128)S(1)}, u32[]{:S(2)}, u32[]{:S(2)}) collective-permute-start(s32[2]{0:T(128)S(1)} %get-tuple-element.27), channel_id=1, source_target_pairs={{0,8},{4,12},{1,9},{5,13},{2,10},{6,14},{3,11},{7,15},{16,24},{20,... | collective-permute-start | bytes 32 | tf_op jit(solution)/shard_map/ppermute | solution.py:14
  16.5 33.0 %collective-permute-start.6 = (s32[2]{0:T(128)S(1)}, s32[2]{0:T(128)S(1)}, u32[]{:S(2)}, u32[]{:S(2)}) collective-permute-start(s32[2]{0:T(128)S(1)} %get-tuple-element.28), channel_id=1, source_target_pairs={{0,4},{4,8},{8,12},{1,5},{5,9},{9,13},{2,6},{6,10},{10,14},{3,7},{... | collective-permute-start | bytes 32 | tf_op jit(solution)/shard_map/ppermute | solution.py:14
  19.0 30.6 %collective-permute-start.4 = (s32[2]{0:T(128)S(1)}, s32[2]{0:T(128)S(1)}, u32[]{:S(2)}, u32[]{:S(2)}) collective-permute-start(s32[2]{0:T(128)S(1)} %get-tuple-element.29), channel_id=1, source_target_pairs={{4,0},{8,4},{12,8},{5,1},{9,5},{13,9},{6,2},{10,6},{14,10},{7,3},{... | collective-permute-start | bytes 32 | tf_op jit(solution)/shard_map/ppermute | solution.py:14
  20.3 16.6 %collective-permute-start.2 = (s32[2]{0:T(128)S(1)}, s32[2]{0:T(128)S(1)}, u32[]{:S(2)}, u32[]{:S(2)}) collective-permute-start(s32[2]{0:T(128)S(1)} %get-tuple-element.30), channel_id=1, source_target_pairs={{8,0},{12,4},{9,1},{13,5},{10,2},{14,6},{11,3},{15,7},{24,16},{28,... | collective-permute-start | bytes 32 | tf_op jit(solution)/shard_map/ppermute | solution.py:14
  35.5 8.4 %collective-permute-start = (s32[2]{0:T(128)S(1)}, s32[2]{0:T(128)S(1)}, u32[]{:S(2)}, u32[]{:S(2)}) collective-permute-start(s32[2]{0:T(128)S(1)} %get-tuple-element.31), channel_id=1, source_target_pairs={{12,0},{13,1},{14,2},{15,3},{28,16},{29,17},{30,18},{31,19}} | collective-permute-start | bytes 32 | tf_op jit(solution)/shard_map/ppermute | solution.py:14
  45.1 13.2 %collective-permute-start.1 = (bf16[2,128,512]{2,1,0:T(8,128)(2,1)S(1)}, bf16[2,128,512]{2,1,0:T(8,128)(2,1)}, u32[]{:S(2)}, u32[]{:S(2)}) collective-permute-start(bf16[2,128,512]{2,1,0:T(8,128)(2,1)S(1)} %gather_fusion), channel_id=1, source_target_pairs={{0,12},{1,13},{2,14},{3,15},{16,28},{17,29},{18,30},{19,31}} | collective-permute-start | bytes 786440 | tf_op jit(solution)/shard_map/ppermute | solution.py:14
  47.5 13.7 %collective-permute-start.3 = (bf16[2,128,512]{2,1,0:T(8,128)(2,1)S(1)}, bf16[2,128,512]{2,1,0:T(8,128)(2,1)}, u32[]{:S(2)}, u32[]{:S(2)}) collective-permute-start(bf16[2,128,512]{2,1,0:T(8,128)(2,1)S(1)} %gather_fusion.1), channel_id=1, source_target_pairs={{0,8},{4,12},{1,9},{5,13},{2,10},{6,14},{3,11},{7,15},{16,24},{20,... | collective-permute-start | bytes 786440 | tf_op jit(solution)/shard_map/ppermute | solution.py:14
  50.8 12.1 %collective-permute-start.5 = (bf16[2,128,512]{2,1,0:T(8,128)(2,1)}, bf16[2,128,512]{2,1,0:T(8,128)(2,1)}, u32[]{:S(2)}, u32[]{:S(2)}) collective-permute-start(bf16[2,128,512]{2,1,0:T(8,128)(2,1)} %gather_fusion.2), channel_id=1, source_target_pairs={{0,4},{4,8},{8,12},{1,5},{5,9},{9,13},{2,6},{6,10},{10,14},{3,7},{... | collective-permute-start | bytes 786440 | tf_op jit(solution)/shard_map/ppermute | solution.py:14
  55.7 9.6 %collective-permute-start.7 = (bf16[2,128,512]{2,1,0:T(8,128)(2,1)}, bf16[2,128,512]{2,1,0:T(8,128)(2,1)S(1)}, u32[]{:S(2)}, u32[]{:S(2)}) collective-permute-start(bf16[2,128,512]{2,1,0:T(8,128)(2,1)} %gather_fusion.4), channel_id=1, source_target_pairs={{4,0},{8,4},{12,8},{5,1},{9,5},{13,9},{6,2},{10,6},{14,10},{7,3},{... | collective-permute-start | bytes 786440 | tf_op jit(solution)/shard_map/ppermute | solution.py:14
  57.0 21.5 %collective-permute-start.9 = (bf16[2,128,512]{2,1,0:T(8,128)(2,1)S(1)}, bf16[2,128,512]{2,1,0:T(8,128)(2,1)S(1)}, u32[]{:S(2)}, u32[]{:S(2)}) collective-permute-start(bf16[2,128,512]{2,1,0:T(8,128)(2,1)S(1)} %gather_fusion.5), channel_id=1, source_target_pairs={{8,0},{12,4},{9,1},{13,5},{10,2},{14,6},{11,3},{15,7},{24,16},{28,... | collective-permute-start | bytes 786440 | tf_op jit(solution)/shard_map/ppermute | solution.py:14
  58.3 20.9 %collective-permute-start.11 = (bf16[2,128,512]{2,1,0:T(8,128)(2,1)S(1)}, bf16[2,128,512]{2,1,0:T(8,128)(2,1)S(1)}, u32[]{:S(2)}, u32[]{:S(2)}) collective-permute-start(bf16[2,128,512]{2,1,0:T(8,128)(2,1)S(1)} %gather_fusion.6), channel_id=1, source_target_pairs={{12,0},{13,1},{14,2},{15,3},{28,16},{29,17},{30,18},{31,19}} | collective-permute-start | bytes 786440 | tf_op jit(solution)/shard_map/ppermute | solution.py:14
  65.3 18.3 %copy-start = (bf16[8,2,1,32,512]{4,3,1,0,2:T(8,128)(2,1)S(1)}, bf16[8,2,1,32,512]{4,3,1,0,2:T(8,128)(2,1)}, u32[]{:S(2)}) copy-start(bf16[8,2,1,32,512]{4,3,1,0,2:T(8,128)(2,1)} %copy_select_fusion) | copy-start | bytes 1572868
  82.1 8.3 %collective-permute-start.12 = (bf16[8,128,24]{2,1,0:T(8,128)(2,1)S(1)}, bf16[8,128,24]{2,1,0:T(8,128)(2,1)S(1)}, u32[]{:S(2)}, u32[]{:S(2)}) collective-permute-start(bf16[8,128,24]{2,1,0:T(8,128)(2,1)S(1)} %slice.181), channel_id=1, source_target_pairs={{2,0},{3,1},{6,4},{7,5},{10,8},{11,9},{14,12},{15,13},{18,16},{19,... | collective-permute-start | bytes 147464 | tf_op jit(solution)/shard_map/ppermute | solution.py:14
  120.5 97.6 %all-reduce.3.cloned.1.call-start = ((), (), s32[]{:S(2)}) async-start(), calls=%async_computation.2 | async-start | bytes 204800 | tf_op jit(solution)/shard_map/psum | solution.py:108
  165.6 11.6 %collective-permute-start.18 = (f32[2,25,128]{2,0,1:T(2,128)S(1)}, f32[2,25,128]{2,0,1:T(2,128)S(1)}, u32[]{:S(2)}, u32[]{:S(2)}) collective-permute-start(f32[2,25,128]{2,0,1:T(2,128)S(1)} %get-tuple-element.17), channel_id=1, source_target_pairs={{0,12},{1,13},{2,14},{3,15},{16,28},{17,29},{18,30},{19,31}} | collective-permute-start | bytes 76808 | tf_op jit(solution)/shard_map/ppermute | solution.py:14
  170.8 7.8 %collective-permute-start.17 = (f32[2,25,128]{2,0,1:T(2,128)S(1)}, f32[2,25,128]{2,0,1:T(2,128)S(1)}, u32[]{:S(2)}, u32[]{:S(2)}) collective-permute-start(f32[2,25,128]{2,0,1:T(2,128)S(1)} %get-tuple-element.18), channel_id=1, source_target_pairs={{0,8},{4,12},{1,9},{5,13},{2,10},{6,14},{3,11},{7,15},{16,24},{20,... | collective-permute-start | bytes 76808 | tf_op jit(solution)/shard_map/ppermute | solution.py:14
  172.1 6.5 %collective-permute-start.16 = (f32[2,25,128]{2,0,1:T(2,128)S(1)}, f32[2,25,128]{2,0,1:T(2,128)S(1)}, u32[]{:S(2)}, u32[]{:S(2)}) collective-permute-start(f32[2,25,128]{2,0,1:T(2,128)S(1)} %get-tuple-element.19), channel_id=1, source_target_pairs={{0,4},{4,8},{8,12},{1,5},{5,9},{9,13},{2,6},{6,10},{10,14},{3,7},{... | collective-permute-start | bytes 76808 | tf_op jit(solution)/shard_map/ppermute | solution.py:14
  174.6 5.7 %collective-permute-start.15 = (f32[2,25,128]{2,0,1:T(2,128)S(1)}, f32[2,25,128]{2,0,1:T(2,128)S(1)}, u32[]{:S(2)}, u32[]{:S(2)}) collective-permute-start(f32[2,25,128]{2,0,1:T(2,128)S(1)} %get-tuple-element.21), channel_id=1, source_target_pairs={{4,0},{8,4},{12,8},{5,1},{9,5},{13,9},{6,2},{10,6},{14,10},{7,3},{... | collective-permute-start | bytes 76808 | tf_op jit(solution)/shard_map/ppermute | solution.py:14
  175.9 6.9 %collective-permute-start.14 = (f32[2,25,128]{2,0,1:T(2,128)S(1)}, f32[2,25,128]{2,0,1:T(2,128)S(1)}, u32[]{:S(2)}, u32[]{:S(2)}) collective-permute-start(f32[2,25,128]{2,0,1:T(2,128)S(1)} %get-tuple-element.22), channel_id=1, source_target_pairs={{8,0},{12,4},{9,1},{13,5},{10,2},{14,6},{11,3},{15,7},{24,16},{28,... | collective-permute-start | bytes 76808 | tf_op jit(solution)/shard_map/ppermute | solution.py:14
  177.2 8.7 %collective-permute-start.13 = (f32[2,25,128]{2,0,1:T(2,128)S(1)}, f32[2,25,128]{2,0,1:T(2,128)S(1)}, u32[]{:S(2)}, u32[]{:S(2)}) collective-permute-start(f32[2,25,128]{2,0,1:T(2,128)S(1)} %get-tuple-element.23), channel_id=1, source_target_pairs={{12,0},{13,1},{14,2},{15,3},{28,16},{29,17},{30,18},{31,19}} | collective-permute-start | bytes 76808 | tf_op jit(solution)/shard_map/ppermute | solution.py:14
Sparse Core Ops, SparseCore 0:
  120.6 42.0 reduce-scatter.1
  188.0 30.0 all-reduce.2
where the time goes:
time: 227 us; the launch traced here: 226 us
  waiting for transfers between devices  103 us (45%)
  starting transfers between devices  39.9 us (18%)
  matrix products  32.1 us (14%)
  local copies, waits for them, and re-layouts  18.3 us (8%)
  between operations  14.5 us (6%)
  other arithmetic  13.5 us (6%)
  blocking collectives  5.07 us (2%)
    reduce_scatter x1, waiting for transfers between devices, local(): lax.psum_scatter(jnp.stack(lagged, axis=2).astype(jnp.bfloat16), 'tm', sc...  41.9 us
    ppermute x19, starting transfers between devices, passed_along(): return lax.ppermute(block, axis, route)  39.6 us
    ppermute x19, waiting for transfers between devices, passed_along(): return lax.ppermute(block, axis, route)  32.4 us
    dot_general x25, matrix products, local(): jnp.einsum('pat,pbt->apb', own_rows, extended[:, :, lag_step:lag_step + s...  31.1 us
    psum x1, waiting for transfers between devices, local(): lax.psum(partial_value.astype(jnp.bfloat16), ('tm', 'lag'))  28.7 us
    unnamed x10, local copies, waits for them, and re-layouts  8.68 us
    psum x1, blocking collectives, local(): totals, counts = lax.psum((totals, counts), 'tm')  5.07 us
    gather x6, local copies, waits for them, and re-layouts, local(): block_list.append(passed_along(centered[requested], 'sensor', -shift_by))  4.78 us
  transfers between devices with their start and end apart: 21, of which 8 were waited for; matrix products, arithmetic and copies ran while one was open for 10% of the time, Pallas kernels for 0%

commit v1 on v0

v1 whole, which is shorter than its diff:
```python
import jax
import jax.numpy as jnp
import numpy as np
from jax import lax
from jax.experimental import pallas as pl
from jax.experimental.pallas import tpu as pltpu
from jax.sharding import PartitionSpec as P

LAGS = 25
REACH = 3
CAP = 2
PAD = 16
LAG_ROWS = 32
VMEM = pl.BlockSpec(memory_space=pltpu.VMEM)
SMEM = pl.BlockSpec(memory_space=pltpu.SMEM)
ANY = pl.BlockSpec(memory_space=pl.ANY)
PARAMS = pltpu.CompilerParams(vmem_limit_bytes=24 * 1024 * 1024)


def rotated(block, axis, distance):
    size = lax.axis_size(axis)
    return lax.ppermute(block, axis, [(i, (i + distance) % size) for i in range(size)])


def mask_rows(present_ref, index, rows):
    row = present_ref[pl.ds(index, 1), :].astype(jnp.float32)
    return jnp.broadcast_to(row, (rows, row.shape[1]))


def pack_blocks(readings, present, indices):
    _, rows, steps = readings.shape
    count = indices.shape[0]

    def kernel(index_ref, readings_ref, present_ref, *rest):
        outs, sems = rest[:count], rest[count]
        copies = [
            pltpu.make_async_copy(
                readings_ref.at[index_ref[i]], outs[i].at[pl.ds(0, rows)], sems.at[i]
            )
            for i in range(count)
        ]
        for copy in copies:
            copy.start()
        for i in range(count):
            outs[i][rows : rows + PAD, :] = mask_rows(present_ref, index_ref[i], PAD).astype(
                jnp.bfloat16
            )
        for copy in copies:
            copy.wait()

    return pl.pallas_call(
        kernel,
        out_shape=[jax.ShapeDtypeStruct((rows + PAD, steps), jnp.bfloat16)] * count,
        in_specs=[SMEM, ANY, VMEM],
        out_specs=[VMEM] * count,
        scratch_shapes=[pltpu.SemaphoreType.DMA((count,))],
        compiler_params=PARAMS,
    )(indices, readings, present)


def pack_first(readings, present, first_index, row_starts, per_row):
    _, _, steps = readings.shape
    pairs = first_index.shape[0]
    count = row_starts.shape[0]

    def kernel(first_ref, start_ref, readings_ref, present_ref, *rest):
        outs, sems = rest[:count], rest[count]
        copies = []
        for k in range(count):
            start = pl.multiple_of(start_ref[k], per_row)
            for p in range(pairs):
                copies.append(
                    pltpu.make_async_copy(
                        readings_ref.at[first_ref[p], pl.ds(start, per_row)],
                        outs[k].at[pl.ds(p * per_row, per_row)],
                        sems.at[k, p],
                    )
                )
        for copy in copies:
            copy.start()
        rows = lax.broadcasted_iota(jnp.int32, (PAD, steps), 0)
        masks = jnp.zeros((PAD, steps), jnp.float32)
        for p in range(pairs):
            masks = jnp.where(rows == p, mask_rows(present_ref, first_ref[p], PAD), masks)
        for k in range(count):
            outs[k][pairs * per_row : pairs * per_row + PAD, :] = masks.astype(jnp.bfloat16)
        for copy in copies:
            copy.wait()

    return pl.pallas_call(
        kernel,
        out_shape=[jax.ShapeDtypeStruct((pairs * per_row + PAD, steps), jnp.bfloat16)] * count,
        in_specs=[SMEM, SMEM, ANY, VMEM],
        out_specs=[VMEM] * count,
        scratch_shapes=[pltpu.SemaphoreType.DMA((count, pairs))],
        compiler_params=PARAMS,
    )(first_index, row_starts, readings, present)


def centered_windows(raw, masks):
    total = sum(jnp.sum(r * m, axis=1, keepdims=True) for r, m in zip(raw, masks))
    count = sum(jnp.sum(m, axis=1, keepdims=True) for m in masks)
    average = total / count
    return [(r - average) * m for r, m in zip(raw, masks)]


def covariances(pair_of, places, firsts, blocks, carried, pairs, per_row, block_size):
    windows = len(firsts)
    slots = len(blocks)
    steps = firsts[0].shape[1]
    total_steps = windows * steps
    shifts = (LAGS + 1) // 2
    scales = 1.0 / np.sqrt(np.float32(total_steps) - np.arange(LAGS, dtype=np.float32))
    quarter = 128 // per_row
    flat = [block for slot in blocks for block in slot]

    def kernel(pair_ref, place_ref, *rest):
        first_refs = rest[:windows]
        block_refs = rest[windows : windows + slots * windows]
        rest = rest[windows + slots * windows + (carried is not None) :]
        cov_ref, row_ref, col_ref, left, right, squares, ready, first_part, sems = rest

        def one(j):
            pair = pair_ref[j]
            base = pl.multiple_of(pair * per_row, per_row)
            which = lax.broadcasted_iota(jnp.int32, (PAD, steps), 0) == pair
            raw, masks = [], []
            for k in range(windows):
                raw.append(first_refs[k][pl.ds(base, per_row), :].astype(jnp.float32))
                all_masks = first_refs[k][pairs * per_row : pairs * per_row + PAD, :]
                masks.append(
                    jnp.sum(
                        jnp.where(which, all_masks.astype(jnp.float32), 0.0), axis=0, keepdims=True
                    )
                )
            for k, part in enumerate(centered_windows(raw, masks)):
                at = pl.multiple_of(place_ref[k] * steps, steps)
                first_part[:, pl.ds(at, steps)] = part
            raw, masks = [], []
            for k in range(windows):
                ref = block_refs[j * windows + k]
                raw.append(ref[0:block_size, :].astype(jnp.float32))
                masks.append(ref[block_size : block_size + 1, :].astype(jnp.float32))
            for k, part in enumerate(centered_windows(raw, masks)):
                at = pl.multiple_of(place_ref[k] * steps, steps)
                right[0:block_size, pl.ds(at, steps)] = part.astype(jnp.bfloat16)
            whole = right[0:block_size, :].astype(jnp.float32)
            lane = lax.broadcasted_iota(jnp.int32, whole.shape, 1)
            moved = pltpu.roll(whole, total_steps - 1, 1)
            right[block_size : 2 * block_size, :] = jnp.where(
                lane < total_steps - 1, moved, 0.0
            ).astype(jnp.bfloat16)
            whole = first_part[...]
            lane = lax.broadcasted_iota(jnp.int32, whole.shape, 1)
            for m in range(shifts):
                moved = whole if m == 0 else pltpu.roll(whole, 2 * m, 1)
                left[m * per_row : (m + 1) * per_row, :] = jnp.where(
                    lane >= 2 * m, moved, 0.0
                ).astype(jnp.bfloat16)
            product = lax.dot_general(
                left[...], right[...], (((1,), (1,)), ((), ())), preferred_element_type=jnp.float32
            )
            for lag in range(LAGS):
                m, odd = lag // 2, lag % 2
                standard = product[
                    m * per_row : (m + 1) * per_row, odd * block_size : (odd + 1) * block_size
                ] * float(scales[lag])
                ready[j, lag] = standard.astype(jnp.bfloat16)
                square = standard * standard
                col_ref[lag, j : j + 1, :] = (
                    jnp.sum(square, axis=0, keepdims=True) * (1.0 / block_size)
                )
                squares[lag * per_row : (lag + 1) * per_row, :] = square.astype(jnp.bfloat16)
            ones = jnp.full((8, block_size), 1.0 / block_size, jnp.bfloat16)
            sums = lax.dot_general(
                ones, squares[...], (((1,), (1,)), ((), ())), preferred_element_type=jnp.float32
            )
            start = place_ref[windows]
            lane = lax.broadcasted_iota(jnp.int32, (8, 128), 1)
            level = lax.broadcasted_iota(jnp.int32, (8, 128), 0)
            mine = (lane >= start) & (lane < start + per_row)
            tiles = [jnp.zeros((8, 128), jnp.float32) for _ in range(LAG_ROWS // 8)]
            for lag in range(LAGS):
                q, r = lag // quarter, lag % quarter
                piece = sums[:, q * 128 : (q + 1) * 128]
                piece = pltpu.roll(piece, lax.rem(start + 128 - r * per_row, 128), 1)
                tiles[lag // 8] = jnp.where(mine & (level == lag % 8), piece, tiles[lag // 8])
            for i, tile in enumerate(tiles):
                row_ref[j, i * 8 : (i + 1) * 8, :] = tile
            return None

        for j in range(slots):
            used = pair_ref[j] >= 0

            @pl.when(used)
            def _():
                one(j)
                pltpu.make_async_copy(ready.at[j], cov_ref.at[pair_ref[j]], sems.at[j]).start()

            @pl.when(jnp.logical_not(used))
            def _():
                row_ref[j] = jnp.zeros(row_ref.shape[1:], jnp.float32)
                col_ref[:, j : j + 1, :] = jnp.zeros((LAGS, 1, block_size), jnp.float32)

        for j in range(slots):

            @pl.when(pair_ref[j] >= 0)
            def _():
                pltpu.make_async_copy(ready.at[j], cov_ref.at[pair_ref[j]], sems.at[j]).wait()

    operands = [pair_of, places, *firsts, *flat]
    specs = [SMEM, SMEM] + [VMEM] * (len(firsts) + len(flat))
    aliases = {}
    if carried is not None:
        aliases = {len(operands): 0}
        operands.append(carried)
        specs.append(ANY)
    wide = -(-LAGS * per_row // 128) * 128
    return pl.pallas_call(
        kernel,
        out_shape=[
            jax.ShapeDtypeStruct((pairs, LAGS, per_row, block_size), jnp.bfloat16),
            jax.ShapeDtypeStruct((slots, LAG_ROWS, block_size), jnp.float32),
            jax.ShapeDtypeStruct((LAGS, slots, block_size), jnp.float32),
        ],
        in_specs=specs,
        out_specs=[ANY, VMEM, VMEM],
        scratch_shapes=[
            pltpu.VMEM((shifts * per_row, total_steps), jnp.bfloat16),
            pltpu.VMEM((2 * block_size, total_steps), jnp.bfloat16),
            pltpu.VMEM((wide, block_size), jnp.bfloat16),
            pltpu.VMEM((slots, LAGS, per_row, block_size), jnp.bfloat16),
            pltpu.VMEM((per_row, total_steps), jnp.float32),
            pltpu.SemaphoreType.DMA((slots,)),
        ],
        input_output_aliases=aliases,
        compiler_params=PARAMS,
        cost_estimate=pl.CostEstimate(
            flops=slots * 2 * LAGS * per_row * block_size * total_steps,
            bytes_accessed=slots * LAGS * per_row * block_size * 2 + slots * 600000,
            transcendentals=0,
        ),
    )(*operands)


def fold(first_of, served, rows, cols, blk_dev):
    groups = len(rows)
    slots, _, block_size = rows[0].shape

    def kernel(first_ref, served_ref, *rest):
        row_refs, col_refs, out_ref = rest[:groups], rest[groups : 2 * groups], rest[2 * groups]
        place = lax.broadcasted_iota(jnp.int32, (blk_dev, block_size), 0)
        own, other = [], []
        for d in range(groups):
            for j in range(slots):
                own.append(place == first_ref[d * slots + j])
                other.append(place == served_ref[d * slots + j])
        for lag in range(LAGS):
            total = jnp.zeros((blk_dev, block_size), jnp.float32)
            for d in range(groups):
                for j in range(slots):
                    total = total + jnp.where(
                        own[d * slots + j], row_refs[d][j, lag : lag + 1, :], 0.0
                    )
                    total = total + jnp.where(
                        other[d * slots + j], col_refs[d][lag, j : j + 1, :], 0.0
                    )
            out_ref[lag] = total.astype(jnp.bfloat16)

    return pl.pallas_call(
        kernel,
        out_shape=jax.ShapeDtypeStruct((LAGS, blk_dev, block_size), jnp.bfloat16),
        in_specs=[SMEM, SMEM] + [VMEM] * (2 * groups),
        out_specs=VMEM,
        compiler_params=PARAMS,
    )(first_of, served, *rows, *cols)


def local(readings, present, pair_first, pair_second):
    blk_dev, block_size, steps_here = readings.shape
    pair_count = pair_first.shape[0]
    sensor_count = lax.axis_size("sensor")
    tm_count = lax.axis_size("tm")
    lag_count = lax.axis_size("lag")
    home = lax.axis_index("sensor")
    tm_place = lax.axis_index("tm")
    lag_place = lax.axis_index("lag")
    per_row = block_size // (tm_count * lag_count)
    groups = sorted({d % sensor_count for d in range(-REACH, REACH + 1)})
    slot_count = len(groups) * CAP

    first_index = pair_first - home * blk_dev
    owner = pair_second // blk_dev
    partner_index = pair_second - owner * blk_dev
    positions = jnp.arange(pair_count)
    earlier = (owner[:, None] == owner[None, :]) & (positions[None, :] < positions[:, None])
    rank = jnp.sum(earlier.astype(jnp.int32), axis=1)
    distance = (owner - home + sensor_count) % sensor_count
    group = jnp.sum(
        jnp.where(distance[:, None] == jnp.array(groups)[None, :], jnp.arange(len(groups)), 0),
        axis=1,
    )
    slot = group * CAP + (lag_place - rank + CAP) % CAP
    hot = slot[:, None] == jnp.arange(slot_count)[None, :]
    requests = jnp.sum(jnp.where(hot, partner_index[:, None], 0), axis=0)
    pair_of = jnp.sum(jnp.where(hot, positions[:, None] + 1, 0), axis=0) - 1
    first_of = jnp.sum(jnp.where(hot, first_index[:, None], 0), axis=0)

    served = [requests[:CAP]] + [
        rotated(requests[i * CAP : (i + 1) * CAP], "sensor", d)
        for i, d in enumerate(groups)
        if i > 0
    ]
    turns = jnp.arange(tm_count)
    row_starts = ((tm_place + turns) % tm_count * lag_count + lag_place) * per_row
    sent = pack_first(readings, present, first_index, row_starts, per_row)
    firsts = [sent[0]] + [rotated(sent[k], "tm", k) for k in range(1, tm_count)]
    places = jnp.concatenate([(tm_place - turns) % tm_count, row_starts[:1]])

    here = pack_blocks(readings, present, requests[:CAP])
    away = pack_blocks(readings, present, jnp.stack([s[0] for s in served[1:]]))
    cov = None
    rows, cols = [], []
    for i, d in enumerate(groups):
        own = here[0] if i == 0 else rotated(away[i - 1], "sensor", -d)
        own_windows = [own] + [rotated(own, "tm", k) for k in range(1, tm_count)]
        blocks = [own_windows]
        for j in range(1, lag_count):
            blocks.append(
                [
                    here[j] if i == 0 and k == 0 else rotated(own_windows[k], "lag", j)
                    for k in range(tm_count)
                ]
            )
        cov, row, col = covariances(
            pair_of[i * CAP : (i + 1) * CAP],
            places,
            firsts,
            blocks,
            cov,
            pair_count,
            per_row,
            block_size,
        )
        rows.append(row)
        cols.append(col if i == 0 else rotated(col, "sensor", d))
    partial = fold(first_of, jnp.concatenate(served), rows, cols, blk_dev)
    partial = partial.astype(jnp.float32)
    if lag_count == 2:
        partial = partial + rotated(partial.astype(jnp.bfloat16), "lag", 1).astype(jnp.float32)
    else:
        partial = lax.psum(partial.astype(jnp.bfloat16), "lag").astype(jnp.float32)
    partial = partial.astype(jnp.bfloat16)
    if tm_count == 2:
        strength = partial.astype(jnp.float32) + rotated(partial, "tm", 1).astype(jnp.float32)
    else:
        strength = lax.psum(partial, "tm").astype(jnp.float32)
    return (cov, strength)


def solution(mesh):
    in_specs = (
        P(("parts", "sensor"), None, "tm"),
        P(("parts", "sensor"), "tm"),
        P(("parts", "sensor")),
        P(("parts", "sensor")),
    )
    out_specs = (
        P(("parts", "sensor"), None, ("tm", "lag"), None),
        P(None, ("parts", "sensor"), None),
    )
    return jax.shard_map(local, mesh=mesh, in_specs=in_specs, out_specs=out_specs, check_vma=False)
```

time: 227 us -> 72.4 us (0.32)
  waiting for transfers between devices: 103 us -> 28.5 us
  matrix products: 32.1 us -> 0 us
  starting transfers between devices: 39.9 us -> 21.2 us
  Pallas kernels: 0 us -> 16.4 us
  local copies, waits for them, and re-layouts: 18.3 us -> 2.51 us
  between operations: 14.5 us -> 0.82 us
  other arithmetic: 13.5 us -> 2.7 us
  blocking collectives: 5.07 us -> 0 us
    reduce_scatter x1 -> x0, waiting for transfers between devices: 41.9 us -> none  [local(): lax.psum_scatter(jnp.stack(lagged, axis=2).astype(jnp.bfloat16), 'tm', sc...]
    dot_general x28 -> x0, matrix products: 32.1 us -> none  [the longest x25 31.1 us: local(): jnp.einsum('pat,pbt->apb', own_rows, extended[:, :, lag_step:lag_step + s...]
    psum x1 -> x0, waiting for transfers between devices: 28.7 us -> none  [local(): lax.psum(partial_value.astype(jnp.bfloat16), ('tm', 'lag'))]
    ppermute x19 -> x23, starting transfers between devices: 39.6 us -> 21.2 us  [rotated(): lax.ppermute(block, axis, [(i, (i + distance) % size) for i in range(size)])]
    pallas_call x0 -> x8, Pallas kernels: none -> 16.4 us  [the longest x4 12.1 us: covariances(): pl.pallas_call(kernel, out_shape=[jax.ShapeDtypeStruct((pairs, LAGS, per_...]
    gather x9 -> x0, local copies, waits for them, and re-layouts: 8.07 us -> none  [the longest x6 4.78 us: local(): block_list.append(passed_along(centered[requested], 'sensor', -shift_by))]
    unnamed x10 -> x8, local copies, waits for them, and re-layouts: 8.68 us -> 2.36 us
    reduce_sum x5 -> x3, other arithmetic: 5.69 us -> 0.29 us  [the longest x1 0.18 us: local(): rank = jnp.sum(earlier.astype(jnp.int32), axis=1)]
  transfers between devices with their start and end apart: 21 -> 23, of which waited for: 8 -> 12; matrix products, arithmetic and copies ran while one was open for 10% -> 1% of each run, Pallas kernels for 0% -> 16%
where the time goes in v1:
time: 72.4 us; the launch traced here: 72.1 us
  waiting for transfers between devices  28.5 us (39%)
  starting transfers between devices  21.2 us (29%)
  Pallas kernels  16.4 us (23%)
  other arithmetic  2.7 us (4%)
  local copies, waits for them, and re-layouts  2.51 us (3%)
  between operations  0.82 us (1%)
    ppermute x23, waiting for transfers between devices, rotated(): lax.ppermute(block, axis, [(i, (i + distance) % size) for i in range(size)])  28.5 us
    ppermute x23, starting transfers between devices, rotated(): lax.ppermute(block, axis, [(i, (i + distance) % size) for i in range(size)])  21.2 us
    pallas_call x4, Pallas kernels, covariances(): pl.pallas_call(kernel, out_shape=[jax.ShapeDtypeStruct((pairs, LAGS, per_...  12.1 us
    unnamed x8, local copies, waits for them, and re-layouts  2.36 us
    pallas_call x2, Pallas kernels, pack_blocks(): pl.pallas_call(kernel, out_shape=[jax.ShapeDtypeStruct((rows + PAD, steps...  2.01 us
  transfers between devices with their start and end apart: 23, of which 12 were waited for; matrix products, arithmetic and copies ran while one was open for 1% of the time, Pallas kernels for 16%

profile of v1, /device:TPU:0, one launch (start us, length us, event | category | flops | bytes accessed | tf_op | source)
XLA Modules:
  0.0 72.1 jit_solution(9111252595981786485)
XLA Ops:
  0.6 0.0 copy-start.3
  0.6 0.7 multiply_subtract_fusion
  1.3 0.2 convert_reduce_fusion
  1.5 0.7 broadcast_subtract_fusion.first_ref
  2.2 0.1 select_reduce_fusion
  2.3 0.1 fusion.9
  2.4 1.6 %copy-done = bf16[16,128,512]{2,1,0:T(8,128)(2,1)S(1)} copy-done((bf16[16,128,512]{2,1,0:T(8,128)(2,1)S(1)}, bf16[16,128,512]{2,1,0:T(8,128)(2,1)}, u32[]{:S(2)}) %copy-start) | copy-done | bytes 2097176
  4.0 0.8 %copy-done.2 = s32[16,512]{1,0:T(8,128)S(1)} copy-done((s32[16,512]{1,0:T(8,128)S(1)}, s32[16,512]{1,0:T(8,128)}, u32[]{:S(2)}) %copy-start.2) | copy-done | bytes 32792
  4.7 0.9 %shard_map.70 = (bf16[144,512]{1,0:T(8,128)(2,1)S(1)}, bf16[144,512]{1,0:T(8,128)(2,1)S(1)}) custom-call(s32[2]{0:T(128)S(1)} %get-tuple-element.45.index_ref, bf16[16,128,512]{2,1,0:T(8,128)(2,1)S(1)} %copy-done, s32[16,512]{1,0:T(8,128)S(1)} %copy-done.2), custom_call_target="tpu_custom_call" | custom-call | tf_op jit(solution)/shard_map/pallas_call | solution.py:51
  5.6 3.0 %collective-permute-start.16 = (bf16[144,512]{1,0:T(8,128)(2,1)S(1)}, bf16[144,512]{1,0:T(8,128)(2,1)S(1)}, u32[]{:S(2)}, u32[]{:S(2)}) collective-permute-start(bf16[144,512]{1,0:T(8,128)(2,1)S(1)} %get-tuple-element.26.rest_2_), channel_id=1, source_target_pairs={{0,2},{2,0},{1,3},{3,1},{4,6},{6,4},{5,7},{7,5},{8,10},{10,8},{9,1... | collective-permute-start | bytes 442376 | tf_op jit(solution)/shard_map/ppermute | solution.py:22
  8.7 1.4 %shard_map.68 = (bf16[272,512]{1,0:T(8,128)(2,1)S(1)}, bf16[272,512]{1,0:T(8,128)(2,1)S(1)}) custom-call(s32[8]{0:T(128)S(1)} %broadcast_subtract_fusion.first_ref, s32[2]{0:T(128)S(1)} %fusion.4.start_ref, bf16[16,128,512]{2,1,0:T(8,128)(2,1)S(1)} %copy-done.1, s32[16,512]{1,0:T(8,128)S(1)} %copy-done.3), custom_call_target="tpu_custom_call" | custom-call | tf_op jit(solution)/shard_map/pallas_call | solution.py:90
  10.1 0.6 collective-permute-start
  10.8 3.6 %collective-permute-start.3 = (s32[2]{0:T(128)S(1)}, s32[2]{0:T(128)S(1)}, u32[]{:S(2)}, u32[]{:S(2)}) collective-permute-start(s32[2]{0:T(128)S(1)} %get-tuple-element.46), channel_id=1, source_target_pairs={{0,12},{4,0},{8,4},{12,8},{1,13},{5,1},{9,5},{13,9},{2,14},{6,2},{... | collective-permute-start | bytes 32 | tf_op jit(solution)/shard_map/ppermute | solution.py:22
  14.4 0.0 collective-permute-start.2
  14.4 1.0 %collective-permute-start.1 = (s32[2]{0:T(128)S(1)}, s32[2]{0:T(128)S(1)}, u32[]{:S(2)}, u32[]{:S(2)}) collective-permute-start(s32[2]{0:T(128)S(1)} %get-tuple-element.48), channel_id=1, source_target_pairs={{0,4},{4,8},{8,12},{12,0},{1,5},{5,9},{9,13},{13,1},{2,6},{6,10},{... | collective-permute-start | bytes 32 | tf_op jit(solution)/shard_map/ppermute | solution.py:22
  15.4 0.3 collective-permute-done.3
  15.7 3.1 %collective-permute-done.2 = s32[2]{0:T(128)S(1)} collective-permute-done((s32[2]{0:T(128)S(1)}, s32[2]{0:T(128)S(1)}, u32[]{:S(2)}, u32[]{:S(2)}) %collective-permute-start.2) | collective-permute-done | bytes 40 | tf_op jit(solution)/shard_map/ppermute | solution.py:22
  18.8 0.9 %collective-permute-done.1 = s32[2]{0:T(128)S(1)} collective-permute-done((s32[2]{0:T(128)S(1)}, s32[2]{0:T(128)S(1)}, u32[]{:S(2)}, u32[]{:S(2)}) %collective-permute-start.1) | collective-permute-done | bytes 40 | tf_op jit(solution)/shard_map/ppermute | solution.py:22
  19.7 0.1 pad_add_fusion.1.index_ref
  19.8 1.1 %shard_map.69 = (bf16[144,512]{1,0:T(8,128)(2,1)S(1)}, bf16[144,512]{1,0:T(8,128)(2,1)S(1)}, bf16[144,512]{1,0:T(8,128)(2,1)S(1)}) custom-call(s32[3]{0:T(128)S(1)} %pad_add_fusion.1.index_ref, bf16[16,128,512]{2,1,0:T(8,128)(2,1)S(1)} %copy-done.1, s32[16,512]{1,0:T(8,128)S(1)} %copy-done.3), custom_call_target="tpu_custom_call" | custom-call | tf_op jit(solution)/shard_map/pallas_call | solution.py:51
  20.9 0.6 collective-permute-start.12
  21.5 0.6 collective-permute-start.8
  22.2 1.9 %collective-permute-start.4 = (bf16[144,512]{1,0:T(8,128)(2,1)S(1)}, bf16[144,512]{1,0:T(8,128)(2,1)S(1)}, u32[]{:S(2)}, u32[]{:S(2)}) collective-permute-start(bf16[144,512]{1,0:T(8,128)(2,1)S(1)} %get-tuple-element.23), channel_id=1, source_target_pairs={{0,4},{4,8},{8,12},{12,0},{1,5},{5,9},{9,13},{13,1},{2,6},{6,10},{... | collective-permute-start | bytes 442376 | tf_op jit(solution)/shard_map/ppermute | solution.py:22
  24.1 0.0 collective-permute-done.16.rest_3_
  24.1 0.0 collective-permute-start.17
  24.1 3.5 %collective-permute-done.12.rest_2_ = bf16[144,512]{1,0:T(8,128)(2,1)S(1)} collective-permute-done((bf16[144,512]{1,0:T(8,128)(2,1)S(1)}, bf16[144,512]{1,0:T(8,128)(2,1)S(1)}, u32[]{:S(2)}, u32[]{:S(2)}) %collective-permute-start.12) | collective-permute-done | bytes 147488 | tf_op jit(solution)/shard_map/ppermute | solution.py:22
  27.6 2.3 %collective-permute-start.13 = (bf16[144,512]{1,0:T(8,128)(2,1)S(1)}, bf16[144,512]{1,0:T(8,128)(2,1)S(1)}, u32[]{:S(2)}, u32[]{:S(2)}) collective-permute-start(bf16[144,512]{1,0:T(8,128)(2,1)S(1)} %collective-permute-done.12.rest_2_), channel_id=1, source_target_pairs={{0,2},{2,0},{1,3},{3,1},{4,6},{6,4},{5,7},{7,5},{8,10},{10,8},{9,1... | collective-permute-start | bytes 442376 | tf_op jit(solution)/shard_map/ppermute | solution.py:22
  29.9 4.3 %collective-permute-done.8.rest_2_ = bf16[144,512]{1,0:T(8,128)(2,1)S(1)} collective-permute-done((bf16[144,512]{1,0:T(8,128)(2,1)S(1)}, bf16[144,512]{1,0:T(8,128)(2,1)S(1)}, u32[]{:S(2)}, u32[]{:S(2)}) %collective-permute-start.8) | collective-permute-done | bytes 147488 | tf_op jit(solution)/shard_map/ppermute | solution.py:22
  34.2 0.0 collective-permute-start.14
  34.2 0.0 collective-permute-done.4.rest_2_
  34.2 1.2 %collective-permute-start.9 = (bf16[144,512]{1,0:T(8,128)(2,1)S(1)}, bf16[144,512]{1,0:T(8,128)(2,1)S(1)}, u32[]{:S(2)}, u32[]{:S(2)}) collective-permute-start(bf16[144,512]{1,0:T(8,128)(2,1)S(1)} %collective-permute-done.8.rest_2_), channel_id=1, source_target_pairs={{0,2},{2,0},{1,3},{3,1},{4,6},{6,4},{5,7},{7,5},{8,10},{10,8},{9,1... | collective-permute-start | bytes 442376 | tf_op jit(solution)/shard_map/ppermute | solution.py:22
  35.4 0.0 collective-permute-done.rest_1_
  35.4 0.9 %collective-permute-start.5 = (bf16[144,512]{1,0:T(8,128)(2,1)S(1)}, bf16[144,512]{1,0:T(8,128)(2,1)S(1)}, u32[]{:S(2)}, u32[]{:S(2)}) collective-permute-start(bf16[144,512]{1,0:T(8,128)(2,1)S(1)} %collective-permute-done.4.rest_2_), channel_id=1, source_target_pairs={{0,2},{2,0},{1,3},{3,1},{4,6},{6,4},{5,7},{7,5},{8,10},{10,8},{9,1... | collective-permute-start | bytes 442376 | tf_op jit(solution)/shard_map/ppermute | solution.py:22
  36.3 0.1 fusion.10
  36.3 0.1 collective-permute-start.10
  36.4 0.5 collective-permute-start.6
  36.9 0.0 collective-permute-done.14.rest_4_
  36.9 0.1 collective-permute-start.15
  37.0 3.9 %collective-permute-done.9.rest_3_ = bf16[144,512]{1,0:T(8,128)(2,1)S(1)} collective-permute-done((bf16[144,512]{1,0:T(8,128)(2,1)S(1)}, bf16[144,512]{1,0:T(8,128)(2,1)S(1)}, u32[]{:S(2)}, u32[]{:S(2)}) %collective-permute-start.9) | collective-permute-done | bytes 147488 | tf_op jit(solution)/shard_map/ppermute | solution.py:22
  40.9 0.0 collective-permute-start.11
  40.9 2.8 %collective-permute-done.5.rest_3_ = bf16[144,512]{1,0:T(8,128)(2,1)S(1)} collective-permute-done((bf16[144,512]{1,0:T(8,128)(2,1)S(1)}, bf16[144,512]{1,0:T(8,128)(2,1)S(1)}, u32[]{:S(2)}, u32[]{:S(2)}) %collective-permute-start.5) | collective-permute-done | bytes 147488 | tf_op jit(solution)/shard_map/ppermute | solution.py:22
  43.6 0.0 collective-permute-start.7
  43.7 0.1 pad_add_fusion.place_ref
  43.8 3.0 %shard_map.71 = (bf16[8,25,32,128]{3,2,1,0:T(8,128)(2,1)}, f32[2,32,128]{2,1,0:T(8,128)S(1)}, f32[25,2,128]{2,1,0:T(2,128)S(1)}) custom-call(s32[2]{0:T(128)S(1)} %get-tuple-element.49.pair_ref, s32[3]{0:T(128)S(1)} %pad_add_fusion.place_ref, bf16[272,512]{1,0:T(8,128)(2,1)S(1)} %get-tuple-element.21.rest_0_, ...), custom_call_target="tpu_custom_call" | custom-call | flops 419430400 | bytes 1609600 | tf_op jit(solution)/shard_map/pallas_call | solution.py:219
  46.8 0.0 collective-permute-done.15.rest_5_
  46.8 3.0 %shard_map.72 = (bf16[8,25,32,128]{3,2,1,0:T(8,128)(2,1)}, f32[2,32,128]{2,1,0:T(8,128)S(1)}, f32[25,2,128]{2,1,0:T(2,128)S(1)}) custom-call(s32[2]{0:T(128)S(1)} %get-tuple-element.50.pair_ref, s32[3]{0:T(128)S(1)} %pad_add_fusion.place_ref, bf16[272,512]{1,0:T(8,128)(2,1)S(1)} %get-tuple-element.21.rest_0_, ...), custom_call_target="tpu_custom_call", output_to_operand_aliasing={{0}: (8, {})} | custom-call | flops 419430400 | bytes 1609600 | tf_op jit(solution)/shard_map/pallas_call | solution.py:219
  49.8 0.0 collective-permute-done.10.rest_4_
  49.9 3.0 %shard_map.73 = (bf16[8,25,32,128]{3,2,1,0:T(8,128)(2,1)}, f32[2,32,128]{2,1,0:T(8,128)S(1)}, f32[25,2,128]{2,1,0:T(2,128)S(1)}) custom-call(s32[2]{0:T(128)S(1)} %get-tuple-element.51.pair_ref, s32[3]{0:T(128)S(1)} %pad_add_fusion.place_ref, bf16[272,512]{1,0:T(8,128)(2,1)S(1)} %get-tuple-element.21.rest_0_, ...), custom_call_target="tpu_custom_call", output_to_operand_aliasing={{0}: (8, {})} | custom-call | flops 419430400 | bytes 1609600 | tf_op jit(solution)/shard_map/pallas_call | solution.py:219
  52.9 0.0 collective-permute-done.6.rest_4_
  52.9 0.0 collective-permute-done.7.rest_5_
  52.9 3.0 %shard_map.74 = (bf16[8,25,32,128]{3,2,1,0:T(8,128)(2,1)}, f32[2,32,128]{2,1,0:T(8,128)S(1)}, f32[25,2,128]{2,1,0:T(2,128)S(1)}) custom-call(s32[2]{0:T(128)S(1)} %get-tuple-element.52.pair_ref, s32[3]{0:T(128)S(1)} %pad_add_fusion.place_ref, bf16[272,512]{1,0:T(8,128)(2,1)S(1)} %get-tuple-element.21.rest_0_, ...), custom_call_target="tpu_custom_call", output_to_operand_aliasing={{0}: (8, {})} | custom-call | flops 419430400 | bytes 1609600 | tf_op jit(solution)/shard_map/pallas_call | solution.py:219
  56.0 0.1 collective-permute-start.20
  56.0 2.5 %collective-permute-start.19 = (f32[25,2,128]{2,1,0:T(2,128)S(1)}, f32[25,2,128]{2,1,0:T(2,128)S(1)}, u32[]{:S(2)}, u32[]{:S(2)}) collective-permute-start(f32[25,2,128]{2,1,0:T(2,128)S(1)} %get-tuple-element.38), channel_id=1, source_target_pairs={{0,8},{4,12},{8,0},{12,4},{1,9},{5,13},{9,1},{13,5},{2,10},{6,14},... | collective-permute-start | bytes 76808 | tf_op jit(solution)/shard_map/ppermute | solution.py:22
  58.5 0.9 %collective-permute-start.18 = (f32[25,2,128]{2,1,0:T(2,128)S(1)}, f32[25,2,128]{2,1,0:T(2,128)S(1)}, u32[]{:S(2)}, u32[]{:S(2)}) collective-permute-start(f32[25,2,128]{2,1,0:T(2,128)S(1)} %get-tuple-element.37), channel_id=1, source_target_pairs={{0,4},{4,8},{8,12},{12,0},{1,5},{5,9},{9,13},{13,1},{2,6},{6,10},{... | collective-permute-start | bytes 76808 | tf_op jit(solution)/shard_map/ppermute | solution.py:22
  59.4 0.1 pad_add_fusion.2.served_ref
  59.5 0.4 collective-permute-done.20.rest_7_
  59.9 1.0 %collective-permute-done.19.rest_6_ = f32[25,2,128]{2,1,0:T(2,128)S(1)} collective-permute-done((f32[25,2,128]{2,1,0:T(2,128)S(1)}, f32[25,2,128]{2,1,0:T(2,128)S(1)}, u32[]{:S(2)}, u32[]{:S(2)}) %collective-permute-start.19) | collective-permute-done | bytes 25632 | tf_op jit(solution)/shard_map/ppermute | solution.py:22
  60.9 3.3 %collective-permute-done.18.rest_5_ = f32[25,2,128]{2,1,0:T(2,128)S(1)} collective-permute-done((f32[25,2,128]{2,1,0:T(2,128)S(1)}, f32[25,2,128]{2,1,0:T(2,128)S(1)}, u32[]{:S(2)}, u32[]{:S(2)}) %collective-permute-start.18) | collective-permute-done | bytes 25632 | tf_op jit(solution)/shard_map/ppermute | solution.py:22
  64.1 0.8 %shard_map.75 = bf16[25,16,128]{2,1,0:T(8,128)(2,1)S(1)} custom-call(s32[8]{0:T(128)S(1)} %get-tuple-element.40.first_ref, s32[8]{0:T(128)S(1)} %pad_add_fusion.2.served_ref, f32[2,32,128]{2,1,0:T(8,128)S(1)} %get-tuple-element.32.rest_0_, f32[2,32,128]{2,1,0:T(8,128)S(1)} %get-tuple-element.33.rest_1_, f32[2,32,128]{2,1,0:T(8,128)S(1)} %get-tuple-element.34.rest_2_, ...), custom_call_target="tpu_custom_call" | custom-call | tf_op jit(solution)/shard_map/pallas_call | solution.py:270
  65.0 0.1 collective-permute-start.21
  65.1 1.3 %collective-permute-done.21 = bf16[25,16,128]{2,1,0:T(8,128)(2,1)S(1)} collective-permute-done((bf16[25,16,128]{2,1,0:T(8,128)(2,1)S(1)}, bf16[25,16,128]{2,1,0:T(8,128)(2,1)S(1)}, u32[]{:S(2)}, u32[]{:S(2)}) %collective-permute-start.21) | collective-permute-done | bytes 102432 | tf_op jit(solution)/shard_map/ppermute | solution.py:22
  66.4 1.3 %collective-permute-start.22 = (bf16[25,16,128]{2,1,0:T(8,128)(2,1)S(1)}, bf16[25,16,128]{2,1,0:T(8,128)(2,1)S(1)}, u32[]{:S(2)}, u32[]{:S(2)}) collective-permute-start(bf16[25,16,128]{2,1,0:T(8,128)(2,1)S(1)} %add_convert_fusion), channel_id=1, source_target_pairs={{0,2},{2,0},{1,3},{3,1},{4,6},{6,4},{5,7},{7,5},{8,10},{10,8},{9,1... | collective-permute-start | bytes 307208 | tf_op jit(solution)/shard_map/ppermute | solution.py:22
  67.6 3.7 %collective-permute-done.22 = bf16[25,16,128]{2,1,0:T(8,128)(2,1)S(1)} collective-permute-done((bf16[25,16,128]{2,1,0:T(8,128)(2,1)S(1)}, bf16[25,16,128]{2,1,0:T(8,128)(2,1)S(1)}, u32[]{:S(2)}, u32[]{:S(2)}) %collective-permute-start.22) | collective-permute-done | bytes 102432 | tf_op jit(solution)/shard_map/ppermute | solution.py:22
  71.4 0.7 convert_add_fusion
  (15 shorter events, 0.1 us)
Async XLA Ops:
  0.6 8.0 %copy-start.3 = (s32[16,512]{1,0:T(8,128)S(1)}, s32[16,512]{1,0:T(8,128)}, u32[]{:S(2)}) copy-start(s32[16,512]{1,0:T(8,128)} %present_ref.5) | copy-start | bytes 98308
  2.4 1.6 %copy-start = (bf16[16,128,512]{2,1,0:T(8,128)(2,1)S(1)}, bf16[16,128,512]{2,1,0:T(8,128)(2,1)}, u32[]{:S(2)}) copy-start(bf16[16,128,512]{2,1,0:T(8,128)(2,1)} %readings_ref.5) | copy-start | bytes 6291460
  4.0 0.8 %copy-start.2 = (s32[16,512]{1,0:T(8,128)S(1)}, s32[16,512]{1,0:T(8,128)}, u32[]{:S(2)}) copy-start(s32[16,512]{1,0:T(8,128)} %present_ref.5) | copy-start | bytes 98308
  4.7 3.9 %copy-start.1 = (bf16[16,128,512]{2,1,0:T(8,128)(2,1)S(1)}, bf16[16,128,512]{2,1,0:T(8,128)(2,1)}, u32[]{:S(2)}) copy-start(bf16[16,128,512]{2,1,0:T(8,128)(2,1)} %readings_ref.5) | copy-start | bytes 6291460
  5.6 18.5 %collective-permute-start.16 = (bf16[144,512]{1,0:T(8,128)(2,1)S(1)}, bf16[144,512]{1,0:T(8,128)(2,1)S(1)}, u32[]{:S(2)}, u32[]{:S(2)}) collective-permute-start(bf16[144,512]{1,0:T(8,128)(2,1)S(1)} %get-tuple-element.26.rest_2_), channel_id=1, source_target_pairs={{0,2},{2,0},{1,3},{3,1},{4,6},{6,4},{5,7},{7,5},{8,10},{10,8},{9,1... | collective-permute-start | bytes 442376 | tf_op jit(solution)/shard_map/ppermute | solution.py:22
  10.1 25.3 %collective-permute-start = (bf16[272,512]{1,0:T(8,128)(2,1)S(1)}, bf16[272,512]{1,0:T(8,128)(2,1)S(1)}, u32[]{:S(2)}, u32[]{:S(2)}) collective-permute-start(bf16[272,512]{1,0:T(8,128)(2,1)S(1)} %get-tuple-element.22), channel_id=1, source_target_pairs={{0,2},{2,0},{1,3},{3,1},{4,6},{6,4},{5,7},{7,5},{8,10},{10,8},{9,1... | collective-permute-start | bytes 835592 | tf_op jit(solution)/shard_map/ppermute | solution.py:22
  10.8 4.9 %collective-permute-start.3 = (s32[2]{0:T(128)S(1)}, s32[2]{0:T(128)S(1)}, u32[]{:S(2)}, u32[]{:S(2)}) collective-permute-start(s32[2]{0:T(128)S(1)} %get-tuple-element.46), channel_id=1, source_target_pairs={{0,12},{4,0},{8,4},{12,8},{1,13},{5,1},{9,5},{13,9},{2,14},{6,2},{... | collective-permute-start | bytes 32 | tf_op jit(solution)/shard_map/ppermute | solution.py:22
  14.4 4.4 %collective-permute-start.2 = (s32[2]{0:T(128)S(1)}, s32[2]{0:T(128)S(1)}, u32[]{:S(2)}, u32[]{:S(2)}) collective-permute-start(s32[2]{0:T(128)S(1)} %get-tuple-element.47), channel_id=1, source_target_pairs={{0,8},{4,12},{8,0},{12,4},{1,9},{5,13},{9,1},{13,5},{2,10},{6,14},... | collective-permute-start | bytes 32 | tf_op jit(solution)/shard_map/ppermute | solution.py:22
  14.4 5.3 %collective-permute-start.1 = (s32[2]{0:T(128)S(1)}, s32[2]{0:T(128)S(1)}, u32[]{:S(2)}, u32[]{:S(2)}) collective-permute-start(s32[2]{0:T(128)S(1)} %get-tuple-element.48), channel_id=1, source_target_pairs={{0,4},{4,8},{8,12},{12,0},{1,5},{5,9},{9,13},{13,1},{2,6},{6,10},{... | collective-permute-start | bytes 32 | tf_op jit(solution)/shard_map/ppermute | solution.py:22
  20.9 6.7 %collective-permute-start.12 = (bf16[144,512]{1,0:T(8,128)(2,1)S(1)}, bf16[144,512]{1,0:T(8,128)(2,1)S(1)}, u32[]{:S(2)}, u32[]{:S(2)}) collective-permute-start(bf16[144,512]{1,0:T(8,128)(2,1)S(1)} %get-tuple-element.25), channel_id=1, source_target_pairs={{0,12},{4,0},{8,4},{12,8},{1,13},{5,1},{9,5},{13,9},{2,14},{6,2},{... | collective-permute-start | bytes 442376 | tf_op jit(solution)/shard_map/ppermute | solution.py:22
  21.5 12.7 %collective-permute-start.8 = (bf16[144,512]{1,0:T(8,128)(2,1)S(1)}, bf16[144,512]{1,0:T(8,128)(2,1)S(1)}, u32[]{:S(2)}, u32[]{:S(2)}) collective-permute-start(bf16[144,512]{1,0:T(8,128)(2,1)S(1)} %get-tuple-element.24), channel_id=1, source_target_pairs={{0,8},{4,12},{8,0},{12,4},{1,9},{5,13},{9,1},{13,5},{2,10},{6,14},... | collective-permute-start | bytes 442376 | tf_op jit(solution)/shard_map/ppermute | solution.py:22
  22.2 12.1 %collective-permute-start.4 = (bf16[144,512]{1,0:T(8,128)(2,1)S(1)}, bf16[144,512]{1,0:T(8,128)(2,1)S(1)}, u32[]{:S(2)}, u32[]{:S(2)}) collective-permute-start(bf16[144,512]{1,0:T(8,128)(2,1)S(1)} %get-tuple-element.23), channel_id=1, source_target_pairs={{0,4},{4,8},{8,12},{12,0},{1,5},{5,9},{9,13},{13,1},{2,6},{6,10},{... | collective-permute-start | bytes 442376 | tf_op jit(solution)/shard_map/ppermute | solution.py:22
  24.1 12.2 %collective-permute-start.17 = (bf16[144,512]{1,0:T(8,128)(2,1)S(1)}, bf16[144,512]{1,0:T(8,128)(2,1)S(1)}, u32[]{:S(2)}, u32[]{:S(2)}) collective-permute-start(bf16[144,512]{1,0:T(8,128)(2,1)S(1)} %collective-permute-done.16.rest_3_), channel_id=1, source_target_pairs={{0,1},{1,0},{2,3},{3,2},{4,5},{5,4},{6,7},{7,6},{8,9},{9,8},{10,11... | collective-permute-start | bytes 442376 | tf_op jit(solution)/shard_map/ppermute | solution.py:22
  27.6 8.8 %collective-permute-start.13 = (bf16[144,512]{1,0:T(8,128)(2,1)S(1)}, bf16[144,512]{1,0:T(8,128)(2,1)S(1)}, u32[]{:S(2)}, u32[]{:S(2)}) collective-permute-start(bf16[144,512]{1,0:T(8,128)(2,1)S(1)} %collective-permute-done.12.rest_2_), channel_id=1, source_target_pairs={{0,2},{2,0},{1,3},{3,1},{4,6},{6,4},{5,7},{7,5},{8,10},{10,8},{9,1... | collective-permute-start | bytes 442376 | tf_op jit(solution)/shard_map/ppermute | solution.py:22
  34.2 2.7 %collective-permute-start.14 = (bf16[144,512]{1,0:T(8,128)(2,1)S(1)}, bf16[144,512]{1,0:T(8,128)(2,1)S(1)}, u32[]{:S(2)}, u32[]{:S(2)}) collective-permute-start(bf16[144,512]{1,0:T(8,128)(2,1)S(1)} %collective-permute-done.12.rest_2_), channel_id=1, source_target_pairs={{0,1},{1,0},{2,3},{3,2},{4,5},{5,4},{6,7},{7,6},{8,9},{9,8},{10,11... | collective-permute-start | bytes 442376 | tf_op jit(solution)/shard_map/ppermute | solution.py:22
  34.2 6.6 %collective-permute-start.9 = (bf16[144,512]{1,0:T(8,128)(2,1)S(1)}, bf16[144,512]{1,0:T(8,128)(2,1)S(1)}, u32[]{:S(2)}, u32[]{:S(2)}) collective-permute-start(bf16[144,512]{1,0:T(8,128)(2,1)S(1)} %collective-permute-done.8.rest_2_), channel_id=1, source_target_pairs={{0,2},{2,0},{1,3},{3,1},{4,6},{6,4},{5,7},{7,5},{8,10},{10,8},{9,1... | collective-permute-start | bytes 442376 | tf_op jit(solution)/shard_map/ppermute | solution.py:22
  35.4 8.2 %collective-permute-start.5 = (bf16[144,512]{1,0:T(8,128)(2,1)S(1)}, bf16[144,512]{1,0:T(8,128)(2,1)S(1)}, u32[]{:S(2)}, u32[]{:S(2)}) collective-permute-start(bf16[144,512]{1,0:T(8,128)(2,1)S(1)} %collective-permute-done.4.rest_2_), channel_id=1, source_target_pairs={{0,2},{2,0},{1,3},{3,1},{4,6},{6,4},{5,7},{7,5},{8,10},{10,8},{9,1... | collective-permute-start | bytes 442376 | tf_op jit(solution)/shard_map/ppermute | solution.py:22
  36.3 13.5 %collective-permute-start.10 = (bf16[144,512]{1,0:T(8,128)(2,1)S(1)}, bf16[144,512]{1,0:T(8,128)(2,1)S(1)}, u32[]{:S(2)}, u32[]{:S(2)}) collective-permute-start(bf16[144,512]{1,0:T(8,128)(2,1)S(1)} %collective-permute-done.8.rest_2_), channel_id=1, source_target_pairs={{0,1},{1,0},{2,3},{3,2},{4,5},{5,4},{6,7},{7,6},{8,9},{9,8},{10,11... | collective-permute-start | bytes 442376 | tf_op jit(solution)/shard_map/ppermute | solution.py:22
  36.4 16.5 %collective-permute-start.6 = (bf16[144,512]{1,0:T(8,128)(2,1)S(1)}, bf16[144,512]{1,0:T(8,128)(2,1)S(1)}, u32[]{:S(2)}, u32[]{:S(2)}) collective-permute-start(bf16[144,512]{1,0:T(8,128)(2,1)S(1)} %collective-permute-done.4.rest_2_), channel_id=1, source_target_pairs={{0,1},{1,0},{2,3},{3,2},{4,5},{5,4},{6,7},{7,6},{8,9},{9,8},{10,11... | collective-permute-start | bytes 442376 | tf_op jit(solution)/shard_map/ppermute | solution.py:22
  36.9 9.9 %collective-permute-start.15 = (bf16[144,512]{1,0:T(8,128)(2,1)S(1)}, bf16[144,512]{1,0:T(8,128)(2,1)S(1)}, u32[]{:S(2)}, u32[]{:S(2)}) collective-permute-start(bf16[144,512]{1,0:T(8,128)(2,1)S(1)} %collective-permute-done.13.rest_3_), channel_id=1, source_target_pairs={{0,1},{1,0},{2,3},{3,2},{4,5},{5,4},{6,7},{7,6},{8,9},{9,8},{10,11... | collective-permute-start | bytes 442376 | tf_op jit(solution)/shard_map/ppermute | solution.py:22
  40.9 9.0 %collective-permute-start.11 = (bf16[144,512]{1,0:T(8,128)(2,1)S(1)}, bf16[144,512]{1,0:T(8,128)(2,1)S(1)}, u32[]{:S(2)}, u32[]{:S(2)}) collective-permute-start(bf16[144,512]{1,0:T(8,128)(2,1)S(1)} %collective-permute-done.9.rest_3_), channel_id=1, source_target_pairs={{0,1},{1,0},{2,3},{3,2},{4,5},{5,4},{6,7},{7,6},{8,9},{9,8},{10,11... | collective-permute-start | bytes 442376 | tf_op jit(solution)/shard_map/ppermute | solution.py:22
  43.6 9.3 %collective-permute-start.7 = (bf16[144,512]{1,0:T(8,128)(2,1)S(1)}, bf16[144,512]{1,0:T(8,128)(2,1)S(1)}, u32[]{:S(2)}, u32[]{:S(2)}) collective-permute-start(bf16[144,512]{1,0:T(8,128)(2,1)S(1)} %collective-permute-done.5.rest_3_), channel_id=1, source_target_pairs={{0,1},{1,0},{2,3},{3,2},{4,5},{5,4},{6,7},{7,6},{8,9},{9,8},{10,11... | collective-permute-start | bytes 442376 | tf_op jit(solution)/shard_map/ppermute | solution.py:22
  56.0 3.9 %collective-permute-start.20 = (f32[25,2,128]{2,1,0:T(2,128)S(1)}, f32[25,2,128]{2,1,0:T(2,128)S(1)}, u32[]{:S(2)}, u32[]{:S(2)}) collective-permute-start(f32[25,2,128]{2,1,0:T(2,128)S(1)} %get-tuple-element.39), channel_id=1, source_target_pairs={{0,12},{4,0},{8,4},{12,8},{1,13},{5,1},{9,5},{13,9},{2,14},{6,2},{... | collective-permute-start | bytes 76808 | tf_op jit(solution)/shard_map/ppermute | solution.py:22
  56.0 4.8 %collective-permute-start.19 = (f32[25,2,128]{2,1,0:T(2,128)S(1)}, f32[25,2,128]{2,1,0:T(2,128)S(1)}, u32[]{:S(2)}, u32[]{:S(2)}) collective-permute-start(f32[25,2,128]{2,1,0:T(2,128)S(1)} %get-tuple-element.38), channel_id=1, source_target_pairs={{0,8},{4,12},{8,0},{12,4},{1,9},{5,13},{9,1},{13,5},{2,10},{6,14},... | collective-permute-start | bytes 76808 | tf_op jit(solution)/shard_map/ppermute | solution.py:22
  58.5 5.6 %collective-permute-start.18 = (f32[25,2,128]{2,1,0:T(2,128)S(1)}, f32[25,2,128]{2,1,0:T(2,128)S(1)}, u32[]{:S(2)}, u32[]{:S(2)}) collective-permute-start(f32[25,2,128]{2,1,0:T(2,128)S(1)} %get-tuple-element.37), channel_id=1, source_target_pairs={{0,4},{4,8},{8,12},{12,0},{1,5},{5,9},{9,13},{13,1},{2,6},{6,10},{... | collective-permute-start | bytes 76808 | tf_op jit(solution)/shard_map/ppermute | solution.py:22
  65.0 1.4 %collective-permute-start.21 = (bf16[25,16,128]{2,1,0:T(8,128)(2,1)S(1)}, bf16[25,16,128]{2,1,0:T(8,128)(2,1)S(1)}, u32[]{:S(2)}, u32[]{:S(2)}) collective-permute-start(bf16[25,16,128]{2,1,0:T(8,128)(2,1)S(1)} %shard_map.75), channel_id=1, source_target_pairs={{0,1},{1,0},{2,3},{3,2},{4,5},{5,4},{6,7},{7,6},{8,9},{9,8},{10,11... | collective-permute-start | bytes 307208 | tf_op jit(solution)/shard_map/ppermute | solution.py:22
  66.4 5.0 %collective-permute-start.22 = (bf16[25,16,128]{2,1,0:T(8,128)(2,1)S(1)}, bf16[25,16,128]{2,1,0:T(8,128)(2,1)S(1)}, u32[]{:S(2)}, u32[]{:S(2)}) collective-permute-start(bf16[25,16,128]{2,1,0:T(8,128)(2,1)S(1)} %add_convert_fusion), channel_id=1, source_target_pairs={{0,2},{2,0},{1,3},{3,1},{4,6},{6,4},{5,7},{7,5},{8,10},{10,8},{9,1... | collective-permute-start | bytes 307208 | tf_op jit(solution)/shard_map/ppermute | solution.py:22

commit v2 on v1

--- a/solution.py
+++ b/solution.py
@@ -10,11 +10,20 @@
 REACH = 3
 CAP = 2
 PAD = 16
+MASK_ROWS = 8
 LAG_ROWS = 32
 VMEM = pl.BlockSpec(memory_space=pltpu.VMEM)
 SMEM = pl.BlockSpec(memory_space=pltpu.SMEM)
 ANY = pl.BlockSpec(memory_space=pl.ANY)
+PEAK = 1.15e9
 PARAMS = pltpu.CompilerParams(vmem_limit_bytes=24 * 1024 * 1024)
+WIDE = pltpu.CompilerParams(vmem_limit_bytes=55_000_000)
+
+
+def cost(microseconds):
+    return pl.CostEstimate(
+        flops=int(microseconds * PEAK), bytes_accessed=1024, transcendentals=0
+    )
 
 
 def rotated(block, axis, distance):
@@ -42,19 +51,20 @@
         for copy in copies:
             copy.start()
         for i in range(count):
-            outs[i][rows : rows + PAD, :] = mask_rows(present_ref, index_ref[i], PAD).astype(
-                jnp.bfloat16
-            )
+            outs[i][rows : rows + MASK_ROWS, :] = mask_rows(
+                present_ref, index_ref[i], MASK_ROWS
+            ).astype(jnp.bfloat16)
         for copy in copies:
             copy.wait()
 
     return pl.pallas_call(
         kernel,
-        out_shape=[jax.ShapeDtypeStruct((rows + PAD, steps), jnp.bfloat16)] * count,
+        out_shape=[jax.ShapeDtypeStruct((rows + MASK_ROWS, steps), jnp.bfloat16)] * count,
         in_specs=[SMEM, ANY, VMEM],
         out_specs=[VMEM] * count,
         scratch_shapes=[pltpu.SemaphoreType.DMA((count,))],
-        compiler_params=PARAMS,
+        compiler_params=WIDE,
+        cost_estimate=cost(1.0),
     )(indices, readings, present)
 
 
@@ -93,7 +103,8 @@
         in_specs=[SMEM, SMEM, ANY, VMEM],
         out_specs=[VMEM] * count,
         scratch_shapes=[pltpu.SemaphoreType.DMA((count, pairs))],
-        compiler_params=PARAMS,
+        compiler_params=WIDE,
+        cost_estimate=cost(1.4),
     )(first_index, row_starts, readings, present)
 
 
@@ -235,11 +246,7 @@
         ],
         input_output_aliases=aliases,
         compiler_params=PARAMS,
-        cost_estimate=pl.CostEstimate(
-            flops=slots * 2 * LAGS * per_row * block_size * total_steps,
-            bytes_accessed=slots * LAGS * per_row * block_size * 2 + slots * 600000,
-            transcendentals=0,
-        ),
+        cost_estimate=cost(1.5 * slots),
     )(*operands)
 
 
@@ -273,6 +280,7 @@
         in_specs=[SMEM, SMEM] + [VMEM] * (2 * groups),
         out_specs=VMEM,
         compiler_params=PARAMS,
+        cost_estimate=cost(0.8),
     )(first_of, served, *rows, *cols)
 
 
@@ -317,8 +325,10 @@
     firsts = [sent[0]] + [rotated(sent[k], "tm", k) for k in range(1, tm_count)]
     places = jnp.concatenate([(tm_place - turns) % tm_count, row_starts[:1]])
 
-    here = pack_blocks(readings, present, requests[:CAP])
-    away = pack_blocks(readings, present, jnp.stack([s[0] for s in served[1:]]))
+    packed = pack_blocks(
+        readings, present, jnp.concatenate([requests[:CAP]] + [s[:1] for s in served[1:]])
+    )
+    here, away = packed[:CAP], packed[CAP:]
     cov = None
     rows, cols = [], []
     for i, d in enumerate(groups):

time: 72.4 us -> 64.4 us (0.89)
  waiting for transfers between devices: 28.5 us -> 22.2 us
  local copies, waits for them, and re-layouts: 2.51 us -> 0.9 us
    ppermute x23, waiting for transfers between devices: 28.5 us -> 22.2 us  [rotated(): lax.ppermute(block, axis, [(i, (i + distance) % size) for i in range(size)])]
    unnamed x8 -> x4, local copies, waits for them, and re-layouts: 2.36 us -> 0.75 us
    pallas_call x2 -> x1, Pallas kernels: 2.01 us -> 1.75 us  [pack_blocks(): pl.pallas_call(kernel, out_shape=[jax.ShapeDtypeStruct((rows + MASK_ROWS,...]
  transfers between devices with their start and end apart: 23 -> 23, of which waited for: 12 -> 11; matrix products, arithmetic and copies ran while one was open for 1% -> 1% of each run, Pallas kernels for 16% -> 20%
where the time goes in v2:
time: 64.4 us; the launch traced here: 64.1 us
  waiting for transfers between devices  22.2 us (34%)
  starting transfers between devices  21 us (33%)
  Pallas kernels  16.4 us (25%)
  other arithmetic  2.7 us (4%)
  local copies, waits for them, and re-layouts  0.9 us (1%)
  between operations  0.78 us (1%)
    ppermute x23, waiting for transfers between devices, rotated(): lax.ppermute(block, axis, [(i, (i + distance) % size) for i in range(size)])  22.2 us
    ppermute x23, starting transfers between devices, rotated(): lax.ppermute(block, axis, [(i, (i + distance) % size) for i in range(size)])  21 us
    pallas_call x4, Pallas kernels, covariances(): pl.pallas_call(kernel, out_shape=[jax.ShapeDtypeStruct((pairs, LAGS, per_...  12.1 us
    pallas_call x1, Pallas kernels, pack_blocks(): pl.pallas_call(kernel, out_shape=[jax.ShapeDtypeStruct((rows + MASK_ROWS,...  1.75 us
    pallas_call x1, Pallas kernels, pack_first(): pl.pallas_call(kernel, out_shape=[jax.ShapeDtypeStruct((pairs * per_row +...  1.73 us
  transfers between devices with their start and end apart: 23, of which 11 were waited for; matrix products, arithmetic and copies ran while one was open for 1% of the time, Pallas kernels for 20%

profile of v2, /device:TPU:0, one launch (start us, length us, event | category | flops | bytes accessed | tf_op | source)
XLA Modules:
  0.0 64.1 jit_solution(16455737010575382596)
XLA Ops:
  0.6 0.7 %multiply_subtract_fusion = (s32[8]{0:T(128)S(1)}, s32[8]{0:T(128)S(1)}) fusion(s32[8]{0:T(128)} %param.8), kind=kLoop, calls=%fused_computation.38 | loop fusion | flops 136 | bytes 96 | tf_op jit(solution)/shard_map/sub | solution.py:302
  1.3 0.2 convert_reduce_fusion
  1.5 0.7 %broadcast_subtract_fusion.first_ref = s32[8]{0:T(128)S(1)} fusion(s32[8]{0:T(128)} %param.7, s32[]{:T(128)S(6)} %mul.22), kind=kLoop, calls=%fused_computation.40 | loop fusion | flops 8 | bytes 68 | tf_op jit(solution)/shard_map/sub | solution.py:300
  2.2 0.1 select_reduce_fusion
  2.3 0.1 fusion.10
  2.4 5.1 %collective-permute-start.3 = (s32[2]{0:T(128)S(1)}, s32[2]{0:T(128)S(1)}, u32[]{:S(2)}, u32[]{:S(2)}) collective-permute-start(s32[2]{0:T(128)S(1)} %get-tuple-element.50), channel_id=1, source_target_pairs={{0,12},{4,0},{8,4},{12,8},{1,13},{5,1},{9,5},{13,9},{2,14},{6,2},{... | collective-permute-start | bytes 32 | tf_op jit(solution)/shard_map/ppermute | solution.py:31
  7.4 0.0 collective-permute-start.2
  7.4 1.0 %collective-permute-start.1 = (s32[2]{0:T(128)S(1)}, s32[2]{0:T(128)S(1)}, u32[]{:S(2)}, u32[]{:S(2)}) collective-permute-start(s32[2]{0:T(128)S(1)} %get-tuple-element.52), channel_id=1, source_target_pairs={{0,4},{4,8},{8,12},{12,0},{1,5},{5,9},{9,13},{13,1},{2,6},{6,10},{... | collective-permute-start | bytes 32 | tf_op jit(solution)/shard_map/ppermute | solution.py:31
  8.4 0.7 %copy-done = s32[16,512]{1,0:T(8,128)S(1)} copy-done((s32[16,512]{1,0:T(8,128)S(1)}, s32[16,512]{1,0:T(8,128)}, u32[]{:S(2)}) %copy-start) | copy-done | bytes 32792
  9.2 1.7 %shard_map.68 = (bf16[272,512]{1,0:T(8,128)(2,1)S(1)}, bf16[272,512]{1,0:T(8,128)(2,1)S(1)}) custom-call(s32[8]{0:T(128)S(1)} %broadcast_subtract_fusion.first_ref, s32[2]{0:T(128)S(1)} %fusion.4.start_ref, bf16[16,128,512]{2,1,0:T(8,128)(2,1)} %readings_ref.3, s32[16,512]{1,0:T(8,128)S(1)} %copy-done), custom_call_target="tpu_custom_call" | custom-call | flops 1610000000 | bytes 1024 | tf_op jit(solution)/shard_map/pallas_call | solution.py:100
  10.9 1.6 %collective-permute-start = (bf16[272,512]{1,0:T(8,128)(2,1)S(1)}, bf16[272,512]{1,0:T(8,128)(2,1)S(1)}, u32[]{:S(2)}, u32[]{:S(2)}) collective-permute-start(bf16[272,512]{1,0:T(8,128)(2,1)S(1)} %get-tuple-element.22), channel_id=1, source_target_pairs={{0,2},{2,0},{1,3},{3,1},{4,6},{6,4},{5,7},{7,5},{8,10},{10,8},{9,1... | collective-permute-start | bytes 835592 | tf_op jit(solution)/shard_map/ppermute | solution.py:31
  12.5 0.0 collective-permute-done.3
  12.5 0.0 collective-permute-done.2
  12.5 0.2 collective-permute-done.1
  12.7 0.1 pad_add_fusion.1.index_ref
  12.9 1.8 %shard_map.69 = (bf16[136,512]{1,0:T(8,128)(2,1)S(1)}, bf16[136,512]{1,0:T(8,128)(2,1)S(1)}, bf16[136,512]{1,0:T(8,128)(2,1)S(1)}, bf16[136,512]{1,0:T(8,128)(2,1)S(1)}, bf16[136,512]{1,0:T(8,128)(2,1)S(1)}) custom-call(s32[5]{0:T(128)S(1)} %pad_add_fusion.1.index_ref, bf16[16,128,512]{2,1,0:T(8,128)(2,1)} %readings_ref.3, s32[16,512]{1,0:T(8,128)S(1)} %copy-done.1), custom_call_target="tpu_custom_call" | custom-call | flops 1150000000 | bytes 1024 | tf_op jit(solution)/shard_map/pallas_call | solution.py:60
  14.6 1.6 %collective-permute-start.16 = (bf16[136,512]{1,0:T(8,128)(2,1)S(1)}, bf16[136,512]{1,0:T(8,128)(2,1)S(1)}, u32[]{:S(2)}, u32[]{:S(2)}) collective-permute-start(bf16[136,512]{1,0:T(8,128)(2,1)S(1)} %get-tuple-element.26.rest_2_), channel_id=1, source_target_pairs={{0,2},{2,0},{1,3},{3,1},{4,6},{6,4},{5,7},{7,5},{8,10},{10,8},{9,1... | collective-permute-start | bytes 417800 | tf_op jit(solution)/shard_map/ppermute | solution.py:31
  16.2 1.6 %collective-permute-start.12 = (bf16[136,512]{1,0:T(8,128)(2,1)S(1)}, bf16[136,512]{1,0:T(8,128)(2,1)S(1)}, u32[]{:S(2)}, u32[]{:S(2)}) collective-permute-start(bf16[136,512]{1,0:T(8,128)(2,1)S(1)} %get-tuple-element.25), channel_id=1, source_target_pairs={{0,12},{4,0},{8,4},{12,8},{1,13},{5,1},{9,5},{13,9},{2,14},{6,2},{... | collective-permute-start | bytes 417800 | tf_op jit(solution)/shard_map/ppermute | solution.py:31
  17.8 0.1 fusion.9
  17.8 1.1 %collective-permute-start.8 = (bf16[136,512]{1,0:T(8,128)(2,1)S(1)}, bf16[136,512]{1,0:T(8,128)(2,1)S(1)}, u32[]{:S(2)}, u32[]{:S(2)}) collective-permute-start(bf16[136,512]{1,0:T(8,128)(2,1)S(1)} %get-tuple-element.24), channel_id=1, source_target_pairs={{0,8},{4,12},{8,0},{12,4},{1,9},{5,13},{9,1},{13,5},{2,10},{6,14},... | collective-permute-start | bytes 417800 | tf_op jit(solution)/shard_map/ppermute | solution.py:31
  19.0 0.4 collective-permute-start.4
  19.4 2.1 %collective-permute-done.16.rest_3_ = bf16[136,512]{1,0:T(8,128)(2,1)S(1)} collective-permute-done((bf16[136,512]{1,0:T(8,128)(2,1)S(1)}, bf16[136,512]{1,0:T(8,128)(2,1)S(1)}, u32[]{:S(2)}, u32[]{:S(2)}) %collective-permute-start.16) | collective-permute-done | bytes 139296 | tf_op jit(solution)/shard_map/ppermute | solution.py:31
  21.5 0.0 collective-permute-start.17
  21.5 0.4 collective-permute-done.12.rest_2_
  21.9 1.5 %collective-permute-start.13 = (bf16[136,512]{1,0:T(8,128)(2,1)S(1)}, bf16[136,512]{1,0:T(8,128)(2,1)S(1)}, u32[]{:S(2)}, u32[]{:S(2)}) collective-permute-start(bf16[136,512]{1,0:T(8,128)(2,1)S(1)} %collective-permute-done.12.rest_2_), channel_id=1, source_target_pairs={{0,2},{2,0},{1,3},{3,1},{4,6},{6,4},{5,7},{7,5},{8,10},{10,8},{9,1... | collective-permute-start | bytes 417800 | tf_op jit(solution)/shard_map/ppermute | solution.py:31
  23.4 0.1 pad_add_fusion.place_ref
  23.5 6.3 %collective-permute-done.8.rest_2_ = bf16[136,512]{1,0:T(8,128)(2,1)S(1)} collective-permute-done((bf16[136,512]{1,0:T(8,128)(2,1)S(1)}, bf16[136,512]{1,0:T(8,128)(2,1)S(1)}, u32[]{:S(2)}, u32[]{:S(2)}) %collective-permute-start.8) | collective-permute-done | bytes 139296 | tf_op jit(solution)/shard_map/ppermute | solution.py:31
  29.8 0.0 collective-permute-start.14
  29.8 0.0 collective-permute-done.4.rest_2_
  29.8 1.5 %collective-permute-start.9 = (bf16[136,512]{1,0:T(8,128)(2,1)S(1)}, bf16[136,512]{1,0:T(8,128)(2,1)S(1)}, u32[]{:S(2)}, u32[]{:S(2)}) collective-permute-start(bf16[136,512]{1,0:T(8,128)(2,1)S(1)} %collective-permute-done.8.rest_2_), channel_id=1, source_target_pairs={{0,2},{2,0},{1,3},{3,1},{4,6},{6,4},{5,7},{7,5},{8,10},{10,8},{9,1... | collective-permute-start | bytes 417800 | tf_op jit(solution)/shard_map/ppermute | solution.py:31
  31.3 0.0 collective-permute-done.rest_1_
  31.3 0.2 collective-permute-start.10
  31.6 0.0 collective-permute-done.17.rest_5_
  31.6 0.5 collective-permute-start.5
  32.1 0.0 collective-permute-done.13.rest_3_
  32.1 0.0 collective-permute-start.15
  32.1 3.0 %shard_map.70 = (bf16[8,25,32,128]{3,2,1,0:T(8,128)(2,1)}, f32[2,32,128]{2,1,0:T(8,128)S(1)}, f32[25,2,128]{2,1,0:T(2,128)S(1)}) custom-call(s32[2]{0:T(128)S(1)} %get-tuple-element.45.pair_ref, s32[3]{0:T(128)S(1)} %pad_add_fusion.place_ref, bf16[272,512]{1,0:T(8,128)(2,1)S(1)} %get-tuple-element.21.rest_0_, ...), custom_call_target="tpu_custom_call" | custom-call | flops 3449999872 | bytes 1024 | tf_op jit(solution)/shard_map/pallas_call | solution.py:230
  35.1 0.0 collective-permute-done.14.rest_4_
  35.1 0.6 collective-permute-start.6
  35.7 0.6 collective-permute-done.9.rest_3_
  36.3 0.0 collective-permute-start.11
  36.3 2.6 %collective-permute-done.5.rest_3_ = bf16[136,512]{1,0:T(8,128)(2,1)S(1)} collective-permute-done((bf16[136,512]{1,0:T(8,128)(2,1)S(1)}, bf16[136,512]{1,0:T(8,128)(2,1)S(1)}, u32[]{:S(2)}, u32[]{:S(2)}) %collective-permute-start.5) | collective-permute-done | bytes 139296 | tf_op jit(solution)/shard_map/ppermute | solution.py:31
  38.9 0.0 collective-permute-start.7
  38.9 0.0 collective-permute-done.15.rest_5_
  38.9 3.0 %shard_map.71 = (bf16[8,25,32,128]{3,2,1,0:T(8,128)(2,1)}, f32[2,32,128]{2,1,0:T(8,128)S(1)}, f32[25,2,128]{2,1,0:T(2,128)S(1)}) custom-call(s32[2]{0:T(128)S(1)} %get-tuple-element.46.pair_ref, s32[3]{0:T(128)S(1)} %pad_add_fusion.place_ref, bf16[272,512]{1,0:T(8,128)(2,1)S(1)} %get-tuple-element.21.rest_0_, ...), custom_call_target="tpu_custom_call", output_to_operand_aliasing={{0}: (8, {})} | custom-call | flops 3449999872 | bytes 1024 | tf_op jit(solution)/shard_map/pallas_call | solution.py:230
  41.9 0.0 collective-permute-done.10.rest_4_
  42.0 0.0 collective-permute-done.11.rest_5_
  42.0 3.0 %shard_map.72 = (bf16[8,25,32,128]{3,2,1,0:T(8,128)(2,1)}, f32[2,32,128]{2,1,0:T(8,128)S(1)}, f32[25,2,128]{2,1,0:T(2,128)S(1)}) custom-call(s32[2]{0:T(128)S(1)} %get-tuple-element.47.pair_ref, s32[3]{0:T(128)S(1)} %pad_add_fusion.place_ref, bf16[272,512]{1,0:T(8,128)(2,1)S(1)} %get-tuple-element.21.rest_0_, ...), custom_call_target="tpu_custom_call", output_to_operand_aliasing={{0}: (8, {})} | custom-call | flops 3449999872 | bytes 1024 | tf_op jit(solution)/shard_map/pallas_call | solution.py:230
  45.0 0.0 collective-permute-done.6.rest_4_
  45.0 0.0 collective-permute-done.7.rest_5_
  45.0 3.0 %shard_map.73 = (bf16[8,25,32,128]{3,2,1,0:T(8,128)(2,1)}, f32[2,32,128]{2,1,0:T(8,128)S(1)}, f32[25,2,128]{2,1,0:T(2,128)S(1)}) custom-call(s32[2]{0:T(128)S(1)} %get-tuple-element.48.pair_ref, s32[3]{0:T(128)S(1)} %pad_add_fusion.place_ref, bf16[272,512]{1,0:T(8,128)(2,1)S(1)} %get-tuple-element.21.rest_0_, ...), custom_call_target="tpu_custom_call", output_to_operand_aliasing={{0}: (8, {})} | custom-call | flops 3449999872 | bytes 1024 | tf_op jit(solution)/shard_map/pallas_call | solution.py:230
  48.1 0.3 collective-permute-start.20
  48.3 2.2 %collective-permute-start.19 = (f32[25,2,128]{2,1,0:T(2,128)S(1)}, f32[25,2,128]{2,1,0:T(2,128)S(1)}, u32[]{:S(2)}, u32[]{:S(2)}) collective-permute-start(f32[25,2,128]{2,1,0:T(2,128)S(1)} %get-tuple-element.38), channel_id=1, source_target_pairs={{0,8},{4,12},{8,0},{12,4},{1,9},{5,13},{9,1},{13,5},{2,10},{6,14},... | collective-permute-start | bytes 76808 | tf_op jit(solution)/shard_map/ppermute | solution.py:31
  50.5 0.2 collective-permute-start.18
  50.7 0.1 pad_add_fusion.2.served_ref
  50.8 1.2 %collective-permute-done.20.rest_7_ = f32[25,2,128]{2,1,0:T(2,128)S(1)} collective-permute-done((f32[25,2,128]{2,1,0:T(2,128)S(1)}, f32[25,2,128]{2,1,0:T(2,128)S(1)}, u32[]{:S(2)}, u32[]{:S(2)}) %collective-permute-start.20) | collective-permute-done | bytes 25632 | tf_op jit(solution)/shard_map/ppermute | solution.py:31
  52.0 1.1 %collective-permute-done.19.rest_6_ = f32[25,2,128]{2,1,0:T(2,128)S(1)} collective-permute-done((f32[25,2,128]{2,1,0:T(2,128)S(1)}, f32[25,2,128]{2,1,0:T(2,128)S(1)}, u32[]{:S(2)}, u32[]{:S(2)}) %collective-permute-start.19) | collective-permute-done | bytes 25632 | tf_op jit(solution)/shard_map/ppermute | solution.py:31
  53.1 3.0 %collective-permute-done.18.rest_5_ = f32[25,2,128]{2,1,0:T(2,128)S(1)} collective-permute-done((f32[25,2,128]{2,1,0:T(2,128)S(1)}, f32[25,2,128]{2,1,0:T(2,128)S(1)}, u32[]{:S(2)}, u32[]{:S(2)}) %collective-permute-start.18) | collective-permute-done | bytes 25632 | tf_op jit(solution)/shard_map/ppermute | solution.py:31
  56.1 0.8 %shard_map.74 = bf16[25,16,128]{2,1,0:T(8,128)(2,1)S(1)} custom-call(s32[8]{0:T(128)S(1)} %get-tuple-element.40.first_ref, s32[8]{0:T(128)S(1)} %pad_add_fusion.2.served_ref, f32[2,32,128]{2,1,0:T(8,128)S(1)} %get-tuple-element.32.rest_0_, f32[2,32,128]{2,1,0:T(8,128)S(1)} %get-tuple-element.33.rest_1_, f32[2,32,128]{2,1,0:T(8,128)S(1)} %get-tuple-element.34.rest_2_, ...), custom_call_target="tpu_custom_call" | custom-call | flops 920000000 | bytes 1024 | tf_op jit(solution)/shard_map/pallas_call | solution.py:277
  57.0 0.1 collective-permute-start.21
  57.0 1.3 %collective-permute-done.21 = bf16[25,16,128]{2,1,0:T(8,128)(2,1)S(1)} collective-permute-done((bf16[25,16,128]{2,1,0:T(8,128)(2,1)S(1)}, bf16[25,16,128]{2,1,0:T(8,128)(2,1)S(1)}, u32[]{:S(2)}, u32[]{:S(2)}) %collective-permute-start.21) | collective-permute-done | bytes 102432 | tf_op jit(solution)/shard_map/ppermute | solution.py:31
  58.4 1.7 %collective-permute-start.22 = (bf16[25,16,128]{2,1,0:T(8,128)(2,1)S(1)}, bf16[25,16,128]{2,1,0:T(8,128)(2,1)S(1)}, u32[]{:S(2)}, u32[]{:S(2)}) collective-permute-start(bf16[25,16,128]{2,1,0:T(8,128)(2,1)S(1)} %add_convert_fusion), channel_id=1, source_target_pairs={{0,2},{2,0},{1,3},{3,1},{4,6},{6,4},{5,7},{7,5},{8,10},{10,8},{9,1... | collective-permute-start | bytes 307208 | tf_op jit(solution)/shard_map/ppermute | solution.py:31
  60.0 3.3 %collective-permute-done.22 = bf16[25,16,128]{2,1,0:T(8,128)(2,1)S(1)} collective-permute-done((bf16[25,16,128]{2,1,0:T(8,128)(2,1)S(1)}, bf16[25,16,128]{2,1,0:T(8,128)(2,1)S(1)}, u32[]{:S(2)}, u32[]{:S(2)}) %collective-permute-start.22) | collective-permute-done | bytes 102432 | tf_op jit(solution)/shard_map/ppermute | solution.py:31
  63.4 0.7 %convert_add_fusion = f32[25,16,128]{2,1,0:T(8,128)} fusion(bf16[25,16,128]{2,1,0:T(8,128)(2,1)S(1)} %collective-permute-done.22, bf16[25,16,128]{2,1,0:T(8,128)(2,1)S(1)} %add_convert_fusion), kind=kLoop, calls=%fused_computation | loop fusion | flops 153600 | bytes 409600 | tf_op jit(solution)/shard_map/add | solution.py:365
  (10 shorter events, 0.1 us)
Async XLA Ops:
  2.4 10.1 %collective-permute-start.3 = (s32[2]{0:T(128)S(1)}, s32[2]{0:T(128)S(1)}, u32[]{:S(2)}, u32[]{:S(2)}) collective-permute-start(s32[2]{0:T(128)S(1)} %get-tuple-element.50), channel_id=1, source_target_pairs={{0,12},{4,0},{8,4},{12,8},{1,13},{5,1},{9,5},{13,9},{2,14},{6,2},{... | collective-permute-start | bytes 32 | tf_op jit(solution)/shard_map/ppermute | solution.py:31
  7.4 5.1 %collective-permute-start.2 = (s32[2]{0:T(128)S(1)}, s32[2]{0:T(128)S(1)}, u32[]{:S(2)}, u32[]{:S(2)}) collective-permute-start(s32[2]{0:T(128)S(1)} %get-tuple-element.51), channel_id=1, source_target_pairs={{0,8},{4,12},{8,0},{12,4},{1,9},{5,13},{9,1},{13,5},{2,10},{6,14},... | collective-permute-start | bytes 32 | tf_op jit(solution)/shard_map/ppermute | solution.py:31
  7.4 5.3 %collective-permute-start.1 = (s32[2]{0:T(128)S(1)}, s32[2]{0:T(128)S(1)}, u32[]{:S(2)}, u32[]{:S(2)}) collective-permute-start(s32[2]{0:T(128)S(1)} %get-tuple-element.52), channel_id=1, source_target_pairs={{0,4},{4,8},{8,12},{12,0},{1,5},{5,9},{9,13},{13,1},{2,6},{6,10},{... | collective-permute-start | bytes 32 | tf_op jit(solution)/shard_map/ppermute | solution.py:31
  8.4 0.8 %copy-start = (s32[16,512]{1,0:T(8,128)S(1)}, s32[16,512]{1,0:T(8,128)}, u32[]{:S(2)}) copy-start(s32[16,512]{1,0:T(8,128)} %present_ref.3) | copy-start | bytes 98308
  9.2 3.7 %copy-start.1 = (s32[16,512]{1,0:T(8,128)S(1)}, s32[16,512]{1,0:T(8,128)}, u32[]{:S(2)}) copy-start(s32[16,512]{1,0:T(8,128)} %present_ref.3) | copy-start | bytes 98308
  10.9 20.4 %collective-permute-start = (bf16[272,512]{1,0:T(8,128)(2,1)S(1)}, bf16[272,512]{1,0:T(8,128)(2,1)S(1)}, u32[]{:S(2)}, u32[]{:S(2)}) collective-permute-start(bf16[272,512]{1,0:T(8,128)(2,1)S(1)} %get-tuple-element.22), channel_id=1, source_target_pairs={{0,2},{2,0},{1,3},{3,1},{4,6},{6,4},{5,7},{7,5},{8,10},{10,8},{9,1... | collective-permute-start | bytes 835592 | tf_op jit(solution)/shard_map/ppermute | solution.py:31
  14.6 6.9 %collective-permute-start.16 = (bf16[136,512]{1,0:T(8,128)(2,1)S(1)}, bf16[136,512]{1,0:T(8,128)(2,1)S(1)}, u32[]{:S(2)}, u32[]{:S(2)}) collective-permute-start(bf16[136,512]{1,0:T(8,128)(2,1)S(1)} %get-tuple-element.26.rest_2_), channel_id=1, source_target_pairs={{0,2},{2,0},{1,3},{3,1},{4,6},{6,4},{5,7},{7,5},{8,10},{10,8},{9,1... | collective-permute-start | bytes 417800 | tf_op jit(solution)/shard_map/ppermute | solution.py:31
  16.2 5.7 %collective-permute-start.12 = (bf16[136,512]{1,0:T(8,128)(2,1)S(1)}, bf16[136,512]{1,0:T(8,128)(2,1)S(1)}, u32[]{:S(2)}, u32[]{:S(2)}) collective-permute-start(bf16[136,512]{1,0:T(8,128)(2,1)S(1)} %get-tuple-element.25), channel_id=1, source_target_pairs={{0,12},{4,0},{8,4},{12,8},{1,13},{5,1},{9,5},{13,9},{2,14},{6,2},{... | collective-permute-start | bytes 417800 | tf_op jit(solution)/shard_map/ppermute | solution.py:31
  17.8 12.0 %collective-permute-start.8 = (bf16[136,512]{1,0:T(8,128)(2,1)S(1)}, bf16[136,512]{1,0:T(8,128)(2,1)S(1)}, u32[]{:S(2)}, u32[]{:S(2)}) collective-permute-start(bf16[136,512]{1,0:T(8,128)(2,1)S(1)} %get-tuple-element.24), channel_id=1, source_target_pairs={{0,8},{4,12},{8,0},{12,4},{1,9},{5,13},{9,1},{13,5},{2,10},{6,14},... | collective-permute-start | bytes 417800 | tf_op jit(solution)/shard_map/ppermute | solution.py:31
  19.0 10.9 %collective-permute-start.4 = (bf16[136,512]{1,0:T(8,128)(2,1)S(1)}, bf16[136,512]{1,0:T(8,128)(2,1)S(1)}, u32[]{:S(2)}, u32[]{:S(2)}) collective-permute-start(bf16[136,512]{1,0:T(8,128)(2,1)S(1)} %get-tuple-element.23), channel_id=1, source_target_pairs={{0,4},{4,8},{8,12},{12,0},{1,5},{5,9},{9,13},{13,1},{2,6},{6,10},{... | collective-permute-start | bytes 417800 | tf_op jit(solution)/shard_map/ppermute | solution.py:31
  21.5 10.1 %collective-permute-start.17 = (bf16[136,512]{1,0:T(8,128)(2,1)S(1)}, bf16[136,512]{1,0:T(8,128)(2,1)S(1)}, u32[]{:S(2)}, u32[]{:S(2)}) collective-permute-start(bf16[136,512]{1,0:T(8,128)(2,1)S(1)} %collective-permute-done.16.rest_3_), channel_id=1, source_target_pairs={{0,1},{1,0},{2,3},{3,2},{4,5},{5,4},{6,7},{7,6},{8,9},{9,8},{10,11... | collective-permute-start | bytes 417800 | tf_op jit(solution)/shard_map/ppermute | solution.py:31
  21.9 10.2 %collective-permute-start.13 = (bf16[136,512]{1,0:T(8,128)(2,1)S(1)}, bf16[136,512]{1,0:T(8,128)(2,1)S(1)}, u32[]{:S(2)}, u32[]{:S(2)}) collective-permute-start(bf16[136,512]{1,0:T(8,128)(2,1)S(1)} %collective-permute-done.12.rest_2_), channel_id=1, source_target_pairs={{0,2},{2,0},{1,3},{3,1},{4,6},{6,4},{5,7},{7,5},{8,10},{10,8},{9,1... | collective-permute-start | bytes 417800 | tf_op jit(solution)/shard_map/ppermute | solution.py:31
  29.8 5.3 %collective-permute-start.14 = (bf16[136,512]{1,0:T(8,128)(2,1)S(1)}, bf16[136,512]{1,0:T(8,128)(2,1)S(1)}, u32[]{:S(2)}, u32[]{:S(2)}) collective-permute-start(bf16[136,512]{1,0:T(8,128)(2,1)S(1)} %collective-permute-done.12.rest_2_), channel_id=1, source_target_pairs={{0,1},{1,0},{2,3},{3,2},{4,5},{5,4},{6,7},{7,6},{8,9},{9,8},{10,11... | collective-permute-start | bytes 417800 | tf_op jit(solution)/shard_map/ppermute | solution.py:31
  29.8 6.5 %collective-permute-start.9 = (bf16[136,512]{1,0:T(8,128)(2,1)S(1)}, bf16[136,512]{1,0:T(8,128)(2,1)S(1)}, u32[]{:S(2)}, u32[]{:S(2)}) collective-permute-start(bf16[136,512]{1,0:T(8,128)(2,1)S(1)} %collective-permute-done.8.rest_2_), channel_id=1, source_target_pairs={{0,2},{2,0},{1,3},{3,1},{4,6},{6,4},{5,7},{7,5},{8,10},{10,8},{9,1... | collective-permute-start | bytes 417800 | tf_op jit(solution)/shard_map/ppermute | solution.py:31
  31.3 10.6 %collective-permute-start.10 = (bf16[136,512]{1,0:T(8,128)(2,1)S(1)}, bf16[136,512]{1,0:T(8,128)(2,1)S(1)}, u32[]{:S(2)}, u32[]{:S(2)}) collective-permute-start(bf16[136,512]{1,0:T(8,128)(2,1)S(1)} %collective-permute-done.8.rest_2_), channel_id=1, source_target_pairs={{0,1},{1,0},{2,3},{3,2},{4,5},{5,4},{6,7},{7,6},{8,9},{9,8},{10,11... | collective-permute-start | bytes 417800 | tf_op jit(solution)/shard_map/ppermute | solution.py:31
  31.6 7.3 %collective-permute-start.5 = (bf16[136,512]{1,0:T(8,128)(2,1)S(1)}, bf16[136,512]{1,0:T(8,128)(2,1)S(1)}, u32[]{:S(2)}, u32[]{:S(2)}) collective-permute-start(bf16[136,512]{1,0:T(8,128)(2,1)S(1)} %collective-permute-done.4.rest_2_), channel_id=1, source_target_pairs={{0,2},{2,0},{1,3},{3,1},{4,6},{6,4},{5,7},{7,5},{8,10},{10,8},{9,1... | collective-permute-start | bytes 417800 | tf_op jit(solution)/shard_map/ppermute | solution.py:31
  32.1 6.8 %collective-permute-start.15 = (bf16[136,512]{1,0:T(8,128)(2,1)S(1)}, bf16[136,512]{1,0:T(8,128)(2,1)S(1)}, u32[]{:S(2)}, u32[]{:S(2)}) collective-permute-start(bf16[136,512]{1,0:T(8,128)(2,1)S(1)} %collective-permute-done.13.rest_3_), channel_id=1, source_target_pairs={{0,1},{1,0},{2,3},{3,2},{4,5},{5,4},{6,7},{7,6},{8,9},{9,8},{10,11... | collective-permute-start | bytes 417800 | tf_op jit(solution)/shard_map/ppermute | solution.py:31
  35.1 9.9 %collective-permute-start.6 = (bf16[136,512]{1,0:T(8,128)(2,1)S(1)}, bf16[136,512]{1,0:T(8,128)(2,1)S(1)}, u32[]{:S(2)}, u32[]{:S(2)}) collective-permute-start(bf16[136,512]{1,0:T(8,128)(2,1)S(1)} %collective-permute-done.4.rest_2_), channel_id=1, source_target_pairs={{0,1},{1,0},{2,3},{3,2},{4,5},{5,4},{6,7},{7,6},{8,9},{9,8},{10,11... | collective-permute-start | bytes 417800 | tf_op jit(solution)/shard_map/ppermute | solution.py:31
  36.3 5.7 %collective-permute-start.11 = (bf16[136,512]{1,0:T(8,128)(2,1)S(1)}, bf16[136,512]{1,0:T(8,128)(2,1)S(1)}, u32[]{:S(2)}, u32[]{:S(2)}) collective-permute-start(bf16[136,512]{1,0:T(8,128)(2,1)S(1)} %collective-permute-done.9.rest_3_), channel_id=1, source_target_pairs={{0,1},{1,0},{2,3},{3,2},{4,5},{5,4},{6,7},{7,6},{8,9},{9,8},{10,11... | collective-permute-start | bytes 417800 | tf_op jit(solution)/shard_map/ppermute | solution.py:31
  38.9 6.1 %collective-permute-start.7 = (bf16[136,512]{1,0:T(8,128)(2,1)S(1)}, bf16[136,512]{1,0:T(8,128)(2,1)S(1)}, u32[]{:S(2)}, u32[]{:S(2)}) collective-permute-start(bf16[136,512]{1,0:T(8,128)(2,1)S(1)} %collective-permute-done.5.rest_3_), channel_id=1, source_target_pairs={{0,1},{1,0},{2,3},{3,2},{4,5},{5,4},{6,7},{7,6},{8,9},{9,8},{10,11... | collective-permute-start | bytes 417800 | tf_op jit(solution)/shard_map/ppermute | solution.py:31
  48.1 3.9 %collective-permute-start.20 = (f32[25,2,128]{2,1,0:T(2,128)S(1)}, f32[25,2,128]{2,1,0:T(2,128)S(1)}, u32[]{:S(2)}, u32[]{:S(2)}) collective-permute-start(f32[25,2,128]{2,1,0:T(2,128)S(1)} %get-tuple-element.39), channel_id=1, source_target_pairs={{0,12},{4,0},{8,4},{12,8},{1,13},{5,1},{9,5},{13,9},{2,14},{6,2},{... | collective-permute-start | bytes 76808 | tf_op jit(solution)/shard_map/ppermute | solution.py:31
  48.3 4.8 %collective-permute-start.19 = (f32[25,2,128]{2,1,0:T(2,128)S(1)}, f32[25,2,128]{2,1,0:T(2,128)S(1)}, u32[]{:S(2)}, u32[]{:S(2)}) collective-permute-start(f32[25,2,128]{2,1,0:T(2,128)S(1)} %get-tuple-element.38), channel_id=1, source_target_pairs={{0,8},{4,12},{8,0},{12,4},{1,9},{5,13},{9,1},{13,5},{2,10},{6,14},... | collective-permute-start | bytes 76808 | tf_op jit(solution)/shard_map/ppermute | solution.py:31
  50.5 5.6 %collective-permute-start.18 = (f32[25,2,128]{2,1,0:T(2,128)S(1)}, f32[25,2,128]{2,1,0:T(2,128)S(1)}, u32[]{:S(2)}, u32[]{:S(2)}) collective-permute-start(f32[25,2,128]{2,1,0:T(2,128)S(1)} %get-tuple-element.37), channel_id=1, source_target_pairs={{0,4},{4,8},{8,12},{12,0},{1,5},{5,9},{9,13},{13,1},{2,6},{6,10},{... | collective-permute-start | bytes 76808 | tf_op jit(solution)/shard_map/ppermute | solution.py:31
  57.0 1.4 %collective-permute-start.21 = (bf16[25,16,128]{2,1,0:T(8,128)(2,1)S(1)}, bf16[25,16,128]{2,1,0:T(8,128)(2,1)S(1)}, u32[]{:S(2)}, u32[]{:S(2)}) collective-permute-start(bf16[25,16,128]{2,1,0:T(8,128)(2,1)S(1)} %shard_map.74), channel_id=1, source_target_pairs={{0,1},{1,0},{2,3},{3,2},{4,5},{5,4},{6,7},{7,6},{8,9},{9,8},{10,11... | collective-permute-start | bytes 307208 | tf_op jit(solution)/shard_map/ppermute | solution.py:31
  58.4 5.0 %collective-permute-start.22 = (bf16[25,16,128]{2,1,0:T(8,128)(2,1)S(1)}, bf16[25,16,128]{2,1,0:T(8,128)(2,1)S(1)}, u32[]{:S(2)}, u32[]{:S(2)}) collective-permute-start(bf16[25,16,128]{2,1,0:T(8,128)(2,1)S(1)} %add_convert_fusion), channel_id=1, source_target_pairs={{0,2},{2,0},{1,3},{3,1},{4,6},{6,4},{5,7},{7,5},{8,10},{10,8},{9,1... | collective-permute-start | bytes 307208 | tf_op jit(solution)/shard_map/ppermute | solution.py:31

commit v3 on v2

--- a/solution.py
+++ b/solution.py
@@ -40,8 +40,10 @@
     _, rows, steps = readings.shape
     count = indices.shape[0]
 
-    def kernel(index_ref, readings_ref, present_ref, *rest):
-        outs, sems = rest[:count], rest[count]
+    def kernel(index_ref, readings_ref, present_hbm, *rest):
+        outs, sems, present_ref, present_sem = rest[:count], *rest[count:]
+        masks = pltpu.make_async_copy(present_hbm, present_ref, present_sem)
+        masks.start()
         copies = [
             pltpu.make_async_copy(
                 readings_ref.at[index_ref[i]], outs[i].at[pl.ds(0, rows)], sems.at[i]
@@ -50,6 +52,7 @@
         ]
         for copy in copies:
             copy.start()
+        masks.wait()
         for i in range(count):
             outs[i][rows : rows + MASK_ROWS, :] = mask_rows(
                 present_ref, index_ref[i], MASK_ROWS
@@ -60,9 +63,13 @@
     return pl.pallas_call(
         kernel,
         out_shape=[jax.ShapeDtypeStruct((rows + MASK_ROWS, steps), jnp.bfloat16)] * count,
-        in_specs=[SMEM, ANY, VMEM],
+        in_specs=[SMEM, ANY, ANY],
         out_specs=[VMEM] * count,
-        scratch_shapes=[pltpu.SemaphoreType.DMA((count,))],
+        scratch_shapes=[
+            pltpu.SemaphoreType.DMA((count,)),
+            pltpu.VMEM(present.shape, present.dtype),
+            pltpu.SemaphoreType.DMA,
+        ],
         compiler_params=WIDE,
         cost_estimate=cost(1.0),
     )(indices, readings, present)
@@ -73,8 +80,10 @@
     pairs = first_index.shape[0]
     count = row_starts.shape[0]
 
-    def kernel(first_ref, start_ref, readings_ref, present_ref, *rest):
-        outs, sems = rest[:count], rest[count]
+    def kernel(first_ref, start_ref, readings_ref, present_hbm, *rest):
+        outs, sems, present_ref, present_sem = rest[:count], *rest[count:]
+        masks_copy = pltpu.make_async_copy(present_hbm, present_ref, present_sem)
+        masks_copy.start()
         copies = []
         for k in range(count):
             start = pl.multiple_of(start_ref[k], per_row)
@@ -88,6 +97,7 @@
                 )
         for copy in copies:
             copy.start()
+        masks_copy.wait()
         rows = lax.broadcasted_iota(jnp.int32, (PAD, steps), 0)
         masks = jnp.zeros((PAD, steps), jnp.float32)
         for p in range(pairs):
@@ -100,9 +110,13 @@
     return pl.pallas_call(
         kernel,
         out_shape=[jax.ShapeDtypeStruct((pairs * per_row + PAD, steps), jnp.bfloat16)] * count,
-        in_specs=[SMEM, SMEM, ANY, VMEM],
+        in_specs=[SMEM, SMEM, ANY, ANY],
         out_specs=[VMEM] * count,
-        scratch_shapes=[pltpu.SemaphoreType.DMA((count, pairs))],
+        scratch_shapes=[
+            pltpu.SemaphoreType.DMA((count, pairs)),
+            pltpu.VMEM(present.shape, present.dtype),
+            pltpu.SemaphoreType.DMA,
+        ],
         compiler_params=WIDE,
         cost_estimate=cost(1.4),
     )(first_index, row_starts, readings, present)
@@ -129,10 +143,10 @@
         first_refs = rest[:windows]
         block_refs = rest[windows : windows + slots * windows]
         rest = rest[windows + slots * windows + (carried is not None) :]
-        cov_ref, row_ref, col_ref, left, right, squares, ready, first_part, sems = rest
-
-        def one(j):
-            pair = pair_ref[j]
+        cov_ref, row_ref, col_ref, left, right, product, squares, ready, first_part, sems = rest
+
+        def prepare(j):
+            pair = jnp.maximum(pair_ref[j], 0)
             base = pl.multiple_of(pair * per_row, per_row)
             which = lax.broadcasted_iota(jnp.int32, (PAD, steps), 0) == pair
             raw, masks = [], []
@@ -146,7 +160,7 @@
                 )
             for k, part in enumerate(centered_windows(raw, masks)):
                 at = pl.multiple_of(place_ref[k] * steps, steps)
-                first_part[:, pl.ds(at, steps)] = part
+                first_part[j, :, pl.ds(at, steps)] = part
             raw, masks = [], []
             for k in range(windows):
                 ref = block_refs[j * windows + k]
@@ -154,42 +168,56 @@
                 masks.append(ref[block_size : block_size + 1, :].astype(jnp.float32))
             for k, part in enumerate(centered_windows(raw, masks)):
                 at = pl.multiple_of(place_ref[k] * steps, steps)
-                right[0:block_size, pl.ds(at, steps)] = part.astype(jnp.bfloat16)
-            whole = right[0:block_size, :].astype(jnp.float32)
+                right[j, 0:block_size, pl.ds(at, steps)] = part.astype(jnp.bfloat16)
+            whole = right[j, 0:block_size, :].astype(jnp.float32)
             lane = lax.broadcasted_iota(jnp.int32, whole.shape, 1)
             moved = pltpu.roll(whole, total_steps - 1, 1)
-            right[block_size : 2 * block_size, :] = jnp.where(
+            right[j, block_size : 2 * block_size, :] = jnp.where(
                 lane < total_steps - 1, moved, 0.0
             ).astype(jnp.bfloat16)
-            whole = first_part[...]
+            whole = first_part[j]
             lane = lax.broadcasted_iota(jnp.int32, whole.shape, 1)
             for m in range(shifts):
                 moved = whole if m == 0 else pltpu.roll(whole, 2 * m, 1)
-                left[m * per_row : (m + 1) * per_row, :] = jnp.where(
+                left[j, m * per_row : (m + 1) * per_row, :] = jnp.where(
                     lane >= 2 * m, moved, 0.0
                 ).astype(jnp.bfloat16)
-            product = lax.dot_general(
-                left[...], right[...], (((1,), (1,)), ((), ())), preferred_element_type=jnp.float32
+
+        def multiply(j):
+            product[j] = lax.dot_general(
+                left[j], right[j], (((1,), (1,)), ((), ())), preferred_element_type=jnp.float32
             )
+
+        def finish(j):
+            def standard(lag):
+                m, odd = lag // 2, lag % 2
+                return product[
+                    j,
+                    m * per_row : (m + 1) * per_row,
+                    odd * block_size : (odd + 1) * block_size,
+                ] * float(scales[lag])
+
             for lag in range(LAGS):
-                m, odd = lag // 2, lag % 2
-                standard = product[
-                    m * per_row : (m + 1) * per_row, odd * block_size : (odd + 1) * block_size
-                ] * float(scales[lag])
-                ready[j, lag] = standard.astype(jnp.bfloat16)
-                square = standard * standard
-                col_ref[lag, j : j + 1, :] = (
-                    jnp.sum(square, axis=0, keepdims=True) * (1.0 / block_size)
-                )
-                squares[lag * per_row : (lag + 1) * per_row, :] = square.astype(jnp.bfloat16)
+                ready[j, lag] = standard(lag).astype(jnp.bfloat16)
+
+            @pl.when(pair_ref[j] >= 0)
+            def _():
+                pltpu.make_async_copy(ready.at[j], cov_ref.at[pair_ref[j]], sems.at[j]).start()
+
+            used = jnp.where(pair_ref[j] >= 0, 1.0 / block_size, 0.0)
+            for lag in range(LAGS):
+                square = standard(lag)
+                square = square * square
+                col_ref[lag, j : j + 1, :] = jnp.sum(square, axis=0, keepdims=True) * used
+                squares[j, lag * per_row : (lag + 1) * per_row, :] = square.astype(jnp.bfloat16)
             ones = jnp.full((8, block_size), 1.0 / block_size, jnp.bfloat16)
             sums = lax.dot_general(
-                ones, squares[...], (((1,), (1,)), ((), ())), preferred_element_type=jnp.float32
+                ones, squares[j], (((1,), (1,)), ((), ())), preferred_element_type=jnp.float32
             )
             start = place_ref[windows]
             lane = lax.broadcasted_iota(jnp.int32, (8, 128), 1)
             level = lax.broadcasted_iota(jnp.int32, (8, 128), 0)
-            mine = (lane >= start) & (lane < start + per_row)
+            mine = (lane >= start) & (lane < start + per_row) & (pair_ref[j] >= 0)
             tiles = [jnp.zeros((8, 128), jnp.float32) for _ in range(LAG_ROWS // 8)]
             for lag in range(LAGS):
                 q, r = lag // quarter, lag % quarter
@@ -198,21 +226,13 @@
                 tiles[lag // 8] = jnp.where(mine & (level == lag % 8), piece, tiles[lag // 8])
             for i, tile in enumerate(tiles):
                 row_ref[j, i * 8 : (i + 1) * 8, :] = tile
-            return None
 
         for j in range(slots):
-            used = pair_ref[j] >= 0
-
-            @pl.when(used)
-            def _():
-                one(j)
-                pltpu.make_async_copy(ready.at[j], cov_ref.at[pair_ref[j]], sems.at[j]).start()
-
-            @pl.when(jnp.logical_not(used))
-            def _():
-                row_ref[j] = jnp.zeros(row_ref.shape[1:], jnp.float32)
-                col_ref[:, j : j + 1, :] = jnp.zeros((LAGS, 1, block_size), jnp.float32)
-
+            prepare(j)
+        for j in range(slots):
+            multiply(j)
+        for j in range(slots):
+            finish(j)
         for j in range(slots):
 
             @pl.when(pair_ref[j] >= 0)
@@ -237,11 +257,12 @@
         in_specs=specs,
         out_specs=[ANY, VMEM, VMEM],
         scratch_shapes=[
-            pltpu.VMEM((shifts * per_row, total_steps), jnp.bfloat16),
-            pltpu.VMEM((2 * block_size, total_steps), jnp.bfloat16),
-            pltpu.VMEM((wide, block_size), jnp.bfloat16),
+            pltpu.VMEM((slots, shifts * per_row, total_steps), jnp.bfloat16),
+            pltpu.VMEM((slots, 2 * block_size, total_steps), jnp.bfloat16),
+            pltpu.VMEM((slots, shifts * per_row, 2 * block_size), jnp.float32),
+            pltpu.VMEM((slots, wide, block_size), jnp.bfloat16),
             pltpu.VMEM((slots, LAGS, per_row, block_size), jnp.bfloat16),
-            pltpu.VMEM((per_row, total_steps), jnp.float32),
+            pltpu.VMEM((slots, per_row, total_steps), jnp.float32),
             pltpu.SemaphoreType.DMA((slots,)),
         ],
         input_output_aliases=aliases,
@@ -328,12 +349,17 @@
     packed = pack_blocks(
         readings, present, jnp.concatenate([requests[:CAP]] + [s[:1] for s in served[1:]])
     )
-    here, away = packed[:CAP], packed[CAP:]
+    here, away = list(packed[:CAP]), list(packed[CAP:])
     cov = None
     rows, cols = [], []
     for i, d in enumerate(groups):
+        last = i == len(groups) - 1
         own = here[0] if i == 0 else rotated(away[i - 1], "sensor", -d)
+        if last:
+            own, rows[0] = lax.optimization_barrier((own, rows[0]))
         own_windows = [own] + [rotated(own, "tm", k) for k in range(1, tm_count)]
+        if last:
+            own_windows[-1], rows[-1] = lax.optimization_barrier((own_windows[-1], rows[-1]))
         blocks = [own_windows]
         for j in range(1, lag_count):
             blocks.append(

time: 64.4 us -> 57.8 us (0.90)
  waiting for transfers between devices: 22.2 us -> 9.85 us
  starting transfers between devices: 21 us -> 28.6 us
  Pallas kernels: 16.4 us -> 14.6 us
    ppermute x23, waiting for transfers between devices: 22.2 us -> 9.85 us  [rotated(): lax.ppermute(block, axis, [(i, (i + distance) % size) for i in range(size)])]
    ppermute x23, starting transfers between devices: 21 us -> 28.6 us  [rotated(): lax.ppermute(block, axis, [(i, (i + distance) % size) for i in range(size)])]
    pallas_call x4, Pallas kernels: 12.1 us -> 10.2 us  [covariances(): pl.pallas_call(kernel, out_shape=[jax.ShapeDtypeStruct((pairs, LAGS, per_...]
  transfers between devices with their start and end apart: 23 -> 23, of which waited for: 11 -> 7; matrix products, arithmetic and copies ran while one was open for 1% -> 1% of each run, Pallas kernels for 20% -> 24%
where the time goes in v3:
time: 57.8 us; the launch traced here: 57.4 us
  starting transfers between devices  28.6 us (49%)
  Pallas kernels  14.6 us (25%)
  waiting for transfers between devices  9.85 us (17%)
  other arithmetic  2.7 us (5%)
  local copies, waits for them, and re-layouts  0.9 us (2%)
  between operations  0.77 us (1%)
    ppermute x23, starting transfers between devices, rotated(): lax.ppermute(block, axis, [(i, (i + distance) % size) for i in range(size)])  28.6 us
    pallas_call x4, Pallas kernels, covariances(): pl.pallas_call(kernel, out_shape=[jax.ShapeDtypeStruct((pairs, LAGS, per_...  10.2 us
    ppermute x23, waiting for transfers between devices, rotated(): lax.ppermute(block, axis, [(i, (i + distance) % size) for i in range(size)])  9.85 us
    pallas_call x1, Pallas kernels, pack_blocks(): pl.pallas_call(kernel, out_shape=[jax.ShapeDtypeStruct((rows + MASK_ROWS,...  1.8 us
    pallas_call x1, Pallas kernels, pack_first(): pl.pallas_call(kernel, out_shape=[jax.ShapeDtypeStruct((pairs * per_row +...  1.74 us
  transfers between devices with their start and end apart: 23, of which 7 were waited for; matrix products, arithmetic and copies ran while one was open for 1% of the time, Pallas kernels for 24%

profile of v3, /device:TPU:0, one launch (start us, length us, event | category | flops | bytes accessed | tf_op | source)
XLA Modules:
  0.0 57.4 jit_solution(2862023920495957857)
XLA Ops:
  0.6 0.7 %multiply_subtract_fusion = (s32[8]{0:T(128)S(1)}, s32[8]{0:T(128)S(1)}) fusion(s32[8]{0:T(128)} %param.8), kind=kLoop, calls=%fused_computation.38 | loop fusion | flops 136 | bytes 96 | tf_op jit(solution)/shard_map/sub | solution.py:323
  1.3 0.2 convert_reduce_fusion
  1.5 0.7 %broadcast_subtract_fusion.first_ref = s32[8]{0:T(128)S(1)} fusion(s32[8]{0:T(128)} %param.7, s32[]{:T(128)S(6)} %mul.22), kind=kLoop, calls=%fused_computation.40 | loop fusion | flops 8 | bytes 68 | tf_op jit(solution)/shard_map/sub | solution.py:321
  2.2 0.1 select_reduce_fusion
  2.3 0.1 fusion.10
  2.4 5.1 %collective-permute-start.3 = (s32[2]{0:T(128)S(1)}, s32[2]{0:T(128)S(1)}, u32[]{:S(2)}, u32[]{:S(2)}) collective-permute-start(s32[2]{0:T(128)S(1)} %get-tuple-element.58), channel_id=1, source_target_pairs={{0,12},{4,0},{8,4},{12,8},{1,13},{5,1},{9,5},{13,9},{2,14},{6,2},{... | collective-permute-start | bytes 32 | tf_op jit(solution)/shard_map/ppermute | solution.py:31
  7.4 0.0 collective-permute-start.2
  7.4 1.0 %collective-permute-start.1 = (s32[2]{0:T(128)S(1)}, s32[2]{0:T(128)S(1)}, u32[]{:S(2)}, u32[]{:S(2)}) collective-permute-start(s32[2]{0:T(128)S(1)} %get-tuple-element.60), channel_id=1, source_target_pairs={{0,4},{4,8},{8,12},{12,0},{1,5},{5,9},{9,13},{13,1},{2,6},{6,10},{... | collective-permute-start | bytes 32 | tf_op jit(solution)/shard_map/ppermute | solution.py:31
  8.4 0.7 %copy-done = s32[16,512]{1,0:T(8,128)S(1)} copy-done((s32[16,512]{1,0:T(8,128)S(1)}, s32[16,512]{1,0:T(8,128)}, u32[]{:S(2)}) %copy-start) | copy-done | bytes 32792
  9.2 1.7 %shard_map.68 = (bf16[272,512]{1,0:T(8,128)(2,1)S(1)}, bf16[272,512]{1,0:T(8,128)(2,1)S(1)}) custom-call(s32[8]{0:T(128)S(1)} %broadcast_subtract_fusion.first_ref, s32[2]{0:T(128)S(1)} %fusion.4.start_ref, bf16[16,128,512]{2,1,0:T(8,128)(2,1)} %readings_ref.3, s32[16,512]{1,0:T(8,128)S(1)} %copy-done), custom_call_target="tpu_custom_call" | custom-call | flops 1610000000 | bytes 1024 | tf_op jit(solution)/shard_map/pallas_call | solution.py:110
  10.9 1.6 %collective-permute-start = (bf16[272,512]{1,0:T(8,128)(2,1)S(1)}, bf16[272,512]{1,0:T(8,128)(2,1)S(1)}, u32[]{:S(2)}, u32[]{:S(2)}) collective-permute-start(bf16[272,512]{1,0:T(8,128)(2,1)S(1)} %get-tuple-element.26), channel_id=1, source_target_pairs={{0,2},{2,0},{1,3},{3,1},{4,6},{6,4},{5,7},{7,5},{8,10},{10,8},{9,1... | collective-permute-start | bytes 835592 | tf_op jit(solution)/shard_map/ppermute | solution.py:31
  12.5 0.0 collective-permute-done.3
  12.5 0.0 collective-permute-done.2
  12.5 0.2 collective-permute-done.1
  12.7 0.1 pad_add_fusion.1.index_ref
  12.9 1.8 %shard_map.69 = (bf16[136,512]{1,0:T(8,128)(2,1)S(1)}, bf16[136,512]{1,0:T(8,128)(2,1)S(1)}, bf16[136,512]{1,0:T(8,128)(2,1)S(1)}, bf16[136,512]{1,0:T(8,128)(2,1)S(1)}, bf16[136,512]{1,0:T(8,128)(2,1)S(1)}) custom-call(s32[5]{0:T(128)S(1)} %pad_add_fusion.1.index_ref, bf16[16,128,512]{2,1,0:T(8,128)(2,1)} %readings_ref.3, s32[16,512]{1,0:T(8,128)S(1)} %copy-done.1), custom_call_target="tpu_custom_call" | custom-call | flops 1150000000 | bytes 1024 | tf_op jit(solution)/shard_map/pallas_call | solution.py:63
  14.7 1.6 %collective-permute-start.5 = (bf16[136,512]{1,0:T(8,128)(2,1)S(1)}, bf16[136,512]{1,0:T(8,128)(2,1)S(1)}, u32[]{:S(2)}, u32[]{:S(2)}) collective-permute-start(bf16[136,512]{1,0:T(8,128)(2,1)S(1)} %get-tuple-element.28.rest_2_), channel_id=1, source_target_pairs={{0,2},{2,0},{1,3},{3,1},{4,6},{6,4},{5,7},{7,5},{8,10},{10,8},{9,1... | collective-permute-start | bytes 417800 | tf_op jit(solution)/shard_map/ppermute | solution.py:31
  16.2 1.6 %collective-permute-start.12 = (bf16[136,512]{1,0:T(8,128)(2,1)S(1)}, bf16[136,512]{1,0:T(8,128)(2,1)S(1)}, u32[]{:S(2)}, u32[]{:S(2)}) collective-permute-start(bf16[136,512]{1,0:T(8,128)(2,1)S(1)} %get-tuple-element.33), channel_id=1, source_target_pairs={{0,12},{4,0},{8,4},{12,8},{1,13},{5,1},{9,5},{13,9},{2,14},{6,2},{... | collective-permute-start | bytes 417800 | tf_op jit(solution)/shard_map/ppermute | solution.py:31
  17.9 0.1 fusion.9
  17.9 1.1 %collective-permute-start.8 = (bf16[136,512]{1,0:T(8,128)(2,1)S(1)}, bf16[136,512]{1,0:T(8,128)(2,1)S(1)}, u32[]{:S(2)}, u32[]{:S(2)}) collective-permute-start(bf16[136,512]{1,0:T(8,128)(2,1)S(1)} %get-tuple-element.32), channel_id=1, source_target_pairs={{0,8},{4,12},{8,0},{12,4},{1,9},{5,13},{9,1},{13,5},{2,10},{6,14},... | collective-permute-start | bytes 417800 | tf_op jit(solution)/shard_map/ppermute | solution.py:31
  19.1 2.5 %collective-permute-done.5.rest_3_ = bf16[136,512]{1,0:T(8,128)(2,1)S(1)} collective-permute-done((bf16[136,512]{1,0:T(8,128)(2,1)S(1)}, bf16[136,512]{1,0:T(8,128)(2,1)S(1)}, u32[]{:S(2)}, u32[]{:S(2)}) %collective-permute-start.5) | collective-permute-done | bytes 139296 | tf_op jit(solution)/shard_map/ppermute | solution.py:31
  21.5 0.0 collective-permute-start.6
  21.6 0.0 collective-permute-done.12.rest_2_
  21.6 1.5 %collective-permute-start.13 = (bf16[136,512]{1,0:T(8,128)(2,1)S(1)}, bf16[136,512]{1,0:T(8,128)(2,1)S(1)}, u32[]{:S(2)}, u32[]{:S(2)}) collective-permute-start(bf16[136,512]{1,0:T(8,128)(2,1)S(1)} %collective-permute-done.12.rest_2_), channel_id=1, source_target_pairs={{0,2},{2,0},{1,3},{3,1},{4,6},{6,4},{5,7},{7,5},{8,10},{10,8},{9,1... | collective-permute-start | bytes 417800 | tf_op jit(solution)/shard_map/ppermute | solution.py:31
  23.1 0.1 pad_add_fusion.place_ref
  23.2 4.5 %collective-permute-start.4 = (bf16[136,512]{1,0:T(8,128)(2,1)S(1)}, bf16[136,512]{1,0:T(8,128)(2,1)S(1)}, u32[]{:S(2)}, u32[]{:S(2)}) collective-permute-start(bf16[136,512]{1,0:T(8,128)(2,1)S(1)} %get-tuple-element.27), channel_id=1, source_target_pairs={{0,4},{4,8},{8,12},{12,0},{1,5},{5,9},{9,13},{13,1},{2,6},{6,10},{... | collective-permute-start | bytes 417800 | tf_op jit(solution)/shard_map/ppermute | solution.py:31
  27.6 0.0 collective-permute-done.8.rest_2_
  27.6 0.0 collective-permute-start.14
  27.6 0.0 collective-permute-done.rest_1_
  27.6 3.8 %collective-permute-start.9 = (bf16[136,512]{1,0:T(8,128)(2,1)S(1)}, bf16[136,512]{1,0:T(8,128)(2,1)S(1)}, u32[]{:S(2)}, u32[]{:S(2)}) collective-permute-start(bf16[136,512]{1,0:T(8,128)(2,1)S(1)} %collective-permute-done.8.rest_2_), channel_id=1, source_target_pairs={{0,2},{2,0},{1,3},{3,1},{4,6},{6,4},{5,7},{7,5},{8,10},{10,8},{9,1... | collective-permute-start | bytes 417800 | tf_op jit(solution)/shard_map/ppermute | solution.py:31
  31.4 0.0 collective-permute-done.6.rest_5_
  31.4 0.2 collective-permute-start.10
  31.7 0.0 collective-permute-done.13.rest_3_
  31.7 0.3 collective-permute-start.15
  31.9 2.6 %shard_map.70 = (bf16[8,25,32,128]{3,2,1,0:T(8,128)(2,1)}, f32[2,32,128]{2,1,0:T(8,128)S(1)}, f32[25,2,128]{2,1,0:T(2,128)S(1)}) custom-call(s32[2]{0:T(128)S(1)} %get-tuple-element.55.pair_ref, s32[3]{0:T(128)S(1)} %pad_add_fusion.place_ref, bf16[272,512]{1,0:T(8,128)(2,1)S(1)} %get-tuple-element.25.rest_0_, ...), custom_call_target="tpu_custom_call" | custom-call | flops 3449999872 | bytes 1024 | tf_op jit(solution)/shard_map/pallas_call | solution.py:250
  34.5 0.0 collective-permute-done.4.rest_2_
  34.5 0.2 collective-permute-start.7
  34.7 0.0 collective-permute-done.14.rest_4_
  34.7 0.2 collective-permute-start.16
  34.9 0.9 %collective-permute-done.9.rest_3_ = bf16[136,512]{1,0:T(8,128)(2,1)S(1)} collective-permute-done((bf16[136,512]{1,0:T(8,128)(2,1)S(1)}, bf16[136,512]{1,0:T(8,128)(2,1)S(1)}, u32[]{:S(2)}, u32[]{:S(2)}) %collective-permute-start.9) | collective-permute-done | bytes 139296 | tf_op jit(solution)/shard_map/ppermute | solution.py:31
  35.8 0.0 collective-permute-start.11
  35.8 0.0 collective-permute-done.15.rest_5_
  35.8 2.6 %shard_map.71 = (bf16[8,25,32,128]{3,2,1,0:T(8,128)(2,1)}, f32[2,32,128]{2,1,0:T(8,128)S(1)}, f32[25,2,128]{2,1,0:T(2,128)S(1)}) custom-call(s32[2]{0:T(128)S(1)} %get-tuple-element.53.pair_ref, s32[3]{0:T(128)S(1)} %pad_add_fusion.place_ref, bf16[272,512]{1,0:T(8,128)(2,1)S(1)} %get-tuple-element.25.rest_0_, ...), custom_call_target="tpu_custom_call", output_to_operand_aliasing={{0}: (8, {})} | custom-call | flops 3449999872 | bytes 1024 | tf_op jit(solution)/shard_map/pallas_call | solution.py:250
  38.3 0.0 collective-permute-done.10.rest_4_
  38.3 0.0 collective-permute-done.11.rest_5_
  38.4 2.6 %shard_map.72 = (bf16[8,25,32,128]{3,2,1,0:T(8,128)(2,1)}, f32[2,32,128]{2,1,0:T(8,128)S(1)}, f32[25,2,128]{2,1,0:T(2,128)S(1)}) custom-call(s32[2]{0:T(128)S(1)} %get-tuple-element.54.pair_ref, s32[3]{0:T(128)S(1)} %pad_add_fusion.place_ref, bf16[272,512]{1,0:T(8,128)(2,1)S(1)} %get-tuple-element.25.rest_0_, ...), custom_call_target="tpu_custom_call", output_to_operand_aliasing={{0}: (8, {})} | custom-call | flops 3449999872 | bytes 1024 | tf_op jit(solution)/shard_map/pallas_call | solution.py:250
  40.9 0.0 collective-permute-done.7.rest_3_
  40.9 0.6 collective-permute-start.17
  41.5 0.0 collective-permute-start.19
  41.5 0.7 %collective-permute-start.18 = (f32[25,2,128]{2,1,0:T(2,128)S(1)}, f32[25,2,128]{2,1,0:T(2,128)S(1)}, u32[]{:S(2)}, u32[]{:S(2)}) collective-permute-start(f32[25,2,128]{2,1,0:T(2,128)S(1)} %get-tuple-element.45), channel_id=1, source_target_pairs={{0,4},{4,8},{8,12},{12,0},{1,5},{5,9},{9,13},{13,1},{2,6},{6,10},{... | collective-permute-start | bytes 76808 | tf_op jit(solution)/shard_map/ppermute | solution.py:31
  42.2 0.0 collective-permute-done.16.rest_4_
  42.2 0.3 collective-permute-done.17.rest_5_
  42.5 2.6 %shard_map.73 = (bf16[8,25,32,128]{3,2,1,0:T(8,128)(2,1)}, f32[2,32,128]{2,1,0:T(8,128)S(1)}, f32[25,2,128]{2,1,0:T(2,128)S(1)}) custom-call(s32[2]{0:T(128)S(1)} %get-tuple-element.56.pair_ref, s32[3]{0:T(128)S(1)} %pad_add_fusion.place_ref, bf16[272,512]{1,0:T(8,128)(2,1)S(1)} %get-tuple-element.25.rest_0_, ...), custom_call_target="tpu_custom_call", output_to_operand_aliasing={{0}: (8, {})} | custom-call | flops 3449999872 | bytes 1024 | tf_op jit(solution)/shard_map/pallas_call | solution.py:250
  45.1 2.9 %collective-permute-start.20 = (f32[25,2,128]{2,1,0:T(2,128)S(1)}, f32[25,2,128]{2,1,0:T(2,128)S(1)}, u32[]{:S(2)}, u32[]{:S(2)}) collective-permute-start(f32[25,2,128]{2,1,0:T(2,128)S(1)} %get-tuple-element.47), channel_id=1, source_target_pairs={{0,12},{4,0},{8,4},{12,8},{1,13},{5,1},{9,5},{13,9},{2,14},{6,2},{... | collective-permute-start | bytes 76808 | tf_op jit(solution)/shard_map/ppermute | solution.py:31
  48.0 0.1 pad_add_fusion.2.served_ref
  48.0 0.0 collective-permute-done.19.rest_6_
  48.0 0.0 collective-permute-done.18.rest_5_
  48.0 1.4 %collective-permute-done.20.rest_7_ = f32[25,2,128]{2,1,0:T(2,128)S(1)} collective-permute-done((f32[25,2,128]{2,1,0:T(2,128)S(1)}, f32[25,2,128]{2,1,0:T(2,128)S(1)}, u32[]{:S(2)}, u32[]{:S(2)}) %collective-permute-start.20) | collective-permute-done | bytes 25632 | tf_op jit(solution)/shard_map/ppermute | solution.py:31
  49.5 0.8 %shard_map.74 = bf16[25,16,128]{2,1,0:T(8,128)(2,1)S(1)} custom-call(s32[8]{0:T(128)S(1)} %get-tuple-element.48.first_ref, s32[8]{0:T(128)S(1)} %pad_add_fusion.2.served_ref, f32[2,32,128]{2,1,0:T(8,128)S(1)} %get-tuple-element.40.rest_0_, f32[2,32,128]{2,1,0:T(8,128)S(1)} %get-tuple-element.41.rest_1_, f32[2,32,128]{2,1,0:T(8,128)S(1)} %get-tuple-element.42.rest_2_, ...), custom_call_target="tpu_custom_call" | custom-call | flops 920000000 | bytes 1024 | tf_op jit(solution)/shard_map/pallas_call | solution.py:298
  50.3 0.1 collective-permute-start.21
  50.4 1.3 %collective-permute-done.21 = bf16[25,16,128]{2,1,0:T(8,128)(2,1)S(1)} collective-permute-done((bf16[25,16,128]{2,1,0:T(8,128)(2,1)S(1)}, bf16[25,16,128]{2,1,0:T(8,128)(2,1)S(1)}, u32[]{:S(2)}, u32[]{:S(2)}) %collective-permute-start.21) | collective-permute-done | bytes 102432 | tf_op jit(solution)/shard_map/ppermute | solution.py:31
  51.7 1.8 %collective-permute-start.22 = (bf16[25,16,128]{2,1,0:T(8,128)(2,1)S(1)}, bf16[25,16,128]{2,1,0:T(8,128)(2,1)S(1)}, u32[]{:S(2)}, u32[]{:S(2)}) collective-permute-start(bf16[25,16,128]{2,1,0:T(8,128)(2,1)S(1)} %add_convert_fusion), channel_id=1, source_target_pairs={{0,2},{2,0},{1,3},{3,1},{4,6},{6,4},{5,7},{7,5},{8,10},{10,8},{9,1... | collective-permute-start | bytes 307208 | tf_op jit(solution)/shard_map/ppermute | solution.py:31
  53.5 3.2 %collective-permute-done.22 = bf16[25,16,128]{2,1,0:T(8,128)(2,1)S(1)} collective-permute-done((bf16[25,16,128]{2,1,0:T(8,128)(2,1)S(1)}, bf16[25,16,128]{2,1,0:T(8,128)(2,1)S(1)}, u32[]{:S(2)}, u32[]{:S(2)}) %collective-permute-start.22) | collective-permute-done | bytes 102432 | tf_op jit(solution)/shard_map/ppermute | solution.py:31
  56.7 0.7 %convert_add_fusion = f32[25,16,128]{2,1,0:T(8,128)} fusion(bf16[25,16,128]{2,1,0:T(8,128)(2,1)S(1)} %collective-permute-done.22, bf16[25,16,128]{2,1,0:T(8,128)(2,1)S(1)} %add_convert_fusion), kind=kLoop, calls=%fused_computation | loop fusion | flops 153600 | bytes 409600 | tf_op jit(solution)/shard_map/add | solution.py:391
  (10 shorter events, 0.1 us)
Async XLA Ops:
  2.4 10.2 %collective-permute-start.3 = (s32[2]{0:T(128)S(1)}, s32[2]{0:T(128)S(1)}, u32[]{:S(2)}, u32[]{:S(2)}) collective-permute-start(s32[2]{0:T(128)S(1)} %get-tuple-element.58), channel_id=1, source_target_pairs={{0,12},{4,0},{8,4},{12,8},{1,13},{5,1},{9,5},{13,9},{2,14},{6,2},{... | collective-permute-start | bytes 32 | tf_op jit(solution)/shard_map/ppermute | solution.py:31
  7.4 5.1 %collective-permute-start.2 = (s32[2]{0:T(128)S(1)}, s32[2]{0:T(128)S(1)}, u32[]{:S(2)}, u32[]{:S(2)}) collective-permute-start(s32[2]{0:T(128)S(1)} %get-tuple-element.59), channel_id=1, source_target_pairs={{0,8},{4,12},{8,0},{12,4},{1,9},{5,13},{9,1},{13,5},{2,10},{6,14},... | collective-permute-start | bytes 32 | tf_op jit(solution)/shard_map/ppermute | solution.py:31
  7.4 5.3 %collective-permute-start.1 = (s32[2]{0:T(128)S(1)}, s32[2]{0:T(128)S(1)}, u32[]{:S(2)}, u32[]{:S(2)}) collective-permute-start(s32[2]{0:T(128)S(1)} %get-tuple-element.60), channel_id=1, source_target_pairs={{0,4},{4,8},{8,12},{12,0},{1,5},{5,9},{9,13},{13,1},{2,6},{6,10},{... | collective-permute-start | bytes 32 | tf_op jit(solution)/shard_map/ppermute | solution.py:31
  8.4 0.8 %copy-start = (s32[16,512]{1,0:T(8,128)S(1)}, s32[16,512]{1,0:T(8,128)}, u32[]{:S(2)}) copy-start(s32[16,512]{1,0:T(8,128)} %present_hbm.3) | copy-start | bytes 98308
  9.2 3.7 %copy-start.1 = (s32[16,512]{1,0:T(8,128)S(1)}, s32[16,512]{1,0:T(8,128)}, u32[]{:S(2)}) copy-start(s32[16,512]{1,0:T(8,128)} %present_hbm.3) | copy-start | bytes 98308
  10.9 16.7 %collective-permute-start = (bf16[272,512]{1,0:T(8,128)(2,1)S(1)}, bf16[272,512]{1,0:T(8,128)(2,1)S(1)}, u32[]{:S(2)}, u32[]{:S(2)}) collective-permute-start(bf16[272,512]{1,0:T(8,128)(2,1)S(1)} %get-tuple-element.26), channel_id=1, source_target_pairs={{0,2},{2,0},{1,3},{3,1},{4,6},{6,4},{5,7},{7,5},{8,10},{10,8},{9,1... | collective-permute-start | bytes 835592 | tf_op jit(solution)/shard_map/ppermute | solution.py:31
  14.7 6.9 %collective-permute-start.5 = (bf16[136,512]{1,0:T(8,128)(2,1)S(1)}, bf16[136,512]{1,0:T(8,128)(2,1)S(1)}, u32[]{:S(2)}, u32[]{:S(2)}) collective-permute-start(bf16[136,512]{1,0:T(8,128)(2,1)S(1)} %get-tuple-element.28.rest_2_), channel_id=1, source_target_pairs={{0,2},{2,0},{1,3},{3,1},{4,6},{6,4},{5,7},{7,5},{8,10},{10,8},{9,1... | collective-permute-start | bytes 417800 | tf_op jit(solution)/shard_map/ppermute | solution.py:31
  16.2 5.3 %collective-permute-start.12 = (bf16[136,512]{1,0:T(8,128)(2,1)S(1)}, bf16[136,512]{1,0:T(8,128)(2,1)S(1)}, u32[]{:S(2)}, u32[]{:S(2)}) collective-permute-start(bf16[136,512]{1,0:T(8,128)(2,1)S(1)} %get-tuple-element.33), channel_id=1, source_target_pairs={{0,12},{4,0},{8,4},{12,8},{1,13},{5,1},{9,5},{13,9},{2,14},{6,2},{... | collective-permute-start | bytes 417800 | tf_op jit(solution)/shard_map/ppermute | solution.py:31
  17.9 9.7 %collective-permute-start.8 = (bf16[136,512]{1,0:T(8,128)(2,1)S(1)}, bf16[136,512]{1,0:T(8,128)(2,1)S(1)}, u32[]{:S(2)}, u32[]{:S(2)}) collective-permute-start(bf16[136,512]{1,0:T(8,128)(2,1)S(1)} %get-tuple-element.32), channel_id=1, source_target_pairs={{0,8},{4,12},{8,0},{12,4},{1,9},{5,13},{9,1},{13,5},{2,10},{6,14},... | collective-permute-start | bytes 417800 | tf_op jit(solution)/shard_map/ppermute | solution.py:31
  21.5 9.9 %collective-permute-start.6 = (bf16[136,512]{1,0:T(8,128)(2,1)S(1)}, bf16[136,512]{1,0:T(8,128)(2,1)S(1)}, u32[]{:S(2)}, u32[]{:S(2)}) collective-permute-start(bf16[136,512]{1,0:T(8,128)(2,1)S(1)} %collective-permute-done.5.rest_3_), channel_id=1, source_target_pairs={{0,1},{1,0},{2,3},{3,2},{4,5},{5,4},{6,7},{7,6},{8,9},{9,8},{10,11... | collective-permute-start | bytes 417800 | tf_op jit(solution)/shard_map/ppermute | solution.py:31
  21.6 10.1 %collective-permute-start.13 = (bf16[136,512]{1,0:T(8,128)(2,1)S(1)}, bf16[136,512]{1,0:T(8,128)(2,1)S(1)}, u32[]{:S(2)}, u32[]{:S(2)}) collective-permute-start(bf16[136,512]{1,0:T(8,128)(2,1)S(1)} %collective-permute-done.12.rest_2_), channel_id=1, source_target_pairs={{0,2},{2,0},{1,3},{3,1},{4,6},{6,4},{5,7},{7,5},{8,10},{10,8},{9,1... | collective-permute-start | bytes 417800 | tf_op jit(solution)/shard_map/ppermute | solution.py:31
  23.2 11.3 %collective-permute-start.4 = (bf16[136,512]{1,0:T(8,128)(2,1)S(1)}, bf16[136,512]{1,0:T(8,128)(2,1)S(1)}, u32[]{:S(2)}, u32[]{:S(2)}) collective-permute-start(bf16[136,512]{1,0:T(8,128)(2,1)S(1)} %get-tuple-element.27), channel_id=1, source_target_pairs={{0,4},{4,8},{8,12},{12,0},{1,5},{5,9},{9,13},{13,1},{2,6},{6,10},{... | collective-permute-start | bytes 417800 | tf_op jit(solution)/shard_map/ppermute | solution.py:31
  27.6 7.1 %collective-permute-start.14 = (bf16[136,512]{1,0:T(8,128)(2,1)S(1)}, bf16[136,512]{1,0:T(8,128)(2,1)S(1)}, u32[]{:S(2)}, u32[]{:S(2)}) collective-permute-start(bf16[136,512]{1,0:T(8,128)(2,1)S(1)} %collective-permute-done.12.rest_2_), channel_id=1, source_target_pairs={{0,1},{1,0},{2,3},{3,2},{4,5},{5,4},{6,7},{7,6},{8,9},{9,8},{10,11... | collective-permute-start | bytes 417800 | tf_op jit(solution)/shard_map/ppermute | solution.py:31
  27.6 8.1 %collective-permute-start.9 = (bf16[136,512]{1,0:T(8,128)(2,1)S(1)}, bf16[136,512]{1,0:T(8,128)(2,1)S(1)}, u32[]{:S(2)}, u32[]{:S(2)}) collective-permute-start(bf16[136,512]{1,0:T(8,128)(2,1)S(1)} %collective-permute-done.8.rest_2_), channel_id=1, source_target_pairs={{0,2},{2,0},{1,3},{3,1},{4,6},{6,4},{5,7},{7,5},{8,10},{10,8},{9,1... | collective-permute-start | bytes 417800 | tf_op jit(solution)/shard_map/ppermute | solution.py:31
  31.4 6.9 %collective-permute-start.10 = (bf16[136,512]{1,0:T(8,128)(2,1)S(1)}, bf16[136,512]{1,0:T(8,128)(2,1)S(1)}, u32[]{:S(2)}, u32[]{:S(2)}) collective-permute-start(bf16[136,512]{1,0:T(8,128)(2,1)S(1)} %collective-permute-done.8.rest_2_), channel_id=1, source_target_pairs={{0,1},{1,0},{2,3},{3,2},{4,5},{5,4},{6,7},{7,6},{8,9},{9,8},{10,11... | collective-permute-start | bytes 417800 | tf_op jit(solution)/shard_map/ppermute | solution.py:31
  31.7 4.1 %collective-permute-start.15 = (bf16[136,512]{1,0:T(8,128)(2,1)S(1)}, bf16[136,512]{1,0:T(8,128)(2,1)S(1)}, u32[]{:S(2)}, u32[]{:S(2)}) collective-permute-start(bf16[136,512]{1,0:T(8,128)(2,1)S(1)} %collective-permute-done.13.rest_3_), channel_id=1, source_target_pairs={{0,1},{1,0},{2,3},{3,2},{4,5},{5,4},{6,7},{7,6},{8,9},{9,8},{10,11... | collective-permute-start | bytes 417800 | tf_op jit(solution)/shard_map/ppermute | solution.py:31
  34.5 6.4 %collective-permute-start.7 = (bf16[136,512]{1,0:T(8,128)(2,1)S(1)}, bf16[136,512]{1,0:T(8,128)(2,1)S(1)}, u32[]{:S(2)}, u32[]{:S(2)}) collective-permute-start(bf16[136,512]{1,0:T(8,128)(2,1)S(1)} %collective-permute-done.4.rest_2_), channel_id=1, source_target_pairs={{0,2},{2,0},{1,3},{3,1},{4,6},{6,4},{5,7},{7,5},{8,10},{10,8},{9,1... | collective-permute-start | bytes 417800 | tf_op jit(solution)/shard_map/ppermute | solution.py:31
  34.7 7.5 %collective-permute-start.16 = (bf16[136,512]{1,0:T(8,128)(2,1)S(1)}, bf16[136,512]{1,0:T(8,128)(2,1)S(1)}, u32[]{:S(2)}, u32[]{:S(2)}) collective-permute-start(bf16[136,512]{1,0:T(8,128)(2,1)S(1)} %collective-permute-done.4.rest_2_), channel_id=1, source_target_pairs={{0,1},{1,0},{2,3},{3,2},{4,5},{5,4},{6,7},{7,6},{8,9},{9,8},{10,11... | collective-permute-start | bytes 417800 | tf_op jit(solution)/shard_map/ppermute | solution.py:31
  35.8 2.6 %collective-permute-start.11 = (bf16[136,512]{1,0:T(8,128)(2,1)S(1)}, bf16[136,512]{1,0:T(8,128)(2,1)S(1)}, u32[]{:S(2)}, u32[]{:S(2)}) collective-permute-start(bf16[136,512]{1,0:T(8,128)(2,1)S(1)} %collective-permute-done.9.rest_3_), channel_id=1, source_target_pairs={{0,1},{1,0},{2,3},{3,2},{4,5},{5,4},{6,7},{7,6},{8,9},{9,8},{10,11... | collective-permute-start | bytes 417800 | tf_op jit(solution)/shard_map/ppermute | solution.py:31
  40.9 1.6 %collective-permute-start.17 = (bf16[136,512]{1,0:T(8,128)(2,1)S(1)}, bf16[136,512]{1,0:T(8,128)(2,1)S(1)}, u32[]{:S(2)}, u32[]{:S(2)}) collective-permute-start(bf16[136,512]{1,0:T(8,128)(2,1)S(1)} %collective-permute-done.7.rest_3_), channel_id=1, source_target_pairs={{0,1},{1,0},{2,3},{3,2},{4,5},{5,4},{6,7},{7,6},{8,9},{9,8},{10,11... | collective-permute-start | bytes 417800 | tf_op jit(solution)/shard_map/ppermute | solution.py:31
  41.5 6.5 %collective-permute-start.19 = (f32[25,2,128]{2,1,0:T(2,128)S(1)}, f32[25,2,128]{2,1,0:T(2,128)S(1)}, u32[]{:S(2)}, u32[]{:S(2)}) collective-permute-start(f32[25,2,128]{2,1,0:T(2,128)S(1)} %get-tuple-element.46), channel_id=1, source_target_pairs={{0,8},{4,12},{8,0},{12,4},{1,9},{5,13},{9,1},{13,5},{2,10},{6,14},... | collective-permute-start | bytes 76808 | tf_op jit(solution)/shard_map/ppermute | solution.py:31
  41.5 6.5 %collective-permute-start.18 = (f32[25,2,128]{2,1,0:T(2,128)S(1)}, f32[25,2,128]{2,1,0:T(2,128)S(1)}, u32[]{:S(2)}, u32[]{:S(2)}) collective-permute-start(f32[25,2,128]{2,1,0:T(2,128)S(1)} %get-tuple-element.45), channel_id=1, source_target_pairs={{0,4},{4,8},{8,12},{12,0},{1,5},{5,9},{9,13},{13,1},{2,6},{6,10},{... | collective-permute-start | bytes 76808 | tf_op jit(solution)/shard_map/ppermute | solution.py:31
  45.1 4.4 %collective-permute-start.20 = (f32[25,2,128]{2,1,0:T(2,128)S(1)}, f32[25,2,128]{2,1,0:T(2,128)S(1)}, u32[]{:S(2)}, u32[]{:S(2)}) collective-permute-start(f32[25,2,128]{2,1,0:T(2,128)S(1)} %get-tuple-element.47), channel_id=1, source_target_pairs={{0,12},{4,0},{8,4},{12,8},{1,13},{5,1},{9,5},{13,9},{2,14},{6,2},{... | collective-permute-start | bytes 76808 | tf_op jit(solution)/shard_map/ppermute | solution.py:31
  50.3 1.4 %collective-permute-start.21 = (bf16[25,16,128]{2,1,0:T(8,128)(2,1)S(1)}, bf16[25,16,128]{2,1,0:T(8,128)(2,1)S(1)}, u32[]{:S(2)}, u32[]{:S(2)}) collective-permute-start(bf16[25,16,128]{2,1,0:T(8,128)(2,1)S(1)} %shard_map.74), channel_id=1, source_target_pairs={{0,1},{1,0},{2,3},{3,2},{4,5},{5,4},{6,7},{7,6},{8,9},{9,8},{10,11... | collective-permute-start | bytes 307208 | tf_op jit(solution)/shard_map/ppermute | solution.py:31
  51.7 5.0 %collective-permute-start.22 = (bf16[25,16,128]{2,1,0:T(8,128)(2,1)S(1)}, bf16[25,16,128]{2,1,0:T(8,128)(2,1)S(1)}, u32[]{:S(2)}, u32[]{:S(2)}) collective-permute-start(bf16[25,16,128]{2,1,0:T(8,128)(2,1)S(1)} %add_convert_fusion), channel_id=1, source_target_pairs={{0,2},{2,0},{1,3},{3,1},{4,6},{6,4},{5,7},{7,5},{8,10},{10,8},{9,1... | collective-permute-start | bytes 307208 | tf_op jit(solution)/shard_map/ppermute | solution.py:31

commit v4 on v3

--- a/solution.py
+++ b/solution.py
@@ -188,25 +188,26 @@
                 left[j], right[j], (((1,), (1,)), ((), ())), preferred_element_type=jnp.float32
             )
 
-        def finish(j):
-            def standard(lag):
-                m, odd = lag // 2, lag % 2
-                return product[
-                    j,
-                    m * per_row : (m + 1) * per_row,
-                    odd * block_size : (odd + 1) * block_size,
-                ] * float(scales[lag])
-
+        def standard(j, lag):
+            m, odd = lag // 2, lag % 2
+            return product[
+                j,
+                m * per_row : (m + 1) * per_row,
+                odd * block_size : (odd + 1) * block_size,
+            ] * float(scales[lag])
+
+        def hand_over(j):
             for lag in range(LAGS):
-                ready[j, lag] = standard(lag).astype(jnp.bfloat16)
+                ready[j, lag] = standard(j, lag).astype(jnp.bfloat16)
 
             @pl.when(pair_ref[j] >= 0)
             def _():
                 pltpu.make_async_copy(ready.at[j], cov_ref.at[pair_ref[j]], sems.at[j]).start()
 
+        def finish(j):
             used = jnp.where(pair_ref[j] >= 0, 1.0 / block_size, 0.0)
             for lag in range(LAGS):
-                square = standard(lag)
+                square = standard(j, lag)
                 square = square * square
                 col_ref[lag, j : j + 1, :] = jnp.sum(square, axis=0, keepdims=True) * used
                 squares[j, lag * per_row : (lag + 1) * per_row, :] = square.astype(jnp.bfloat16)
@@ -231,6 +232,8 @@
             prepare(j)
         for j in range(slots):
             multiply(j)
+        for j in range(slots):
+            hand_over(j)
         for j in range(slots):
             finish(j)
         for j in range(slots):
@@ -318,6 +321,8 @@
     groups = sorted({d % sensor_count for d in range(-REACH, REACH + 1)})
     slot_count = len(groups) * CAP
 
+    both = lax.optimization_barrier(jnp.concatenate([pair_first, pair_second]))
+    pair_first, pair_second = both[:pair_count], both[pair_count:]
     first_index = pair_first - home * blk_dev
     owner = pair_second // blk_dev
     partner_index = pair_second - owner * blk_dev

time: 57.8 us -> 56.9 us (0.984)
  starting transfers between devices: 28.6 us -> 27.8 us
    ppermute x23, starting transfers between devices: 28.6 us -> 27.8 us  [rotated(): lax.ppermute(block, axis, [(i, (i + distance) % size) for i in range(size)])]
    concatenate x0 -> x1, other arithmetic: none -> 0.75 us  [local(): both = lax.optimization_barrier(jnp.concatenate([pair_first, pair_second]))]
    sub x1 -> x0, other arithmetic: 0.66 us -> none  [local(): first_index = pair_first - home * blk_dev]
    sub x1, other arithmetic: 0.67 us -> 0.08 us  [local(): partner_index = pair_second - owner * blk_dev]
  transfers between devices with their start and end apart: 23 -> 23, of which waited for: 7 -> 6; matrix products, arithmetic and copies ran while one was open for 1% -> 1% of each run, Pallas kernels for 24% -> 25%
where the time goes in v4:
time: 56.9 us; the launch traced here: 56.2 us
  starting transfers between devices  27.8 us (49%)
  Pallas kernels  14.6 us (26%)
  waiting for transfers between devices  9.82 us (17%)
  other arithmetic  2.2 us (4%)
  local copies, waits for them, and re-layouts  0.9 us (2%)
  between operations  0.77 us (1%)
    ppermute x23, starting transfers between devices, rotated(): lax.ppermute(block, axis, [(i, (i + distance) % size) for i in range(size)])  27.8 us
    pallas_call x4, Pallas kernels, covariances(): pl.pallas_call(kernel, out_shape=[jax.ShapeDtypeStruct((pairs, LAGS, per_...  10.2 us
    ppermute x23, waiting for transfers between devices, rotated(): lax.ppermute(block, axis, [(i, (i + distance) % size) for i in range(size)])  9.82 us
    pallas_call x1, Pallas kernels, pack_blocks(): pl.pallas_call(kernel, out_shape=[jax.ShapeDtypeStruct((rows + MASK_ROWS,...  1.8 us
    pallas_call x1, Pallas kernels, pack_first(): pl.pallas_call(kernel, out_shape=[jax.ShapeDtypeStruct((pairs * per_row +...  1.74 us
  transfers between devices with their start and end apart: 23, of which 6 were waited for; matrix products, arithmetic and copies ran while one was open for 1% of the time, Pallas kernels for 25%

profile of v4, /device:TPU:0, one launch (start us, length us, event | category | flops | bytes accessed | tf_op | source)
XLA Modules:
  0.0 56.2 jit_solution(13013980292573188794)
XLA Ops:
  0.6 0.7 %pad_add_fusion = s32[16]{0:T(128)S(1)} fusion(s32[8]{0:T(128)} %param.8, s32[8]{0:T(128)} %param.7), kind=kLoop, calls=%fused_computation.35 | loop fusion | flops 16 | bytes 128 | tf_op jit(solution)/shard_map/concatenate | solution.py:324
  1.4 0.1 multiply_subtract_fusion
  1.5 0.2 convert_reduce_fusion
  1.7 0.1 select_reduce_fusion
  1.8 0.1 fusion.10
  1.9 5.1 %collective-permute-start.3 = (s32[2]{0:T(128)S(1)}, s32[2]{0:T(128)S(1)}, u32[]{:S(2)}, u32[]{:S(2)}) collective-permute-start(s32[2]{0:T(128)S(1)} %get-tuple-element.58), channel_id=1, source_target_pairs={{0,12},{4,0},{8,4},{12,8},{1,13},{5,1},{9,5},{13,9},{2,14},{6,2},{... | collective-permute-start | bytes 32 | tf_op jit(solution)/shard_map/ppermute | solution.py:31
  6.9 0.0 collective-permute-start.2
  6.9 1.0 %collective-permute-start.1 = (s32[2]{0:T(128)S(1)}, s32[2]{0:T(128)S(1)}, u32[]{:S(2)}, u32[]{:S(2)}) collective-permute-start(s32[2]{0:T(128)S(1)} %get-tuple-element.60), channel_id=1, source_target_pairs={{0,4},{4,8},{8,12},{12,0},{1,5},{5,9},{9,13},{13,1},{2,6},{6,10},{... | collective-permute-start | bytes 32 | tf_op jit(solution)/shard_map/ppermute | solution.py:31
  8.0 0.7 %copy-done = s32[16,512]{1,0:T(8,128)S(1)} copy-done((s32[16,512]{1,0:T(8,128)S(1)}, s32[16,512]{1,0:T(8,128)}, u32[]{:S(2)}) %copy-start) | copy-done | bytes 32792
  8.7 1.7 %shard_map.68 = (bf16[272,512]{1,0:T(8,128)(2,1)S(1)}, bf16[272,512]{1,0:T(8,128)(2,1)S(1)}) custom-call(s32[8]{0:T(128)S(1)} %get-tuple-element.61.first_ref, s32[2]{0:T(128)S(1)} %fusion.4.start_ref, bf16[16,128,512]{2,1,0:T(8,128)(2,1)} %readings_ref.3, s32[16,512]{1,0:T(8,128)S(1)} %copy-done), custom_call_target="tpu_custom_call" | custom-call | flops 1610000000 | bytes 1024 | tf_op jit(solution)/shard_map/pallas_call | solution.py:110
  10.4 1.6 %collective-permute-start = (bf16[272,512]{1,0:T(8,128)(2,1)S(1)}, bf16[272,512]{1,0:T(8,128)(2,1)S(1)}, u32[]{:S(2)}, u32[]{:S(2)}) collective-permute-start(bf16[272,512]{1,0:T(8,128)(2,1)S(1)} %get-tuple-element.26), channel_id=1, source_target_pairs={{0,2},{2,0},{1,3},{3,1},{4,6},{6,4},{5,7},{7,5},{8,10},{10,8},{9,1... | collective-permute-start | bytes 835592 | tf_op jit(solution)/shard_map/ppermute | solution.py:31
  12.0 0.0 collective-permute-done.3
  12.0 0.0 collective-permute-done.2
  12.0 0.2 collective-permute-done.1
  12.3 0.1 pad_add_fusion.2.index_ref
  12.4 1.8 %shard_map.69 = (bf16[136,512]{1,0:T(8,128)(2,1)S(1)}, bf16[136,512]{1,0:T(8,128)(2,1)S(1)}, bf16[136,512]{1,0:T(8,128)(2,1)S(1)}, bf16[136,512]{1,0:T(8,128)(2,1)S(1)}, bf16[136,512]{1,0:T(8,128)(2,1)S(1)}) custom-call(s32[5]{0:T(128)S(1)} %pad_add_fusion.2.index_ref, bf16[16,128,512]{2,1,0:T(8,128)(2,1)} %readings_ref.3, s32[16,512]{1,0:T(8,128)S(1)} %copy-done.1), custom_call_target="tpu_custom_call" | custom-call | flops 1150000000 | bytes 1024 | tf_op jit(solution)/shard_map/pallas_call | solution.py:63
  14.2 1.6 %collective-permute-start.5 = (bf16[136,512]{1,0:T(8,128)(2,1)S(1)}, bf16[136,512]{1,0:T(8,128)(2,1)S(1)}, u32[]{:S(2)}, u32[]{:S(2)}) collective-permute-start(bf16[136,512]{1,0:T(8,128)(2,1)S(1)} %get-tuple-element.28.rest_2_), channel_id=1, source_target_pairs={{0,2},{2,0},{1,3},{3,1},{4,6},{6,4},{5,7},{7,5},{8,10},{10,8},{9,1... | collective-permute-start | bytes 417800 | tf_op jit(solution)/shard_map/ppermute | solution.py:31
  15.7 1.6 %collective-permute-start.12 = (bf16[136,512]{1,0:T(8,128)(2,1)S(1)}, bf16[136,512]{1,0:T(8,128)(2,1)S(1)}, u32[]{:S(2)}, u32[]{:S(2)}) collective-permute-start(bf16[136,512]{1,0:T(8,128)(2,1)S(1)} %get-tuple-element.33), channel_id=1, source_target_pairs={{0,12},{4,0},{8,4},{12,8},{1,13},{5,1},{9,5},{13,9},{2,14},{6,2},{... | collective-permute-start | bytes 417800 | tf_op jit(solution)/shard_map/ppermute | solution.py:31
  17.4 0.1 fusion.9
  17.4 1.1 %collective-permute-start.8 = (bf16[136,512]{1,0:T(8,128)(2,1)S(1)}, bf16[136,512]{1,0:T(8,128)(2,1)S(1)}, u32[]{:S(2)}, u32[]{:S(2)}) collective-permute-start(bf16[136,512]{1,0:T(8,128)(2,1)S(1)} %get-tuple-element.32), channel_id=1, source_target_pairs={{0,8},{4,12},{8,0},{12,4},{1,9},{5,13},{9,1},{13,5},{2,10},{6,14},... | collective-permute-start | bytes 417800 | tf_op jit(solution)/shard_map/ppermute | solution.py:31
  18.6 2.5 %collective-permute-done.5.rest_3_ = bf16[136,512]{1,0:T(8,128)(2,1)S(1)} collective-permute-done((bf16[136,512]{1,0:T(8,128)(2,1)S(1)}, bf16[136,512]{1,0:T(8,128)(2,1)S(1)}, u32[]{:S(2)}, u32[]{:S(2)}) %collective-permute-start.5) | collective-permute-done | bytes 139296 | tf_op jit(solution)/shard_map/ppermute | solution.py:31
  21.1 0.0 collective-permute-start.6
  21.1 0.0 collective-permute-done.12.rest_2_
  21.1 1.5 %collective-permute-start.13 = (bf16[136,512]{1,0:T(8,128)(2,1)S(1)}, bf16[136,512]{1,0:T(8,128)(2,1)S(1)}, u32[]{:S(2)}, u32[]{:S(2)}) collective-permute-start(bf16[136,512]{1,0:T(8,128)(2,1)S(1)} %collective-permute-done.12.rest_2_), channel_id=1, source_target_pairs={{0,2},{2,0},{1,3},{3,1},{4,6},{6,4},{5,7},{7,5},{8,10},{10,8},{9,1... | collective-permute-start | bytes 417800 | tf_op jit(solution)/shard_map/ppermute | solution.py:31
  22.6 0.1 pad_add_fusion.1.place_ref
  22.7 4.4 %collective-permute-start.4 = (bf16[136,512]{1,0:T(8,128)(2,1)S(1)}, bf16[136,512]{1,0:T(8,128)(2,1)S(1)}, u32[]{:S(2)}, u32[]{:S(2)}) collective-permute-start(bf16[136,512]{1,0:T(8,128)(2,1)S(1)} %get-tuple-element.27), channel_id=1, source_target_pairs={{0,4},{4,8},{8,12},{12,0},{1,5},{5,9},{9,13},{13,1},{2,6},{6,10},{... | collective-permute-start | bytes 417800 | tf_op jit(solution)/shard_map/ppermute | solution.py:31
  27.1 0.0 collective-permute-done.8.rest_2_
  27.1 0.0 collective-permute-start.14
  27.1 0.0 collective-permute-done.rest_1_
  27.1 0.8 %collective-permute-start.9 = (bf16[136,512]{1,0:T(8,128)(2,1)S(1)}, bf16[136,512]{1,0:T(8,128)(2,1)S(1)}, u32[]{:S(2)}, u32[]{:S(2)}) collective-permute-start(bf16[136,512]{1,0:T(8,128)(2,1)S(1)} %collective-permute-done.8.rest_2_), channel_id=1, source_target_pairs={{0,2},{2,0},{1,3},{3,1},{4,6},{6,4},{5,7},{7,5},{8,10},{10,8},{9,1... | collective-permute-start | bytes 417800 | tf_op jit(solution)/shard_map/ppermute | solution.py:31
  28.0 0.0 collective-permute-done.6.rest_5_
  28.0 0.2 collective-permute-start.10
  28.2 0.0 collective-permute-done.13.rest_3_
  28.2 0.3 collective-permute-start.15
  28.5 2.6 %shard_map.70 = (bf16[8,25,32,128]{3,2,1,0:T(8,128)(2,1)}, f32[2,32,128]{2,1,0:T(8,128)S(1)}, f32[25,2,128]{2,1,0:T(2,128)S(1)}) custom-call(s32[2]{0:T(128)S(1)} %get-tuple-element.55.pair_ref, s32[3]{0:T(128)S(1)} %pad_add_fusion.1.place_ref, bf16[272,512]{1,0:T(8,128)(2,1)S(1)} %get-tuple-element.25.rest_0_, ...), custom_call_target="tpu_custom_call" | custom-call | flops 3449999872 | bytes 1024 | tf_op jit(solution)/shard_map/pallas_call | solution.py:253
  31.0 0.0 collective-permute-done.4.rest_2_
  31.0 1.3 %collective-permute-start.7 = (bf16[136,512]{1,0:T(8,128)(2,1)S(1)}, bf16[136,512]{1,0:T(8,128)(2,1)S(1)}, u32[]{:S(2)}, u32[]{:S(2)}) collective-permute-start(bf16[136,512]{1,0:T(8,128)(2,1)S(1)} %collective-permute-done.4.rest_2_), channel_id=1, source_target_pairs={{0,2},{2,0},{1,3},{3,1},{4,6},{6,4},{5,7},{7,5},{8,10},{10,8},{9,1... | collective-permute-start | bytes 417800 | tf_op jit(solution)/shard_map/ppermute | solution.py:31
  32.4 0.0 collective-permute-done.14.rest_4_
  32.4 0.0 collective-permute-start.16
  32.4 0.8 %collective-permute-done.9.rest_3_ = bf16[136,512]{1,0:T(8,128)(2,1)S(1)} collective-permute-done((bf16[136,512]{1,0:T(8,128)(2,1)S(1)}, bf16[136,512]{1,0:T(8,128)(2,1)S(1)}, u32[]{:S(2)}, u32[]{:S(2)}) %collective-permute-start.9) | collective-permute-done | bytes 139296 | tf_op jit(solution)/shard_map/ppermute | solution.py:31
  33.2 0.0 collective-permute-start.11
  33.2 0.0 collective-permute-done.15.rest_5_
  33.2 2.6 %shard_map.71 = (bf16[8,25,32,128]{3,2,1,0:T(8,128)(2,1)}, f32[2,32,128]{2,1,0:T(8,128)S(1)}, f32[25,2,128]{2,1,0:T(2,128)S(1)}) custom-call(s32[2]{0:T(128)S(1)} %get-tuple-element.53.pair_ref, s32[3]{0:T(128)S(1)} %pad_add_fusion.1.place_ref, bf16[272,512]{1,0:T(8,128)(2,1)S(1)} %get-tuple-element.25.rest_0_, ...), custom_call_target="tpu_custom_call", output_to_operand_aliasing={{0}: (8, {})} | custom-call | flops 3449999872 | bytes 1024 | tf_op jit(solution)/shard_map/pallas_call | solution.py:253
  35.8 0.0 collective-permute-done.10.rest_4_
  35.8 0.0 collective-permute-done.11.rest_5_
  35.8 2.6 %shard_map.72 = (bf16[8,25,32,128]{3,2,1,0:T(8,128)(2,1)}, f32[2,32,128]{2,1,0:T(8,128)S(1)}, f32[25,2,128]{2,1,0:T(2,128)S(1)}) custom-call(s32[2]{0:T(128)S(1)} %get-tuple-element.54.pair_ref, s32[3]{0:T(128)S(1)} %pad_add_fusion.1.place_ref, bf16[272,512]{1,0:T(8,128)(2,1)S(1)} %get-tuple-element.25.rest_0_, ...), custom_call_target="tpu_custom_call", output_to_operand_aliasing={{0}: (8, {})} | custom-call | flops 3449999872 | bytes 1024 | tf_op jit(solution)/shard_map/pallas_call | solution.py:253
  38.4 0.0 collective-permute-done.7.rest_3_
  38.4 0.6 %collective-permute-start.17 = (bf16[136,512]{1,0:T(8,128)(2,1)S(1)}, bf16[136,512]{1,0:T(8,128)(2,1)S(1)}, u32[]{:S(2)}, u32[]{:S(2)}) collective-permute-start(bf16[136,512]{1,0:T(8,128)(2,1)S(1)} %collective-permute-done.7.rest_3_), channel_id=1, source_target_pairs={{0,1},{1,0},{2,3},{3,2},{4,5},{5,4},{6,7},{7,6},{8,9},{9,8},{10,11... | collective-permute-start | bytes 417800 | tf_op jit(solution)/shard_map/ppermute | solution.py:31
  39.0 0.9 %collective-permute-start.19 = (f32[25,2,128]{2,1,0:T(2,128)S(1)}, f32[25,2,128]{2,1,0:T(2,128)S(1)}, u32[]{:S(2)}, u32[]{:S(2)}) collective-permute-start(f32[25,2,128]{2,1,0:T(2,128)S(1)} %get-tuple-element.46), channel_id=1, source_target_pairs={{0,8},{4,12},{8,0},{12,4},{1,9},{5,13},{9,1},{13,5},{2,10},{6,14},... | collective-permute-start | bytes 76808 | tf_op jit(solution)/shard_map/ppermute | solution.py:31
  39.9 1.9 %collective-permute-start.18 = (f32[25,2,128]{2,1,0:T(2,128)S(1)}, f32[25,2,128]{2,1,0:T(2,128)S(1)}, u32[]{:S(2)}, u32[]{:S(2)}) collective-permute-start(f32[25,2,128]{2,1,0:T(2,128)S(1)} %get-tuple-element.45), channel_id=1, source_target_pairs={{0,4},{4,8},{8,12},{12,0},{1,5},{5,9},{9,13},{13,1},{2,6},{6,10},{... | collective-permute-start | bytes 76808 | tf_op jit(solution)/shard_map/ppermute | solution.py:31
  41.7 0.0 collective-permute-done.16.rest_4_
  41.7 0.0 collective-permute-done.17.rest_5_
  41.7 2.6 %shard_map.73 = (bf16[8,25,32,128]{3,2,1,0:T(8,128)(2,1)}, f32[2,32,128]{2,1,0:T(8,128)S(1)}, f32[25,2,128]{2,1,0:T(2,128)S(1)}) custom-call(s32[2]{0:T(128)S(1)} %get-tuple-element.56.pair_ref, s32[3]{0:T(128)S(1)} %pad_add_fusion.1.place_ref, bf16[272,512]{1,0:T(8,128)(2,1)S(1)} %get-tuple-element.25.rest_0_, ...), custom_call_target="tpu_custom_call", output_to_operand_aliasing={{0}: (8, {})} | custom-call | flops 3449999872 | bytes 1024 | tf_op jit(solution)/shard_map/pallas_call | solution.py:253
  44.3 2.1 %collective-permute-start.20 = (f32[25,2,128]{2,1,0:T(2,128)S(1)}, f32[25,2,128]{2,1,0:T(2,128)S(1)}, u32[]{:S(2)}, u32[]{:S(2)}) collective-permute-start(f32[25,2,128]{2,1,0:T(2,128)S(1)} %get-tuple-element.47), channel_id=1, source_target_pairs={{0,12},{4,0},{8,4},{12,8},{1,13},{5,1},{9,5},{13,9},{2,14},{6,2},{... | collective-permute-start | bytes 76808 | tf_op jit(solution)/shard_map/ppermute | solution.py:31
  46.4 0.1 pad_add_fusion.3.served_ref
  46.5 0.0 collective-permute-done.19.rest_6_
  46.5 0.0 collective-permute-done.18.rest_5_
  46.5 1.7 %collective-permute-done.20.rest_7_ = f32[25,2,128]{2,1,0:T(2,128)S(1)} collective-permute-done((f32[25,2,128]{2,1,0:T(2,128)S(1)}, f32[25,2,128]{2,1,0:T(2,128)S(1)}, u32[]{:S(2)}, u32[]{:S(2)}) %collective-permute-start.20) | collective-permute-done | bytes 25632 | tf_op jit(solution)/shard_map/ppermute | solution.py:31
  48.2 0.8 %shard_map.74 = bf16[25,16,128]{2,1,0:T(8,128)(2,1)S(1)} custom-call(s32[8]{0:T(128)S(1)} %get-tuple-element.48.first_ref, s32[8]{0:T(128)S(1)} %pad_add_fusion.3.served_ref, f32[2,32,128]{2,1,0:T(8,128)S(1)} %get-tuple-element.40.rest_0_, f32[2,32,128]{2,1,0:T(8,128)S(1)} %get-tuple-element.41.rest_1_, f32[2,32,128]{2,1,0:T(8,128)S(1)} %get-tuple-element.42.rest_2_, ...), custom_call_target="tpu_custom_call" | custom-call | flops 920000000 | bytes 1024 | tf_op jit(solution)/shard_map/pallas_call | solution.py:301
  49.0 0.1 collective-permute-start.21
  49.1 1.3 %collective-permute-done.21 = bf16[25,16,128]{2,1,0:T(8,128)(2,1)S(1)} collective-permute-done((bf16[25,16,128]{2,1,0:T(8,128)(2,1)S(1)}, bf16[25,16,128]{2,1,0:T(8,128)(2,1)S(1)}, u32[]{:S(2)}, u32[]{:S(2)}) %collective-permute-start.21) | collective-permute-done | bytes 102432 | tf_op jit(solution)/shard_map/ppermute | solution.py:31
  50.4 1.8 %collective-permute-start.22 = (bf16[25,16,128]{2,1,0:T(8,128)(2,1)S(1)}, bf16[25,16,128]{2,1,0:T(8,128)(2,1)S(1)}, u32[]{:S(2)}, u32[]{:S(2)}) collective-permute-start(bf16[25,16,128]{2,1,0:T(8,128)(2,1)S(1)} %add_convert_fusion), channel_id=1, source_target_pairs={{0,2},{2,0},{1,3},{3,1},{4,6},{6,4},{5,7},{7,5},{8,10},{10,8},{9,1... | collective-permute-start | bytes 307208 | tf_op jit(solution)/shard_map/ppermute | solution.py:31
  52.2 3.2 %collective-permute-done.22 = bf16[25,16,128]{2,1,0:T(8,128)(2,1)S(1)} collective-permute-done((bf16[25,16,128]{2,1,0:T(8,128)(2,1)S(1)}, bf16[25,16,128]{2,1,0:T(8,128)(2,1)S(1)}, u32[]{:S(2)}, u32[]{:S(2)}) %collective-permute-start.22) | collective-permute-done | bytes 102432 | tf_op jit(solution)/shard_map/ppermute | solution.py:31
  55.4 0.7 %convert_add_fusion = f32[25,16,128]{2,1,0:T(8,128)} fusion(bf16[25,16,128]{2,1,0:T(8,128)(2,1)S(1)} %collective-permute-done.22, bf16[25,16,128]{2,1,0:T(8,128)(2,1)S(1)} %add_convert_fusion), kind=kLoop, calls=%fused_computation | loop fusion | flops 153600 | bytes 409600 | tf_op jit(solution)/shard_map/add | solution.py:396
  (10 shorter events, 0.1 us)
Async XLA Ops:
  1.9 10.2 %collective-permute-start.3 = (s32[2]{0:T(128)S(1)}, s32[2]{0:T(128)S(1)}, u32[]{:S(2)}, u32[]{:S(2)}) collective-permute-start(s32[2]{0:T(128)S(1)} %get-tuple-element.58), channel_id=1, source_target_pairs={{0,12},{4,0},{8,4},{12,8},{1,13},{5,1},{9,5},{13,9},{2,14},{6,2},{... | collective-permute-start | bytes 32 | tf_op jit(solution)/shard_map/ppermute | solution.py:31
  6.9 5.1 %collective-permute-start.2 = (s32[2]{0:T(128)S(1)}, s32[2]{0:T(128)S(1)}, u32[]{:S(2)}, u32[]{:S(2)}) collective-permute-start(s32[2]{0:T(128)S(1)} %get-tuple-element.59), channel_id=1, source_target_pairs={{0,8},{4,12},{8,0},{12,4},{1,9},{5,13},{9,1},{13,5},{2,10},{6,14},... | collective-permute-start | bytes 32 | tf_op jit(solution)/shard_map/ppermute | solution.py:31
  6.9 5.3 %collective-permute-start.1 = (s32[2]{0:T(128)S(1)}, s32[2]{0:T(128)S(1)}, u32[]{:S(2)}, u32[]{:S(2)}) collective-permute-start(s32[2]{0:T(128)S(1)} %get-tuple-element.60), channel_id=1, source_target_pairs={{0,4},{4,8},{8,12},{12,0},{1,5},{5,9},{9,13},{13,1},{2,6},{6,10},{... | collective-permute-start | bytes 32 | tf_op jit(solution)/shard_map/ppermute | solution.py:31
  7.9 0.8 %copy-start = (s32[16,512]{1,0:T(8,128)S(1)}, s32[16,512]{1,0:T(8,128)}, u32[]{:S(2)}) copy-start(s32[16,512]{1,0:T(8,128)} %present_hbm.3) | copy-start | bytes 98308
  8.7 3.7 %copy-start.1 = (s32[16,512]{1,0:T(8,128)S(1)}, s32[16,512]{1,0:T(8,128)}, u32[]{:S(2)}) copy-start(s32[16,512]{1,0:T(8,128)} %present_hbm.3) | copy-start | bytes 98308
  10.4 16.7 %collective-permute-start = (bf16[272,512]{1,0:T(8,128)(2,1)S(1)}, bf16[272,512]{1,0:T(8,128)(2,1)S(1)}, u32[]{:S(2)}, u32[]{:S(2)}) collective-permute-start(bf16[272,512]{1,0:T(8,128)(2,1)S(1)} %get-tuple-element.26), channel_id=1, source_target_pairs={{0,2},{2,0},{1,3},{3,1},{4,6},{6,4},{5,7},{7,5},{8,10},{10,8},{9,1... | collective-permute-start | bytes 835592 | tf_op jit(solution)/shard_map/ppermute | solution.py:31
  14.2 6.9 %collective-permute-start.5 = (bf16[136,512]{1,0:T(8,128)(2,1)S(1)}, bf16[136,512]{1,0:T(8,128)(2,1)S(1)}, u32[]{:S(2)}, u32[]{:S(2)}) collective-permute-start(bf16[136,512]{1,0:T(8,128)(2,1)S(1)} %get-tuple-element.28.rest_2_), channel_id=1, source_target_pairs={{0,2},{2,0},{1,3},{3,1},{4,6},{6,4},{5,7},{7,5},{8,10},{10,8},{9,1... | collective-permute-start | bytes 417800 | tf_op jit(solution)/shard_map/ppermute | solution.py:31
  15.7 5.3 %collective-permute-start.12 = (bf16[136,512]{1,0:T(8,128)(2,1)S(1)}, bf16[136,512]{1,0:T(8,128)(2,1)S(1)}, u32[]{:S(2)}, u32[]{:S(2)}) collective-permute-start(bf16[136,512]{1,0:T(8,128)(2,1)S(1)} %get-tuple-element.33), channel_id=1, source_target_pairs={{0,12},{4,0},{8,4},{12,8},{1,13},{5,1},{9,5},{13,9},{2,14},{6,2},{... | collective-permute-start | bytes 417800 | tf_op jit(solution)/shard_map/ppermute | solution.py:31
  17.4 9.7 %collective-permute-start.8 = (bf16[136,512]{1,0:T(8,128)(2,1)S(1)}, bf16[136,512]{1,0:T(8,128)(2,1)S(1)}, u32[]{:S(2)}, u32[]{:S(2)}) collective-permute-start(bf16[136,512]{1,0:T(8,128)(2,1)S(1)} %get-tuple-element.32), channel_id=1, source_target_pairs={{0,8},{4,12},{8,0},{12,4},{1,9},{5,13},{9,1},{13,5},{2,10},{6,14},... | collective-permute-start | bytes 417800 | tf_op jit(solution)/shard_map/ppermute | solution.py:31
  21.1 6.9 %collective-permute-start.6 = (bf16[136,512]{1,0:T(8,128)(2,1)S(1)}, bf16[136,512]{1,0:T(8,128)(2,1)S(1)}, u32[]{:S(2)}, u32[]{:S(2)}) collective-permute-start(bf16[136,512]{1,0:T(8,128)(2,1)S(1)} %collective-permute-done.5.rest_3_), channel_id=1, source_target_pairs={{0,1},{1,0},{2,3},{3,2},{4,5},{5,4},{6,7},{7,6},{8,9},{9,8},{10,11... | collective-permute-start | bytes 417800 | tf_op jit(solution)/shard_map/ppermute | solution.py:31
  21.1 7.1 %collective-permute-start.13 = (bf16[136,512]{1,0:T(8,128)(2,1)S(1)}, bf16[136,512]{1,0:T(8,128)(2,1)S(1)}, u32[]{:S(2)}, u32[]{:S(2)}) collective-permute-start(bf16[136,512]{1,0:T(8,128)(2,1)S(1)} %collective-permute-done.12.rest_2_), channel_id=1, source_target_pairs={{0,2},{2,0},{1,3},{3,1},{4,6},{6,4},{5,7},{7,5},{8,10},{10,8},{9,1... | collective-permute-start | bytes 417800 | tf_op jit(solution)/shard_map/ppermute | solution.py:31
  22.7 8.3 %collective-permute-start.4 = (bf16[136,512]{1,0:T(8,128)(2,1)S(1)}, bf16[136,512]{1,0:T(8,128)(2,1)S(1)}, u32[]{:S(2)}, u32[]{:S(2)}) collective-permute-start(bf16[136,512]{1,0:T(8,128)(2,1)S(1)} %get-tuple-element.27), channel_id=1, source_target_pairs={{0,4},{4,8},{8,12},{12,0},{1,5},{5,9},{9,13},{13,1},{2,6},{6,10},{... | collective-permute-start | bytes 417800 | tf_op jit(solution)/shard_map/ppermute | solution.py:31
  27.1 5.3 %collective-permute-start.14 = (bf16[136,512]{1,0:T(8,128)(2,1)S(1)}, bf16[136,512]{1,0:T(8,128)(2,1)S(1)}, u32[]{:S(2)}, u32[]{:S(2)}) collective-permute-start(bf16[136,512]{1,0:T(8,128)(2,1)S(1)} %collective-permute-done.12.rest_2_), channel_id=1, source_target_pairs={{0,1},{1,0},{2,3},{3,2},{4,5},{5,4},{6,7},{7,6},{8,9},{9,8},{10,11... | collective-permute-start | bytes 417800 | tf_op jit(solution)/shard_map/ppermute | solution.py:31
  27.1 6.1 %collective-permute-start.9 = (bf16[136,512]{1,0:T(8,128)(2,1)S(1)}, bf16[136,512]{1,0:T(8,128)(2,1)S(1)}, u32[]{:S(2)}, u32[]{:S(2)}) collective-permute-start(bf16[136,512]{1,0:T(8,128)(2,1)S(1)} %collective-permute-done.8.rest_2_), channel_id=1, source_target_pairs={{0,2},{2,0},{1,3},{3,1},{4,6},{6,4},{5,7},{7,5},{8,10},{10,8},{9,1... | collective-permute-start | bytes 417800 | tf_op jit(solution)/shard_map/ppermute | solution.py:31
  28.0 7.8 %collective-permute-start.10 = (bf16[136,512]{1,0:T(8,128)(2,1)S(1)}, bf16[136,512]{1,0:T(8,128)(2,1)S(1)}, u32[]{:S(2)}, u32[]{:S(2)}) collective-permute-start(bf16[136,512]{1,0:T(8,128)(2,1)S(1)} %collective-permute-done.8.rest_2_), channel_id=1, source_target_pairs={{0,1},{1,0},{2,3},{3,2},{4,5},{5,4},{6,7},{7,6},{8,9},{9,8},{10,11... | collective-permute-start | bytes 417800 | tf_op jit(solution)/shard_map/ppermute | solution.py:31
  28.2 5.0 %collective-permute-start.15 = (bf16[136,512]{1,0:T(8,128)(2,1)S(1)}, bf16[136,512]{1,0:T(8,128)(2,1)S(1)}, u32[]{:S(2)}, u32[]{:S(2)}) collective-permute-start(bf16[136,512]{1,0:T(8,128)(2,1)S(1)} %collective-permute-done.13.rest_3_), channel_id=1, source_target_pairs={{0,1},{1,0},{2,3},{3,2},{4,5},{5,4},{6,7},{7,6},{8,9},{9,8},{10,11... | collective-permute-start | bytes 417800 | tf_op jit(solution)/shard_map/ppermute | solution.py:31
  31.0 7.3 %collective-permute-start.7 = (bf16[136,512]{1,0:T(8,128)(2,1)S(1)}, bf16[136,512]{1,0:T(8,128)(2,1)S(1)}, u32[]{:S(2)}, u32[]{:S(2)}) collective-permute-start(bf16[136,512]{1,0:T(8,128)(2,1)S(1)} %collective-permute-done.4.rest_2_), channel_id=1, source_target_pairs={{0,2},{2,0},{1,3},{3,1},{4,6},{6,4},{5,7},{7,5},{8,10},{10,8},{9,1... | collective-permute-start | bytes 417800 | tf_op jit(solution)/shard_map/ppermute | solution.py:31
  32.4 9.3 %collective-permute-start.16 = (bf16[136,512]{1,0:T(8,128)(2,1)S(1)}, bf16[136,512]{1,0:T(8,128)(2,1)S(1)}, u32[]{:S(2)}, u32[]{:S(2)}) collective-permute-start(bf16[136,512]{1,0:T(8,128)(2,1)S(1)} %collective-permute-done.4.rest_2_), channel_id=1, source_target_pairs={{0,1},{1,0},{2,3},{3,2},{4,5},{5,4},{6,7},{7,6},{8,9},{9,8},{10,11... | collective-permute-start | bytes 417800 | tf_op jit(solution)/shard_map/ppermute | solution.py:31
  33.2 2.6 %collective-permute-start.11 = (bf16[136,512]{1,0:T(8,128)(2,1)S(1)}, bf16[136,512]{1,0:T(8,128)(2,1)S(1)}, u32[]{:S(2)}, u32[]{:S(2)}) collective-permute-start(bf16[136,512]{1,0:T(8,128)(2,1)S(1)} %collective-permute-done.9.rest_3_), channel_id=1, source_target_pairs={{0,1},{1,0},{2,3},{3,2},{4,5},{5,4},{6,7},{7,6},{8,9},{9,8},{10,11... | collective-permute-start | bytes 417800 | tf_op jit(solution)/shard_map/ppermute | solution.py:31
  38.4 3.3 %collective-permute-start.17 = (bf16[136,512]{1,0:T(8,128)(2,1)S(1)}, bf16[136,512]{1,0:T(8,128)(2,1)S(1)}, u32[]{:S(2)}, u32[]{:S(2)}) collective-permute-start(bf16[136,512]{1,0:T(8,128)(2,1)S(1)} %collective-permute-done.7.rest_3_), channel_id=1, source_target_pairs={{0,1},{1,0},{2,3},{3,2},{4,5},{5,4},{6,7},{7,6},{8,9},{9,8},{10,11... | collective-permute-start | bytes 417800 | tf_op jit(solution)/shard_map/ppermute | solution.py:31
  39.0 7.5 %collective-permute-start.19 = (f32[25,2,128]{2,1,0:T(2,128)S(1)}, f32[25,2,128]{2,1,0:T(2,128)S(1)}, u32[]{:S(2)}, u32[]{:S(2)}) collective-permute-start(f32[25,2,128]{2,1,0:T(2,128)S(1)} %get-tuple-element.46), channel_id=1, source_target_pairs={{0,8},{4,12},{8,0},{12,4},{1,9},{5,13},{9,1},{13,5},{2,10},{6,14},... | collective-permute-start | bytes 76808 | tf_op jit(solution)/shard_map/ppermute | solution.py:31
  39.9 6.6 %collective-permute-start.18 = (f32[25,2,128]{2,1,0:T(2,128)S(1)}, f32[25,2,128]{2,1,0:T(2,128)S(1)}, u32[]{:S(2)}, u32[]{:S(2)}) collective-permute-start(f32[25,2,128]{2,1,0:T(2,128)S(1)} %get-tuple-element.45), channel_id=1, source_target_pairs={{0,4},{4,8},{8,12},{12,0},{1,5},{5,9},{9,13},{13,1},{2,6},{6,10},{... | collective-permute-start | bytes 76808 | tf_op jit(solution)/shard_map/ppermute | solution.py:31
  44.3 3.9 %collective-permute-start.20 = (f32[25,2,128]{2,1,0:T(2,128)S(1)}, f32[25,2,128]{2,1,0:T(2,128)S(1)}, u32[]{:S(2)}, u32[]{:S(2)}) collective-permute-start(f32[25,2,128]{2,1,0:T(2,128)S(1)} %get-tuple-element.47), channel_id=1, source_target_pairs={{0,12},{4,0},{8,4},{12,8},{1,13},{5,1},{9,5},{13,9},{2,14},{6,2},{... | collective-permute-start | bytes 76808 | tf_op jit(solution)/shard_map/ppermute | solution.py:31
  49.0 1.4 %collective-permute-start.21 = (bf16[25,16,128]{2,1,0:T(8,128)(2,1)S(1)}, bf16[25,16,128]{2,1,0:T(8,128)(2,1)S(1)}, u32[]{:S(2)}, u32[]{:S(2)}) collective-permute-start(bf16[25,16,128]{2,1,0:T(8,128)(2,1)S(1)} %shard_map.74), channel_id=1, source_target_pairs={{0,1},{1,0},{2,3},{3,2},{4,5},{5,4},{6,7},{7,6},{8,9},{9,8},{10,11... | collective-permute-start | bytes 307208 | tf_op jit(solution)/shard_map/ppermute | solution.py:31
  50.4 5.0 %collective-permute-start.22 = (bf16[25,16,128]{2,1,0:T(8,128)(2,1)S(1)}, bf16[25,16,128]{2,1,0:T(8,128)(2,1)S(1)}, u32[]{:S(2)}, u32[]{:S(2)}) collective-permute-start(bf16[25,16,128]{2,1,0:T(8,128)(2,1)S(1)} %add_convert_fusion), channel_id=1, source_target_pairs={{0,2},{2,0},{1,3},{3,1},{4,6},{6,4},{5,7},{7,5},{8,10},{10,8},{9,1... | collective-permute-start | bytes 307208 | tf_op jit(solution)/shard_map/ppermute | solution.py:31

commit v5 on v4

--- a/solution.py
+++ b/solution.py
@@ -386,16 +386,15 @@
         rows.append(row)
         cols.append(col if i == 0 else rotated(col, "sensor", d))
     partial = fold(first_of, jnp.concatenate(served), rows, cols, blk_dev)
-    partial = partial.astype(jnp.float32)
-    if lag_count == 2:
-        partial = partial + rotated(partial.astype(jnp.bfloat16), "lag", 1).astype(jnp.float32)
-    else:
-        partial = lax.psum(partial.astype(jnp.bfloat16), "lag").astype(jnp.float32)
-    partial = partial.astype(jnp.bfloat16)
-    if tm_count == 2:
-        strength = partial.astype(jnp.float32) + rotated(partial, "tm", 1).astype(jnp.float32)
-    else:
-        strength = lax.psum(partial, "tm").astype(jnp.float32)
+    for axis, size in (("tm", tm_count), ("lag", lag_count)):
+        if size == 2:
+            other = rotated(partial.astype(jnp.bfloat16), axis, 1)
+            partial = partial.astype(jnp.float32) + other.astype(jnp.float32)
+        else:
+            partial = lax.psum(partial.astype(jnp.bfloat16), axis)
+        if axis == "tm":
+            partial = partial.astype(jnp.bfloat16)
+    strength = partial.astype(jnp.float32)
     return (cov, strength)
 
 

time: 56.9 us -> 57 us (level)
  starting transfers between devices: 27.8 us -> 28.6 us
    ppermute x23, starting transfers between devices: 27.8 us -> 28.6 us  [rotated(): lax.ppermute(block, axis, [(i, (i + distance) % size) for i in range(size)])]
  transfers between devices with their start and end apart: 23 -> 23, of which waited for: 6 -> 7; matrix products, arithmetic and copies ran while one was open for 1% -> 1% of each run, Pallas kernels for 25% -> 24%
where the time goes in v5:
time: 57 us; the launch traced here: 56.7 us
  starting transfers between devices  28.6 us (50%)
  Pallas kernels  14.6 us (26%)
  waiting for transfers between devices  9.57 us (17%)
  other arithmetic  2.2 us (4%)
  local copies, waits for them, and re-layouts  0.9 us (2%)
  between operations  0.77 us (1%)
    ppermute x23, starting transfers between devices, rotated(): lax.ppermute(block, axis, [(i, (i + distance) % size) for i in range(size)])  28.6 us
    pallas_call x4, Pallas kernels, covariances(): pl.pallas_call(kernel, out_shape=[jax.ShapeDtypeStruct((pairs, LAGS, per_...  10.2 us
    ppermute x23, waiting for transfers between devices, rotated(): lax.ppermute(block, axis, [(i, (i + distance) % size) for i in range(size)])  9.57 us
    pallas_call x1, Pallas kernels, pack_blocks(): pl.pallas_call(kernel, out_shape=[jax.ShapeDtypeStruct((rows + MASK_ROWS,...  1.8 us
    pallas_call x1, Pallas kernels, pack_first(): pl.pallas_call(kernel, out_shape=[jax.ShapeDtypeStruct((pairs * per_row +...  1.74 us
  transfers between devices with their start and end apart: 23, of which 7 were waited for; matrix products, arithmetic and copies ran while one was open for 1% of the time, Pallas kernels for 24%

profile of v5, /device:TPU:0, one launch (start us, length us, event | category | flops | bytes accessed | tf_op | source)
XLA Modules:
  0.0 56.7 jit_solution(11503600355040982047)
XLA Ops:
  0.6 0.7 %pad_add_fusion = s32[16]{0:T(128)S(1)} fusion(s32[8]{0:T(128)} %param.8, s32[8]{0:T(128)} %param.7), kind=kLoop, calls=%fused_computation.35 | loop fusion | flops 16 | bytes 128 | tf_op jit(solution)/shard_map/concatenate | solution.py:324
  1.4 0.1 multiply_subtract_fusion
  1.5 0.2 convert_reduce_fusion
  1.7 0.1 select_reduce_fusion
  1.8 0.1 fusion.10
  1.9 5.1 %collective-permute-start.3 = (s32[2]{0:T(128)S(1)}, s32[2]{0:T(128)S(1)}, u32[]{:S(2)}, u32[]{:S(2)}) collective-permute-start(s32[2]{0:T(128)S(1)} %get-tuple-element.58), channel_id=1, source_target_pairs={{0,12},{4,0},{8,4},{12,8},{1,13},{5,1},{9,5},{13,9},{2,14},{6,2},{... | collective-permute-start | bytes 32 | tf_op jit(solution)/shard_map/ppermute | solution.py:31
  6.9 0.0 collective-permute-start.2
  6.9 1.0 %collective-permute-start.1 = (s32[2]{0:T(128)S(1)}, s32[2]{0:T(128)S(1)}, u32[]{:S(2)}, u32[]{:S(2)}) collective-permute-start(s32[2]{0:T(128)S(1)} %get-tuple-element.60), channel_id=1, source_target_pairs={{0,4},{4,8},{8,12},{12,0},{1,5},{5,9},{9,13},{13,1},{2,6},{6,10},{... | collective-permute-start | bytes 32 | tf_op jit(solution)/shard_map/ppermute | solution.py:31
  8.0 0.7 %copy-done = s32[16,512]{1,0:T(8,128)S(1)} copy-done((s32[16,512]{1,0:T(8,128)S(1)}, s32[16,512]{1,0:T(8,128)}, u32[]{:S(2)}) %copy-start) | copy-done | bytes 32792
  8.7 1.7 %shard_map.68 = (bf16[272,512]{1,0:T(8,128)(2,1)S(1)}, bf16[272,512]{1,0:T(8,128)(2,1)S(1)}) custom-call(s32[8]{0:T(128)S(1)} %get-tuple-element.61.first_ref, s32[2]{0:T(128)S(1)} %fusion.4.start_ref, bf16[16,128,512]{2,1,0:T(8,128)(2,1)} %readings_ref.3, s32[16,512]{1,0:T(8,128)S(1)} %copy-done), custom_call_target="tpu_custom_call" | custom-call | flops 1610000000 | bytes 1024 | tf_op jit(solution)/shard_map/pallas_call | solution.py:110
  10.4 1.6 %collective-permute-start = (bf16[272,512]{1,0:T(8,128)(2,1)S(1)}, bf16[272,512]{1,0:T(8,128)(2,1)S(1)}, u32[]{:S(2)}, u32[]{:S(2)}) collective-permute-start(bf16[272,512]{1,0:T(8,128)(2,1)S(1)} %get-tuple-element.26), channel_id=1, source_target_pairs={{0,2},{2,0},{1,3},{3,1},{4,6},{6,4},{5,7},{7,5},{8,10},{10,8},{9,1... | collective-permute-start | bytes 835592 | tf_op jit(solution)/shard_map/ppermute | solution.py:31
  12.0 0.0 collective-permute-done.3
  12.0 0.0 collective-permute-done.2
  12.0 0.2 collective-permute-done.1
  12.3 0.1 pad_add_fusion.2.index_ref
  12.4 1.8 %shard_map.69 = (bf16[136,512]{1,0:T(8,128)(2,1)S(1)}, bf16[136,512]{1,0:T(8,128)(2,1)S(1)}, bf16[136,512]{1,0:T(8,128)(2,1)S(1)}, bf16[136,512]{1,0:T(8,128)(2,1)S(1)}, bf16[136,512]{1,0:T(8,128)(2,1)S(1)}) custom-call(s32[5]{0:T(128)S(1)} %pad_add_fusion.2.index_ref, bf16[16,128,512]{2,1,0:T(8,128)(2,1)} %readings_ref.3, s32[16,512]{1,0:T(8,128)S(1)} %copy-done.1), custom_call_target="tpu_custom_call" | custom-call | flops 1150000000 | bytes 1024 | tf_op jit(solution)/shard_map/pallas_call | solution.py:63
  14.2 1.6 %collective-permute-start.5 = (bf16[136,512]{1,0:T(8,128)(2,1)S(1)}, bf16[136,512]{1,0:T(8,128)(2,1)S(1)}, u32[]{:S(2)}, u32[]{:S(2)}) collective-permute-start(bf16[136,512]{1,0:T(8,128)(2,1)S(1)} %get-tuple-element.28.rest_2_), channel_id=1, source_target_pairs={{0,2},{2,0},{1,3},{3,1},{4,6},{6,4},{5,7},{7,5},{8,10},{10,8},{9,1... | collective-permute-start | bytes 417800 | tf_op jit(solution)/shard_map/ppermute | solution.py:31
  15.7 1.6 %collective-permute-start.12 = (bf16[136,512]{1,0:T(8,128)(2,1)S(1)}, bf16[136,512]{1,0:T(8,128)(2,1)S(1)}, u32[]{:S(2)}, u32[]{:S(2)}) collective-permute-start(bf16[136,512]{1,0:T(8,128)(2,1)S(1)} %get-tuple-element.33), channel_id=1, source_target_pairs={{0,12},{4,0},{8,4},{12,8},{1,13},{5,1},{9,5},{13,9},{2,14},{6,2},{... | collective-permute-start | bytes 417800 | tf_op jit(solution)/shard_map/ppermute | solution.py:31
  17.4 0.1 fusion.9
  17.4 1.1 %collective-permute-start.8 = (bf16[136,512]{1,0:T(8,128)(2,1)S(1)}, bf16[136,512]{1,0:T(8,128)(2,1)S(1)}, u32[]{:S(2)}, u32[]{:S(2)}) collective-permute-start(bf16[136,512]{1,0:T(8,128)(2,1)S(1)} %get-tuple-element.32), channel_id=1, source_target_pairs={{0,8},{4,12},{8,0},{12,4},{1,9},{5,13},{9,1},{13,5},{2,10},{6,14},... | collective-permute-start | bytes 417800 | tf_op jit(solution)/shard_map/ppermute | solution.py:31
  18.6 2.5 %collective-permute-done.5.rest_3_ = bf16[136,512]{1,0:T(8,128)(2,1)S(1)} collective-permute-done((bf16[136,512]{1,0:T(8,128)(2,1)S(1)}, bf16[136,512]{1,0:T(8,128)(2,1)S(1)}, u32[]{:S(2)}, u32[]{:S(2)}) %collective-permute-start.5) | collective-permute-done | bytes 139296 | tf_op jit(solution)/shard_map/ppermute | solution.py:31
  21.1 0.0 collective-permute-start.6
  21.1 0.0 collective-permute-done.12.rest_2_
  21.1 1.5 %collective-permute-start.13 = (bf16[136,512]{1,0:T(8,128)(2,1)S(1)}, bf16[136,512]{1,0:T(8,128)(2,1)S(1)}, u32[]{:S(2)}, u32[]{:S(2)}) collective-permute-start(bf16[136,512]{1,0:T(8,128)(2,1)S(1)} %collective-permute-done.12.rest_2_), channel_id=1, source_target_pairs={{0,2},{2,0},{1,3},{3,1},{4,6},{6,4},{5,7},{7,5},{8,10},{10,8},{9,1... | collective-permute-start | bytes 417800 | tf_op jit(solution)/shard_map/ppermute | solution.py:31
  22.6 0.1 pad_add_fusion.1.place_ref
  22.7 4.5 %collective-permute-start.4 = (bf16[136,512]{1,0:T(8,128)(2,1)S(1)}, bf16[136,512]{1,0:T(8,128)(2,1)S(1)}, u32[]{:S(2)}, u32[]{:S(2)}) collective-permute-start(bf16[136,512]{1,0:T(8,128)(2,1)S(1)} %get-tuple-element.27), channel_id=1, source_target_pairs={{0,4},{4,8},{8,12},{12,0},{1,5},{5,9},{9,13},{13,1},{2,6},{6,10},{... | collective-permute-start | bytes 417800 | tf_op jit(solution)/shard_map/ppermute | solution.py:31
  27.1 0.0 collective-permute-done.8.rest_2_
  27.1 0.0 collective-permute-start.14
  27.1 0.0 collective-permute-done.rest_1_
  27.1 3.8 %collective-permute-start.9 = (bf16[136,512]{1,0:T(8,128)(2,1)S(1)}, bf16[136,512]{1,0:T(8,128)(2,1)S(1)}, u32[]{:S(2)}, u32[]{:S(2)}) collective-permute-start(bf16[136,512]{1,0:T(8,128)(2,1)S(1)} %collective-permute-done.8.rest_2_), channel_id=1, source_target_pairs={{0,2},{2,0},{1,3},{3,1},{4,6},{6,4},{5,7},{7,5},{8,10},{10,8},{9,1... | collective-permute-start | bytes 417800 | tf_op jit(solution)/shard_map/ppermute | solution.py:31
  30.9 0.0 collective-permute-done.6.rest_5_
  30.9 0.2 collective-permute-start.10
  31.2 0.0 collective-permute-done.13.rest_3_
  31.2 0.3 collective-permute-start.15
  31.4 2.6 %shard_map.70 = (bf16[8,25,32,128]{3,2,1,0:T(8,128)(2,1)}, f32[2,32,128]{2,1,0:T(8,128)S(1)}, f32[25,2,128]{2,1,0:T(2,128)S(1)}) custom-call(s32[2]{0:T(128)S(1)} %get-tuple-element.55.pair_ref, s32[3]{0:T(128)S(1)} %pad_add_fusion.1.place_ref, bf16[272,512]{1,0:T(8,128)(2,1)S(1)} %get-tuple-element.25.rest_0_, ...), custom_call_target="tpu_custom_call" | custom-call | flops 3449999872 | bytes 1024 | tf_op jit(solution)/shard_map/pallas_call | solution.py:253
  34.0 0.0 collective-permute-done.4.rest_2_
  34.0 0.2 collective-permute-start.7
  34.2 0.0 collective-permute-done.14.rest_4_
  34.2 0.2 collective-permute-start.16
  34.4 0.9 %collective-permute-done.9.rest_3_ = bf16[136,512]{1,0:T(8,128)(2,1)S(1)} collective-permute-done((bf16[136,512]{1,0:T(8,128)(2,1)S(1)}, bf16[136,512]{1,0:T(8,128)(2,1)S(1)}, u32[]{:S(2)}, u32[]{:S(2)}) %collective-permute-start.9) | collective-permute-done | bytes 139296 | tf_op jit(solution)/shard_map/ppermute | solution.py:31
  35.3 0.0 collective-permute-start.11
  35.3 0.0 collective-permute-done.15.rest_5_
  35.3 2.6 %shard_map.71 = (bf16[8,25,32,128]{3,2,1,0:T(8,128)(2,1)}, f32[2,32,128]{2,1,0:T(8,128)S(1)}, f32[25,2,128]{2,1,0:T(2,128)S(1)}) custom-call(s32[2]{0:T(128)S(1)} %get-tuple-element.53.pair_ref, s32[3]{0:T(128)S(1)} %pad_add_fusion.1.place_ref, bf16[272,512]{1,0:T(8,128)(2,1)S(1)} %get-tuple-element.25.rest_0_, ...), custom_call_target="tpu_custom_call", output_to_operand_aliasing={{0}: (8, {})} | custom-call | flops 3449999872 | bytes 1024 | tf_op jit(solution)/shard_map/pallas_call | solution.py:253
  37.8 0.0 collective-permute-done.10.rest_4_
  37.9 0.0 collective-permute-done.11.rest_5_
  37.9 2.6 %shard_map.72 = (bf16[8,25,32,128]{3,2,1,0:T(8,128)(2,1)}, f32[2,32,128]{2,1,0:T(8,128)S(1)}, f32[25,2,128]{2,1,0:T(2,128)S(1)}) custom-call(s32[2]{0:T(128)S(1)} %get-tuple-element.54.pair_ref, s32[3]{0:T(128)S(1)} %pad_add_fusion.1.place_ref, bf16[272,512]{1,0:T(8,128)(2,1)S(1)} %get-tuple-element.25.rest_0_, ...), custom_call_target="tpu_custom_call", output_to_operand_aliasing={{0}: (8, {})} | custom-call | flops 3449999872 | bytes 1024 | tf_op jit(solution)/shard_map/pallas_call | solution.py:253
  40.4 0.0 collective-permute-done.7.rest_3_
  40.4 0.6 %collective-permute-start.17 = (bf16[136,512]{1,0:T(8,128)(2,1)S(1)}, bf16[136,512]{1,0:T(8,128)(2,1)S(1)}, u32[]{:S(2)}, u32[]{:S(2)}) collective-permute-start(bf16[136,512]{1,0:T(8,128)(2,1)S(1)} %collective-permute-done.7.rest_3_), channel_id=1, source_target_pairs={{0,1},{1,0},{2,3},{3,2},{4,5},{5,4},{6,7},{7,6},{8,9},{9,8},{10,11... | collective-permute-start | bytes 417800 | tf_op jit(solution)/shard_map/ppermute | solution.py:31
  41.0 0.0 collective-permute-start.19
  41.0 0.7 %collective-permute-start.18 = (f32[25,2,128]{2,1,0:T(2,128)S(1)}, f32[25,2,128]{2,1,0:T(2,128)S(1)}, u32[]{:S(2)}, u32[]{:S(2)}) collective-permute-start(f32[25,2,128]{2,1,0:T(2,128)S(1)} %get-tuple-element.45), channel_id=1, source_target_pairs={{0,4},{4,8},{8,12},{12,0},{1,5},{5,9},{9,13},{13,1},{2,6},{6,10},{... | collective-permute-start | bytes 76808 | tf_op jit(solution)/shard_map/ppermute | solution.py:31
  41.7 0.0 collective-permute-done.16.rest_4_
  41.7 0.3 collective-permute-done.17.rest_5_
  42.0 2.6 %shard_map.73 = (bf16[8,25,32,128]{3,2,1,0:T(8,128)(2,1)}, f32[2,32,128]{2,1,0:T(8,128)S(1)}, f32[25,2,128]{2,1,0:T(2,128)S(1)}) custom-call(s32[2]{0:T(128)S(1)} %get-tuple-element.56.pair_ref, s32[3]{0:T(128)S(1)} %pad_add_fusion.1.place_ref, bf16[272,512]{1,0:T(8,128)(2,1)S(1)} %get-tuple-element.25.rest_0_, ...), custom_call_target="tpu_custom_call", output_to_operand_aliasing={{0}: (8, {})} | custom-call | flops 3449999872 | bytes 1024 | tf_op jit(solution)/shard_map/pallas_call | solution.py:253
  44.6 2.9 %collective-permute-start.20 = (f32[25,2,128]{2,1,0:T(2,128)S(1)}, f32[25,2,128]{2,1,0:T(2,128)S(1)}, u32[]{:S(2)}, u32[]{:S(2)}) collective-permute-start(f32[25,2,128]{2,1,0:T(2,128)S(1)} %get-tuple-element.47), channel_id=1, source_target_pairs={{0,12},{4,0},{8,4},{12,8},{1,13},{5,1},{9,5},{13,9},{2,14},{6,2},{... | collective-permute-start | bytes 76808 | tf_op jit(solution)/shard_map/ppermute | solution.py:31
  47.5 0.1 pad_add_fusion.3.served_ref
  47.5 0.0 collective-permute-done.19.rest_6_
  47.5 0.0 collective-permute-done.18.rest_5_
  47.6 1.4 %collective-permute-done.20.rest_7_ = f32[25,2,128]{2,1,0:T(2,128)S(1)} collective-permute-done((f32[25,2,128]{2,1,0:T(2,128)S(1)}, f32[25,2,128]{2,1,0:T(2,128)S(1)}, u32[]{:S(2)}, u32[]{:S(2)}) %collective-permute-start.20) | collective-permute-done | bytes 25632 | tf_op jit(solution)/shard_map/ppermute | solution.py:31
  49.0 0.8 %shard_map.74 = bf16[25,16,128]{2,1,0:T(8,128)(2,1)S(1)} custom-call(s32[8]{0:T(128)S(1)} %get-tuple-element.48.first_ref, s32[8]{0:T(128)S(1)} %pad_add_fusion.3.served_ref, f32[2,32,128]{2,1,0:T(8,128)S(1)} %get-tuple-element.40.rest_0_, f32[2,32,128]{2,1,0:T(8,128)S(1)} %get-tuple-element.41.rest_1_, f32[2,32,128]{2,1,0:T(8,128)S(1)} %get-tuple-element.42.rest_2_, ...), custom_call_target="tpu_custom_call" | custom-call | flops 920000000 | bytes 1024 | tf_op jit(solution)/shard_map/pallas_call | solution.py:301
  49.8 1.8 %collective-permute-start.21 = (bf16[25,16,128]{2,1,0:T(8,128)(2,1)S(1)}, bf16[25,16,128]{2,1,0:T(8,128)(2,1)S(1)}, u32[]{:S(2)}, u32[]{:S(2)}) collective-permute-start(bf16[25,16,128]{2,1,0:T(8,128)(2,1)S(1)} %shard_map.74), channel_id=1, source_target_pairs={{0,2},{2,0},{1,3},{3,1},{4,6},{6,4},{5,7},{7,5},{8,10},{10,8},{9,1... | collective-permute-start | bytes 307208 | tf_op jit(solution)/shard_map/ppermute | solution.py:31
  51.6 2.9 %collective-permute-done.21 = bf16[25,16,128]{2,1,0:T(8,128)(2,1)S(1)} collective-permute-done((bf16[25,16,128]{2,1,0:T(8,128)(2,1)S(1)}, bf16[25,16,128]{2,1,0:T(8,128)(2,1)S(1)}, u32[]{:S(2)}, u32[]{:S(2)}) %collective-permute-start.21) | collective-permute-done | bytes 102432 | tf_op jit(solution)/shard_map/ppermute | solution.py:31
  54.6 0.1 collective-permute-start.22
  54.7 1.3 %collective-permute-done.22 = bf16[25,16,128]{2,1,0:T(8,128)(2,1)S(1)} collective-permute-done((bf16[25,16,128]{2,1,0:T(8,128)(2,1)S(1)}, bf16[25,16,128]{2,1,0:T(8,128)(2,1)S(1)}, u32[]{:S(2)}, u32[]{:S(2)}) %collective-permute-start.22) | collective-permute-done | bytes 102432 | tf_op jit(solution)/shard_map/ppermute | solution.py:31
  56.0 0.7 %convert_add_fusion = f32[25,16,128]{2,1,0:T(8,128)} fusion(bf16[25,16,128]{2,1,0:T(8,128)(2,1)S(1)} %collective-permute-done.22, bf16[25,16,128]{2,1,0:T(8,128)(2,1)S(1)} %add_convert_fusion), kind=kLoop, calls=%fused_computation | loop fusion | flops 153600 | bytes 409600 | tf_op jit(solution)/shard_map/add | solution.py:392
  (10 shorter events, 0.1 us)
Async XLA Ops:
  1.9 10.2 %collective-permute-start.3 = (s32[2]{0:T(128)S(1)}, s32[2]{0:T(128)S(1)}, u32[]{:S(2)}, u32[]{:S(2)}) collective-permute-start(s32[2]{0:T(128)S(1)} %get-tuple-element.58), channel_id=1, source_target_pairs={{0,12},{4,0},{8,4},{12,8},{1,13},{5,1},{9,5},{13,9},{2,14},{6,2},{... | collective-permute-start | bytes 32 | tf_op jit(solution)/shard_map/ppermute | solution.py:31
  6.9 5.1 %collective-permute-start.2 = (s32[2]{0:T(128)S(1)}, s32[2]{0:T(128)S(1)}, u32[]{:S(2)}, u32[]{:S(2)}) collective-permute-start(s32[2]{0:T(128)S(1)} %get-tuple-element.59), channel_id=1, source_target_pairs={{0,8},{4,12},{8,0},{12,4},{1,9},{5,13},{9,1},{13,5},{2,10},{6,14},... | collective-permute-start | bytes 32 | tf_op jit(solution)/shard_map/ppermute | solution.py:31
  6.9 5.3 %collective-permute-start.1 = (s32[2]{0:T(128)S(1)}, s32[2]{0:T(128)S(1)}, u32[]{:S(2)}, u32[]{:S(2)}) collective-permute-start(s32[2]{0:T(128)S(1)} %get-tuple-element.60), channel_id=1, source_target_pairs={{0,4},{4,8},{8,12},{12,0},{1,5},{5,9},{9,13},{13,1},{2,6},{6,10},{... | collective-permute-start | bytes 32 | tf_op jit(solution)/shard_map/ppermute | solution.py:31
  7.9 0.8 %copy-start = (s32[16,512]{1,0:T(8,128)S(1)}, s32[16,512]{1,0:T(8,128)}, u32[]{:S(2)}) copy-start(s32[16,512]{1,0:T(8,128)} %present_hbm.3) | copy-start | bytes 98308
  8.7 3.7 %copy-start.1 = (s32[16,512]{1,0:T(8,128)S(1)}, s32[16,512]{1,0:T(8,128)}, u32[]{:S(2)}) copy-start(s32[16,512]{1,0:T(8,128)} %present_hbm.3) | copy-start | bytes 98308
  10.4 16.7 %collective-permute-start = (bf16[272,512]{1,0:T(8,128)(2,1)S(1)}, bf16[272,512]{1,0:T(8,128)(2,1)S(1)}, u32[]{:S(2)}, u32[]{:S(2)}) collective-permute-start(bf16[272,512]{1,0:T(8,128)(2,1)S(1)} %get-tuple-element.26), channel_id=1, source_target_pairs={{0,2},{2,0},{1,3},{3,1},{4,6},{6,4},{5,7},{7,5},{8,10},{10,8},{9,1... | collective-permute-start | bytes 835592 | tf_op jit(solution)/shard_map/ppermute | solution.py:31
  14.2 6.9 %collective-permute-start.5 = (bf16[136,512]{1,0:T(8,128)(2,1)S(1)}, bf16[136,512]{1,0:T(8,128)(2,1)S(1)}, u32[]{:S(2)}, u32[]{:S(2)}) collective-permute-start(bf16[136,512]{1,0:T(8,128)(2,1)S(1)} %get-tuple-element.28.rest_2_), channel_id=1, source_target_pairs={{0,2},{2,0},{1,3},{3,1},{4,6},{6,4},{5,7},{7,5},{8,10},{10,8},{9,1... | collective-permute-start | bytes 417800 | tf_op jit(solution)/shard_map/ppermute | solution.py:31
  15.7 5.3 %collective-permute-start.12 = (bf16[136,512]{1,0:T(8,128)(2,1)S(1)}, bf16[136,512]{1,0:T(8,128)(2,1)S(1)}, u32[]{:S(2)}, u32[]{:S(2)}) collective-permute-start(bf16[136,512]{1,0:T(8,128)(2,1)S(1)} %get-tuple-element.33), channel_id=1, source_target_pairs={{0,12},{4,0},{8,4},{12,8},{1,13},{5,1},{9,5},{13,9},{2,14},{6,2},{... | collective-permute-start | bytes 417800 | tf_op jit(solution)/shard_map/ppermute | solution.py:31
  17.4 9.7 %collective-permute-start.8 = (bf16[136,512]{1,0:T(8,128)(2,1)S(1)}, bf16[136,512]{1,0:T(8,128)(2,1)S(1)}, u32[]{:S(2)}, u32[]{:S(2)}) collective-permute-start(bf16[136,512]{1,0:T(8,128)(2,1)S(1)} %get-tuple-element.32), channel_id=1, source_target_pairs={{0,8},{4,12},{8,0},{12,4},{1,9},{5,13},{9,1},{13,5},{2,10},{6,14},... | collective-permute-start | bytes 417800 | tf_op jit(solution)/shard_map/ppermute | solution.py:31
  21.1 9.9 %collective-permute-start.6 = (bf16[136,512]{1,0:T(8,128)(2,1)S(1)}, bf16[136,512]{1,0:T(8,128)(2,1)S(1)}, u32[]{:S(2)}, u32[]{:S(2)}) collective-permute-start(bf16[136,512]{1,0:T(8,128)(2,1)S(1)} %collective-permute-done.5.rest_3_), channel_id=1, source_target_pairs={{0,1},{1,0},{2,3},{3,2},{4,5},{5,4},{6,7},{7,6},{8,9},{9,8},{10,11... | collective-permute-start | bytes 417800 | tf_op jit(solution)/shard_map/ppermute | solution.py:31
  21.1 10.1 %collective-permute-start.13 = (bf16[136,512]{1,0:T(8,128)(2,1)S(1)}, bf16[136,512]{1,0:T(8,128)(2,1)S(1)}, u32[]{:S(2)}, u32[]{:S(2)}) collective-permute-start(bf16[136,512]{1,0:T(8,128)(2,1)S(1)} %collective-permute-done.12.rest_2_), channel_id=1, source_target_pairs={{0,2},{2,0},{1,3},{3,1},{4,6},{6,4},{5,7},{7,5},{8,10},{10,8},{9,1... | collective-permute-start | bytes 417800 | tf_op jit(solution)/shard_map/ppermute | solution.py:31
  22.7 11.3 %collective-permute-start.4 = (bf16[136,512]{1,0:T(8,128)(2,1)S(1)}, bf16[136,512]{1,0:T(8,128)(2,1)S(1)}, u32[]{:S(2)}, u32[]{:S(2)}) collective-permute-start(bf16[136,512]{1,0:T(8,128)(2,1)S(1)} %get-tuple-element.27), channel_id=1, source_target_pairs={{0,4},{4,8},{8,12},{12,0},{1,5},{5,9},{9,13},{13,1},{2,6},{6,10},{... | collective-permute-start | bytes 417800 | tf_op jit(solution)/shard_map/ppermute | solution.py:31
  27.1 7.1 %collective-permute-start.14 = (bf16[136,512]{1,0:T(8,128)(2,1)S(1)}, bf16[136,512]{1,0:T(8,128)(2,1)S(1)}, u32[]{:S(2)}, u32[]{:S(2)}) collective-permute-start(bf16[136,512]{1,0:T(8,128)(2,1)S(1)} %collective-permute-done.12.rest_2_), channel_id=1, source_target_pairs={{0,1},{1,0},{2,3},{3,2},{4,5},{5,4},{6,7},{7,6},{8,9},{9,8},{10,11... | collective-permute-start | bytes 417800 | tf_op jit(solution)/shard_map/ppermute | solution.py:31
  27.1 8.1 %collective-permute-start.9 = (bf16[136,512]{1,0:T(8,128)(2,1)S(1)}, bf16[136,512]{1,0:T(8,128)(2,1)S(1)}, u32[]{:S(2)}, u32[]{:S(2)}) collective-permute-start(bf16[136,512]{1,0:T(8,128)(2,1)S(1)} %collective-permute-done.8.rest_2_), channel_id=1, source_target_pairs={{0,2},{2,0},{1,3},{3,1},{4,6},{6,4},{5,7},{7,5},{8,10},{10,8},{9,1... | collective-permute-start | bytes 417800 | tf_op jit(solution)/shard_map/ppermute | solution.py:31
  30.9 6.9 %collective-permute-start.10 = (bf16[136,512]{1,0:T(8,128)(2,1)S(1)}, bf16[136,512]{1,0:T(8,128)(2,1)S(1)}, u32[]{:S(2)}, u32[]{:S(2)}) collective-permute-start(bf16[136,512]{1,0:T(8,128)(2,1)S(1)} %collective-permute-done.8.rest_2_), channel_id=1, source_target_pairs={{0,1},{1,0},{2,3},{3,2},{4,5},{5,4},{6,7},{7,6},{8,9},{9,8},{10,11... | collective-permute-start | bytes 417800 | tf_op jit(solution)/shard_map/ppermute | solution.py:31
  31.2 4.1 %collective-permute-start.15 = (bf16[136,512]{1,0:T(8,128)(2,1)S(1)}, bf16[136,512]{1,0:T(8,128)(2,1)S(1)}, u32[]{:S(2)}, u32[]{:S(2)}) collective-permute-start(bf16[136,512]{1,0:T(8,128)(2,1)S(1)} %collective-permute-done.13.rest_3_), channel_id=1, source_target_pairs={{0,1},{1,0},{2,3},{3,2},{4,5},{5,4},{6,7},{7,6},{8,9},{9,8},{10,11... | collective-permute-start | bytes 417800 | tf_op jit(solution)/shard_map/ppermute | solution.py:31
  34.0 6.4 %collective-permute-start.7 = (bf16[136,512]{1,0:T(8,128)(2,1)S(1)}, bf16[136,512]{1,0:T(8,128)(2,1)S(1)}, u32[]{:S(2)}, u32[]{:S(2)}) collective-permute-start(bf16[136,512]{1,0:T(8,128)(2,1)S(1)} %collective-permute-done.4.rest_2_), channel_id=1, source_target_pairs={{0,2},{2,0},{1,3},{3,1},{4,6},{6,4},{5,7},{7,5},{8,10},{10,8},{9,1... | collective-permute-start | bytes 417800 | tf_op jit(solution)/shard_map/ppermute | solution.py:31
  34.2 7.5 %collective-permute-start.16 = (bf16[136,512]{1,0:T(8,128)(2,1)S(1)}, bf16[136,512]{1,0:T(8,128)(2,1)S(1)}, u32[]{:S(2)}, u32[]{:S(2)}) collective-permute-start(bf16[136,512]{1,0:T(8,128)(2,1)S(1)} %collective-permute-done.4.rest_2_), channel_id=1, source_target_pairs={{0,1},{1,0},{2,3},{3,2},{4,5},{5,4},{6,7},{7,6},{8,9},{9,8},{10,11... | collective-permute-start | bytes 417800 | tf_op jit(solution)/shard_map/ppermute | solution.py:31
  35.3 2.6 %collective-permute-start.11 = (bf16[136,512]{1,0:T(8,128)(2,1)S(1)}, bf16[136,512]{1,0:T(8,128)(2,1)S(1)}, u32[]{:S(2)}, u32[]{:S(2)}) collective-permute-start(bf16[136,512]{1,0:T(8,128)(2,1)S(1)} %collective-permute-done.9.rest_3_), channel_id=1, source_target_pairs={{0,1},{1,0},{2,3},{3,2},{4,5},{5,4},{6,7},{7,6},{8,9},{9,8},{10,11... | collective-permute-start | bytes 417800 | tf_op jit(solution)/shard_map/ppermute | solution.py:31
  40.4 1.6 %collective-permute-start.17 = (bf16[136,512]{1,0:T(8,128)(2,1)S(1)}, bf16[136,512]{1,0:T(8,128)(2,1)S(1)}, u32[]{:S(2)}, u32[]{:S(2)}) collective-permute-start(bf16[136,512]{1,0:T(8,128)(2,1)S(1)} %collective-permute-done.7.rest_3_), channel_id=1, source_target_pairs={{0,1},{1,0},{2,3},{3,2},{4,5},{5,4},{6,7},{7,6},{8,9},{9,8},{10,11... | collective-permute-start | bytes 417800 | tf_op jit(solution)/shard_map/ppermute | solution.py:31
  41.0 6.5 %collective-permute-start.19 = (f32[25,2,128]{2,1,0:T(2,128)S(1)}, f32[25,2,128]{2,1,0:T(2,128)S(1)}, u32[]{:S(2)}, u32[]{:S(2)}) collective-permute-start(f32[25,2,128]{2,1,0:T(2,128)S(1)} %get-tuple-element.46), channel_id=1, source_target_pairs={{0,8},{4,12},{8,0},{12,4},{1,9},{5,13},{9,1},{13,5},{2,10},{6,14},... | collective-permute-start | bytes 76808 | tf_op jit(solution)/shard_map/ppermute | solution.py:31
  41.0 6.5 %collective-permute-start.18 = (f32[25,2,128]{2,1,0:T(2,128)S(1)}, f32[25,2,128]{2,1,0:T(2,128)S(1)}, u32[]{:S(2)}, u32[]{:S(2)}) collective-permute-start(f32[25,2,128]{2,1,0:T(2,128)S(1)} %get-tuple-element.45), channel_id=1, source_target_pairs={{0,4},{4,8},{8,12},{12,0},{1,5},{5,9},{9,13},{13,1},{2,6},{6,10},{... | collective-permute-start | bytes 76808 | tf_op jit(solution)/shard_map/ppermute | solution.py:31
  44.6 4.4 %collective-permute-start.20 = (f32[25,2,128]{2,1,0:T(2,128)S(1)}, f32[25,2,128]{2,1,0:T(2,128)S(1)}, u32[]{:S(2)}, u32[]{:S(2)}) collective-permute-start(f32[25,2,128]{2,1,0:T(2,128)S(1)} %get-tuple-element.47), channel_id=1, source_target_pairs={{0,12},{4,0},{8,4},{12,8},{1,13},{5,1},{9,5},{13,9},{2,14},{6,2},{... | collective-permute-start | bytes 76808 | tf_op jit(solution)/shard_map/ppermute | solution.py:31
  49.8 4.7 %collective-permute-start.21 = (bf16[25,16,128]{2,1,0:T(8,128)(2,1)S(1)}, bf16[25,16,128]{2,1,0:T(8,128)(2,1)S(1)}, u32[]{:S(2)}, u32[]{:S(2)}) collective-permute-start(bf16[25,16,128]{2,1,0:T(8,128)(2,1)S(1)} %shard_map.74), channel_id=1, source_target_pairs={{0,2},{2,0},{1,3},{3,1},{4,6},{6,4},{5,7},{7,5},{8,10},{10,8},{9,1... | collective-permute-start | bytes 307208 | tf_op jit(solution)/shard_map/ppermute | solution.py:31
  54.6 1.4 %collective-permute-start.22 = (bf16[25,16,128]{2,1,0:T(8,128)(2,1)S(1)}, bf16[25,16,128]{2,1,0:T(8,128)(2,1)S(1)}, u32[]{:S(2)}, u32[]{:S(2)}) collective-permute-start(bf16[25,16,128]{2,1,0:T(8,128)(2,1)S(1)} %add_convert_fusion), channel_id=1, source_target_pairs={{0,1},{1,0},{2,3},{3,2},{4,5},{5,4},{6,7},{7,6},{8,9},{9,8},{10,11... | collective-permute-start | bytes 307208 | tf_op jit(solution)/shard_map/ppermute | solution.py:31
